TPU v7x, 32 devices: a whole 2x2x4 slice. The times are simulated.
32 devices in a mesh: pipe: 4 (over z), dp: 2 (over x), tensor: 4 (over y, core).
Axes of the slice: x: 2, y: 2, z: 4, core: 2. Of those that a mesh axis runs over, the one named last changes fastest.
Arguments:
- tokens: bfloat16 [512, 12288], P(('pipe', 'tensor'), 'dp'), may hold values from -6 to 6
- out_grad: bfloat16 [512, 12288], P(('pipe', 'tensor'), 'dp'), may hold values from -3 to 3
- w_in: bfloat16 [12288, 24576], P('dp', ('pipe', 'tensor')), may hold values from -0.0546875 to 0.0546875
- b_in: float32 [24576], P(('pipe', 'tensor')), may hold values from -3 to 3
- w_out: bfloat16 [24576, 12288], P(('pipe', 'tensor'), 'dp'), may hold values from -0.0390625 to 0.0390625
Outputs:
- in_grad: bfloat16 [512, 12288], P(('pipe', 'tensor'), 'dp')
- w_in_grad: bfloat16 [12288, 24576], P('dp', ('pipe', 'tensor'))
- w_out_grad: bfloat16 [24576, 12288], P(('pipe', 'tensor'), 'dp')
- b_in_grad: float32 [24576], P(('pipe', 'tensor'))
All inputs are finite; a program needn't handle non-finite values.
Results may differ from a plain program's by a relative error of at most 0.005.
Values may be sent and summed in bfloat16 or wider, within the bound.
No kernel may reach another device: no remote copies, remote signals or barrier semaphores. Data moves between devices by JAX's collectives and lax.ppermute only.
A program may use at most 256 MiB of HBM per device.

v0:
```python
import jax
import jax.numpy as jnp
from jax import lax
from jax.sharding import PartitionSpec as P

tanh_scale = 0.7978845608028654
cubic_coef = 0.044715


def gelu_pair(value):
    inner = tanh_scale * (value + cubic_coef * value * value * value)
    tangent = jnp.tanh(inner)
    result = 0.5 * value * (1.0 + tangent)
    slope = 0.5 * (1.0 + tangent) + 0.5 * value * (1.0 - tangent * tangent) * tanh_scale * (
        1.0 + 3.0 * cubic_coef * value * value
    )
    return (result, slope)


def times_transpose(left, right):
    return lax.dot_general(
        left, right, (((1,), (1,)), ((), ())), preferred_element_type=jnp.float32
    )


def over_rows(left, right):
    return lax.dot_general(
        left, right, (((0,), (0,)), ((), ())), preferred_element_type=jnp.float32
    )


def shards(tokens, out_grad, w_in, b_in, w_out):
    tok_all, grad_all = (
        lax.all_gather(tokens, ("pipe", "tensor"), axis=0, tiled=True),
        lax.all_gather(out_grad, ("pipe", "tensor"), axis=0, tiled=True),
    )
    proj_part = jnp.dot(tok_all, w_in, preferred_element_type=jnp.float32)
    signal_part = times_transpose(grad_all, w_out)
    projected = lax.psum(proj_part, "dp") + b_in
    active_f, derivative = gelu_pair(projected)
    activated = active_f.astype(jnp.bfloat16)
    back_signal = lax.psum(signal_part, "dp")
    proj_grad = (back_signal * derivative).astype(jnp.bfloat16)
    w_out_grad = over_rows(activated, grad_all).astype(jnp.bfloat16)
    w_in_grad = over_rows(tok_all, proj_grad).astype(jnp.bfloat16)
    b_in_grad = jnp.sum(proj_grad.astype(jnp.float32), axis=0)
    in_total = lax.psum_scatter(
        times_transpose(proj_grad, w_in), ("pipe", "tensor"), scatter_dimension=0, tiled=True
    )
    in_grad = in_total.astype(jnp.bfloat16)
    return (in_grad, w_in_grad, w_out_grad, b_in_grad)


def solution(mesh):
    in_specs = (
        P(("pipe", "tensor"), "dp"),
        P(("pipe", "tensor"), "dp"),
        P("dp", ("pipe", "tensor")),
        P(("pipe", "tensor")),
        P(("pipe", "tensor"), "dp"),
    )
    out_specs = (
        P(("pipe", "tensor"), "dp"),
        P("dp", ("pipe", "tensor")),
        P(("pipe", "tensor"), "dp"),
        P(("pipe", "tensor")),
    )
    return jax.shard_map(shards, mesh=mesh, in_specs=in_specs, out_specs=out_specs, check_vma=False)
```

profile of v0, /device:TPU:0, one launch (start us, length us, event | category | flops | bytes accessed | tf_op | source)
XLA Modules:
  0.0 471.4 jit_solution(10933845564773079919)
XLA Ops:
  7.2 0.0 all-gather.3.cloned.1.call-start
  7.2 0.7 all-gather.3.cloned.1.call-update
  7.9 0.0 all-gather.5.cloned.1.call-start
  7.9 0.7 all-gather.5.cloned.1.call-update
  8.6 0.0 all-reduce.3.cloned.1.call-start
  8.7 66.2 %all-gather.3.cloned.1.call-done = bf16[512,6144]{1,0:T(8,128)(2,1)} async-done(((bf16[32,6144]{1,0:T(8,128)(2,1)}), bf16[512,6144]{1,0:T(8,128)(2,1)}) %all-gather.3.cloned.1.call-update) | async-done | bytes 6291472 | tf_op jit(solution)/shard_map/all_gather | solution.py:35
  74.9 16.8 %fusion.18 = f32[512,1536]{1,0:T(8,128)} fusion(bf16[512,6144]{1,0:T(8,128)(2,1)} %all-gather.3.cloned.1.call-done, bf16[1536,6144]{1,0:T(8,128)(2,1)} %param.9), kind=kOutput, calls=%fused_computation.23 | convolution fusion | flops 9663676416 | bytes 28311552 | tf_op jit(solution)/shard_map/dot_general | solution.py:21
  91.6 46.0 %all-gather.5.cloned.1.call-done = bf16[512,6144]{1,0:T(8,128)(2,1)} async-done(((bf16[32,6144]{1,0:T(8,128)(2,1)}), bf16[512,6144]{1,0:T(8,128)(2,1)}) %all-gather.5.cloned.1.call-update) | async-done | bytes 6291472 | tf_op jit(solution)/shard_map/all_gather | solution.py:34
  137.6 16.9 %fusion.19 = f32[512,1536]{1,0:T(8,128)} fusion(bf16[512,6144]{1,0:T(8,128)(2,1)} %all-gather.5.cloned.1.call-done, bf16[6144,1536]{1,0:T(8,128)(2,1)} %param.7), kind=kOutput, calls=%fused_computation.24 | convolution fusion | flops 9663676416 | bytes 28311552 | tf_op jit(solution)/shard_map/dot_general | solution.py:37
  154.5 0.0 copy-start.1
  154.5 0.0 all-reduce.3.cloned.1.call-update
  154.6 0.2 reduce-scatter.2.cloned.1.call-start
  154.8 152.1 %all-reduce.3.cloned.1.call-done = (f32[512,1536]{1,0:T(8,128)}, f32[512,1536]{1,0:T(8,128)}) async-done(((f32[512,1536]{1,0:T(8,128)}, f32[512,1536]{1,0:T(8,128)}), (f32[512,1536]{1,0:T(8,128)}, f32[512,1536]{1,0:T(8,128)})) %all-reduce.3.cloned.1.call-update) | async-done | bytes 6291472 | tf_op jit(solution)/shard_map/psum | solution.py:42
  306.9 0.0 copy-done.1
  306.9 4.7 %convert_reduce_fusion = (f32[1536]{0:T(1024)}, bf16[512,1536]{1,0:T(8,128)(2,1)S(1)}) fusion(f32[512,1536]{1,0:T(8,128)} %get-tuple-element.8, f32[512,1536]{1,0:T(8,128)} %get-tuple-element.9, f32[1536]{0:T(1024)S(1)} %copy-done.1), kind=kLoop, calls=%fused_computation.12 | loop fusion | flops 17299968 | bytes 7876608 | tf_op jit(solution)/shard_map/reduce_sum | solution.py:46
  311.6 16.4 %fusion.20 = f32[512,6144]{1,0:T(8,128)} fusion(bf16[512,1536]{1,0:T(8,128)(2,1)S(1)} %get-tuple-element.11, bf16[6144,1536]{1,0:T(8,128)(2,1)} %param.7), kind=kOutput, calls=%fused_computation.25 | convolution fusion | flops 9663676416 | bytes 33030144 | tf_op jit(solution)/shard_map/dot_general | solution.py:21
  328.0 0.0 reduce-scatter.2.cloned.1.call-update
  328.1 16.3 %fusion = bf16[6144,1536]{0,1:T(8,128)(2,1)} fusion(bf16[512,1536]{1,0:T(8,128)(2,1)S(1)} %get-tuple-element.11, bf16[512,6144]{1,0:T(8,128)(2,1)} %all-gather.5.cloned.1.call-done), kind=kOutput, calls=%fused_computation.2 | convolution fusion | flops 9673113600 | bytes 26738688 | tf_op jit(solution)/shard_map/dot_general | solution.py:27
  344.4 0.0 copy-start
  344.4 25.3 %copy.9 = bf16[6144,1536]{1,0:T(8,128)(2,1)} copy(bf16[6144,1536]{0,1:T(8,128)(2,1)} %fusion) | data formatting | bytes 37748736
  369.7 0.0 copy-done
  369.7 16.3 %convolution_convert_fusion = bf16[1536,6144]{1,0:T(8,128)(2,1)} fusion(bf16[512,6144]{1,0:T(8,128)(2,1)} %all-gather.3.cloned.1.call-done, f32[512,1536]{1,0:T(8,128)S(1)} %copy-done, f32[1536]{0:T(1024)S(1)} %copy-done.1), kind=kOutput, calls=%fused_computation | convolution fusion | flops 9680977920 | bytes 28317696 | tf_op jit(solution)/shard_map/dot_general | solution.py:27
  386.0 77.0 %reduce-scatter.2.cloned.1.call-done = f32[32,6144]{1,0:T(8,128)} async-done(((f32[512,6144]{1,0:T(8,128)}), f32[32,6144]{1,0:T(8,128)}) %reduce-scatter.2.cloned.1.call-update) | async-done | bytes 786448 | tf_op jit(solution)/shard_map/reduce_scatter | solution.py:47
  463.0 1.9 convert_element_type.22
Async XLA Ops:
  7.2 67.7 %all-gather.3.cloned.1.call-start = ((), (), s32[]{:S(2)}) async-start(), calls=%async_computation.1 | async-start | bytes 6684672 | tf_op jit(solution)/shard_map/all_gather | solution.py:35
  7.9 129.7 %all-gather.5.cloned.1.call-start = ((), (), s32[]{:S(2)}) async-start(), calls=%async_computation.2 | async-start | bytes 6684672 | tf_op jit(solution)/shard_map/all_gather | solution.py:34
  8.6 298.2 %all-reduce.3.cloned.1.call-start = ((), (), s32[]{:S(2)}) async-start(), calls=%async_computation.4 | async-start | bytes 12582912 | tf_op jit(solution)/shard_map/psum | solution.py:42
  154.5 152.3 %copy-start.1 = (f32[1536]{0:T(1024)S(1)}, f32[1536]{0:T(1024)}, u32[]{:S(2)}) copy-start(f32[1536]{0:T(1024)} %param.8) | copy-start | bytes 18436
  154.6 308.4 %reduce-scatter.2.cloned.1.call-start = ((), (), s32[]{:S(2)}) async-start(), calls=%async_computation.3 | async-start | bytes 13369344 | tf_op jit(solution)/shard_map/reduce_scatter | solution.py:47
  344.4 25.3 %copy-start = (f32[512,1536]{1,0:T(8,128)S(1)}, f32[512,1536]{1,0:T(8,128)}, u32[]{:S(2)}) copy-start(f32[512,1536]{1,0:T(8,128)} %get-tuple-element.9) | copy-start | bytes 9437188
Sparse Core Ops, SparseCore 0:
  10.3 64.5 all-gather.2
  77.1 60.4 all-gather.4
  154.7 152.1 all-reduce.2
  328.2 134.7 reduce-scatter.1
where the time goes:
time: 472 us; the launch traced here: 471 us
  waiting for transfers between devices  343 us (73%)
  matrix products  82.7 us (18%)
  local copies, waits for them, and re-layouts  25.3 us (5%)
  between operations  13.8 us (3%)
  other arithmetic  6.64 us (1%)
    psum x1, waiting for transfers between devices, shards(): back_signal = lax.psum(signal_part, 'dp')  152 us
    reduce_scatter x1, waiting for transfers between devices, shards(): lax.psum_scatter(times_transpose(proj_grad, w_in), ('pipe', 'tensor'), sc...  77 us
    all_gather x1, waiting for transfers between devices, shards(): lax.all_gather(out_grad, ('pipe', 'tensor'), axis=0, tiled=True)  66.2 us
    all_gather x1, waiting for transfers between devices, shards(): lax.all_gather(tokens, ('pipe', 'tensor'), axis=0, tiled=True)  46 us
    dot_general x2, matrix products, times_transpose(): lax.dot_general(left, right, (((1,), (1,)), ((), ())), preferred_element_...  33.2 us
    dot_general x2, matrix products, over_rows(): lax.dot_general(left, right, (((0,), (0,)), ((), ())), preferred_element_...  32.6 us
    unnamed x5, local copies, waits for them, and re-layouts  25.3 us
    dot_general x1, matrix products, shards(): proj_part = jnp.dot(tok_all, w_in, preferred_element_type=jnp.float32)  16.9 us
  transfers between devices with their start and end apart: 4, of which 4 were waited for; matrix products, arithmetic and copies ran while one was open for 16% of the time, Pallas kernels for 0%

commit v1 on v0

v1 whole, which is shorter than its diff:
```python
import jax
import jax.numpy as jnp
from jax import lax
from jax.sharding import PartitionSpec as P

tanh_scale = 0.7978845608028654
cubic_coef = 0.044715
ROWS = ("pipe", "tensor")
bf16, f32 = jnp.bfloat16, jnp.float32


def gelu_pair(value):
    inner = tanh_scale * (value + cubic_coef * value * value * value)
    tangent = jnp.tanh(inner)
    result = 0.5 * value * (1.0 + tangent)
    slope = 0.5 * (1.0 + tangent) + 0.5 * value * (1.0 - tangent * tangent) * tanh_scale * (
        1.0 + 3.0 * cubic_coef * value * value
    )
    return (result, slope)


def times_transpose(left, right):
    return lax.dot_general(
        left, right, (((1,), (1,)), ((), ())), preferred_element_type=f32
    )


def over_rows(left, right):
    return lax.dot_general(
        left, right, (((0,), (0,)), ((), ())), preferred_element_type=f32
    )


def shards_plain(tokens, out_grad, w_in, b_in, w_out):
    tok_all, grad_all = (
        lax.all_gather(tokens, ROWS, axis=0, tiled=True),
        lax.all_gather(out_grad, ROWS, axis=0, tiled=True),
    )
    proj_part = jnp.dot(tok_all, w_in, preferred_element_type=f32)
    signal_part = times_transpose(grad_all, w_out)
    projected = lax.psum(proj_part, "dp") + b_in
    active_f, derivative = gelu_pair(projected)
    activated = active_f.astype(bf16)
    back_signal = lax.psum(signal_part, "dp")
    proj_grad = (back_signal * derivative).astype(bf16)
    w_out_grad = over_rows(activated, grad_all).astype(bf16)
    w_in_grad = over_rows(tok_all, proj_grad).astype(bf16)
    b_in_grad = jnp.sum(proj_grad.astype(f32), axis=0)
    in_total = lax.psum_scatter(
        times_transpose(proj_grad, w_in), ROWS, scatter_dimension=0, tiled=True
    )
    return (in_total.astype(bf16), w_in_grad, w_out_grad, b_in_grad)


class Links:
    def __init__(self, pipe, tensor):
        lines = tensor // 2
        ring = []
        for y in range(lines):
            order = range(pipe) if y % 2 == 0 else range(pipe - 1, -1, -1)
            ring += [z * tensor + y * 2 for z in order]
        self.size = len(ring)
        pairs = list(zip(ring, ring[1:] + ring[:1]))
        self.fw = [(a + c, b + c) for a, b in pairs for c in range(2)]
        self.bw = [(b, a) for a, b in self.fw]
        self.core = [(t, t ^ 1) for t in range(tensor)]

    def forward(self, x):
        return lax.ppermute(x, ROWS, self.fw)

    def backward(self, x):
        return lax.ppermute(x, ROWS, self.bw)

    def sibling(self, x):
        return lax.ppermute(x, "tensor", self.core)

    def across(self, x):
        return lax.ppermute(x, "dp", [(0, 1), (1, 0)])

    def gather(self, x):
        far = self.size // 2
        half = x.shape[1] // 2
        blocks = [x]
        ahead = behind = x
        for hop in range(1, far):
            ahead, behind = self.forward(ahead), self.backward(behind)
            blocks += [ahead, behind]
        last = jnp.concatenate(
            [self.forward(ahead[:, :half]), self.backward(behind[:, half:])], axis=1
        )
        first = jnp.concatenate(blocks[: 2 * far - 3])
        rest = jnp.concatenate(blocks[2 * far - 3 :] + [last])
        return jnp.concatenate([first, rest, self.sibling(first), self.sibling(rest)])

    def scatter(self, own):
        far = self.size // 2
        rows = own.shape[0] // self.size
        half = own.shape[1] // 2
        block = lambda i: own[i * rows : (i + 1) * rows]
        opposite = block(2 * far - 1)
        down = self.backward(opposite[:, :half].astype(bf16))
        up = self.forward(opposite[:, half:].astype(bf16))
        for hop in range(far - 1, 0, -1):
            at_behind, at_ahead = block(2 * hop - 1), block(2 * hop)
            if hop == far - 1:
                pad = ((0, 0), (0, half))
                down = at_behind + jnp.pad(down.astype(f32), pad)
                up = at_ahead + jnp.pad(up.astype(f32), ((0, 0), (half, 0)))
            else:
                down, up = at_behind + down.astype(f32), at_ahead + up.astype(f32)
            down, up = self.backward(down.astype(bf16)), self.forward(up.astype(bf16))
        return block(0) + down.astype(f32) + up.astype(f32)


def shards_ring(links, parts, tokens, out_grad, w_in, b_in, w_out):
    rows = tokens.shape[0]
    step = rows // parts
    toks, grads, acts, pgs, ins = [], [], [], [], []
    for k in range(parts):
        here = slice(k * step, (k + 1) * step)
        tok = links.gather(tokens[here])
        grad = links.gather(out_grad[here])
        proj = jnp.dot(tok, w_in, preferred_element_type=f32)
        signal = times_transpose(grad, w_out)
        projected = proj + links.across(proj.astype(bf16)).astype(f32) + b_in
        active_f, derivative = gelu_pair(projected)
        back_signal = signal + links.across(signal.astype(bf16)).astype(f32)
        pg = (back_signal * derivative).astype(bf16)
        partial = times_transpose(pg, w_in)
        mine = partial.shape[0] // 2
        own = partial[:mine] + links.sibling(partial[mine:].astype(bf16)).astype(f32)
        ins.append(links.scatter(own).astype(bf16))
        toks.append(tok)
        grads.append(grad)
        acts.append(active_f.astype(bf16))
        pgs.append(pg)
    cat = jnp.concatenate
    w_out_grad = over_rows(cat(acts), cat(grads)).astype(bf16)
    w_in_grad = over_rows(cat(toks), cat(pgs)).astype(bf16)
    b_in_grad = sum(jnp.sum(pg.astype(f32), axis=0) for pg in pgs)
    return (cat(ins), w_in_grad, w_out_grad, b_in_grad)


def solution(mesh):
    in_specs = (
        P(("pipe", "tensor"), "dp"),
        P(("pipe", "tensor"), "dp"),
        P("dp", ("pipe", "tensor")),
        P(("pipe", "tensor")),
        P(("pipe", "tensor"), "dp"),
    )
    out_specs = (
        P(("pipe", "tensor"), "dp"),
        P("dp", ("pipe", "tensor")),
        P(("pipe", "tensor"), "dp"),
        P(("pipe", "tensor")),
    )
    pipe, dp, tensor = (mesh.shape[a] for a in ("pipe", "dp", "tensor"))
    if dp == 2 and tensor == 4:
        links = Links(pipe, tensor)
        body = lambda *args: shards_ring(links, 2, *args)
    else:
        body = shards_plain
    return jax.shard_map(body, mesh=mesh, in_specs=in_specs, out_specs=out_specs, check_vma=False)
```

time: 472 us -> 270 us (0.57)
  waiting for transfers between devices: 343 us -> 86.7 us
  starting transfers between devices: 0.34 us -> 55.6 us
  between operations: 13.8 us -> 1.16 us
  matrix products: 82.7 us -> 90.8 us
    psum x1 -> x0, waiting for transfers between devices: 152 us -> none  [shards(): back_signal = lax.psum(signal_part, 'dp')]
    all_gather x2 -> x0, waiting for transfers between devices: 112 us -> none  [the longest x1 66.2 us: shards(): lax.all_gather(out_grad, ('pipe', 'tensor'), axis=0, tiled=True)]
    ppermute x0 -> x62, waiting for transfers between devices: none -> 86.7 us  [the longest x24 35.4 us: forward(): return lax.ppermute(x, ROWS, self.fw)]
    reduce_scatter x1 -> x0, waiting for transfers between devices: 77 us -> none  [shards(): lax.psum_scatter(times_transpose(proj_grad, w_in), ('pipe', 'tensor'), sc...]
    ppermute x0 -> x62, starting transfers between devices: none -> 55.6 us  [the longest x24 27.4 us: backward(): return lax.ppermute(x, ROWS, self.bw)]
    dot_general x2 -> x4, matrix products: 33.2 us -> 39.2 us  [times_transpose(): lax.dot_general(left, right, (((1,), (1,)), ((), ())), preferred_element_...]
    unnamed x5 -> x60, local copies, waits for them, and re-layouts: 25.3 us -> 21.1 us
    dot_general x1 -> x2, matrix products: 16.9 us -> 19 us  [shards_ring(): proj = jnp.dot(tok, w_in, preferred_element_type=f32)]
  transfers between devices with their start and end apart: 4 -> 62, of which waited for: 4 -> 31; matrix products, arithmetic and copies ran while one was open for 16% -> 39% of each run, Pallas kernels for 0% -> 0%
where the time goes in v1:
time: 270 us; the launch traced here: 269 us
  matrix products  90.8 us (34%)
  waiting for transfers between devices  86.7 us (32%)
  starting transfers between devices  55.6 us (21%)
  local copies, waits for them, and re-layouts  26.1 us (10%)
  other arithmetic  9.1 us (3%)
    dot_general x4, matrix products, times_transpose(): lax.dot_general(left, right, (((1,), (1,)), ((), ())), preferred_element_...  39.2 us
    ppermute x24, waiting for transfers between devices, forward(): return lax.ppermute(x, ROWS, self.fw)  35.4 us
    dot_general x2, matrix products, over_rows(): lax.dot_general(left, right, (((0,), (0,)), ((), ())), preferred_element_...  32.6 us
    ppermute x24, waiting for transfers between devices, backward(): return lax.ppermute(x, ROWS, self.bw)  29.4 us
    ppermute x24, starting transfers between devices, backward(): return lax.ppermute(x, ROWS, self.bw)  27.4 us
    ppermute x24, starting transfers between devices, forward(): return lax.ppermute(x, ROWS, self.fw)  23.1 us
    ppermute x4, waiting for transfers between devices, across(): return lax.ppermute(x, 'dp', [(0, 1), (1, 0)])  21.9 us
    unnamed x60, local copies, waits for them, and re-layouts  21.1 us
  transfers between devices with their start and end apart: 62, of which 31 were waited for; matrix products, arithmetic and copies ran while one was open for 39% of the time, Pallas kernels for 0%

profile of v1, /device:TPU:0, one launch (start us, length us, event | category | flops | bytes accessed | tf_op | source)
XLA Modules:
  0.0 269.5 jit_solution(2824535117702424542)
XLA Ops:
  1.6 3.0 %collective-permute-start.12 = (bf16[16,6144]{1,0:T(8,128)(2,1)S(1)}, bf16[16,6144]{1,0:T(8,128)(2,1)S(1)}, u32[]{:S(2)}, u32[]{:S(2)}) collective-permute-start(bf16[16,6144]{1,0:T(8,128)(2,1)S(1)} %get-tuple-element.57), channel_id=1, source_target_pairs={{8,0},{9,1},{16,8},{17,9},{24,16},{25,17},{26,24},{27,25},{18,26},... | collective-permute-start | bytes 589832 | tf_op jit(solution)/shard_map/ppermute | solution.py:72
  5.7 2.0 collective-permute-start.1
  7.8 2.6 collective-permute-done.12
  10.4 2.0 collective-permute-start.14
  12.5 2.1 collective-permute-done.1
  14.6 2.0 collective-permute-start.3
  16.9 3.9 %collective-permute-done.13 = bf16[16,6144]{1,0:T(8,128)(2,1)S(1)} collective-permute-done((bf16[16,6144]{1,0:T(8,128)(2,1)S(1)}, bf16[16,6144]{1,0:T(8,128)(2,1)S(1)}, u32[]{:S(2)}, u32[]{:S(2)}) %collective-permute-start.13) | collective-permute-done | bytes 196640 | tf_op jit(solution)/shard_map/ppermute | solution.py:69
  21.1 1.6 collective-permute-start.16
  23.8 1.6 collective-permute-start.5
  25.4 3.4 %collective-permute-done.16 = bf16[16,6144]{1,0:T(8,128)(2,1)S(1)} collective-permute-done((bf16[16,6144]{1,0:T(8,128)(2,1)S(1)}, bf16[16,6144]{1,0:T(8,128)(2,1)S(1)}, u32[]{:S(2)}, u32[]{:S(2)}) %collective-permute-start.16) | collective-permute-done | bytes 196640 | tf_op jit(solution)/shard_map/ppermute | solution.py:72
  31.3 1.7 collective-permute-done.5
  33.2 1.6 collective-permute-done.4
  39.5 1.7 collective-permute-done.6
  42.3 1.6 collective-permute-start.43
  48.4 9.1 %fusion.44 = (bf16[256,1536]{1,0:T(8,128)(2,1)S(1)}, f32[256,1536]{1,0:T(8,128)S(1)}) fusion(bf16[256,6144]{1,0:T(8,128)(2,1)S(1)} %get-tuple-element.41, bf16[6144,1536]{1,0:T(8,128)(2,1)} %param.7), kind=kOutput, calls=%fused_computation.185 | convolution fusion | flops 4832231424 | bytes 24379392 | tf_op jit(solution)/shard_map/dot_general | solution.py:123
  59.0 10.7 %fusion.45 = (bf16[256,1536]{1,0:T(8,128)(2,1)}, f32[256,1536]{1,0:T(8,128)S(1)}) fusion(bf16[256,6144]{1,0:T(8,128)(2,1)} %copy-done.5, bf16[1536,6144]{1,0:T(8,128)(2,1)} %param.9), kind=kOutput, calls=%fused_computation.186 | convolution fusion | flops 4832231424 | bytes 24379392 | tf_op jit(solution)/shard_map/dot_general | solution.py:23
  70.3 1.6 collective-permute-start.45
  76.9 2.1 collective-permute-done.44
  80.8 3.8 %collective-permute-done.33 = bf16[16,6144]{1,0:T(8,128)(2,1)S(1)} collective-permute-done((bf16[16,6144]{1,0:T(8,128)(2,1)S(1)}, bf16[16,6144]{1,0:T(8,128)(2,1)S(1)}, u32[]{:S(2)}, u32[]{:S(2)}) %collective-permute-start.33) | collective-permute-done | bytes 196640 | tf_op jit(solution)/shard_map/ppermute | solution.py:69
  88.2 4.4 %collective-permute-done.46 = bf16[16,6144]{1,0:T(8,128)(2,1)S(1)} collective-permute-done((bf16[16,6144]{1,0:T(8,128)(2,1)S(1)}, bf16[16,6144]{1,0:T(8,128)(2,1)S(1)}, u32[]{:S(2)}, u32[]{:S(2)}) %collective-permute-start.46) | collective-permute-done | bytes 196640 | tf_op jit(solution)/shard_map/ppermute | solution.py:69
  96.1 4.5 %collective-permute-done.35 = bf16[16,6144]{1,0:T(8,128)(2,1)S(1)} collective-permute-done((bf16[16,6144]{1,0:T(8,128)(2,1)S(1)}, bf16[16,6144]{1,0:T(8,128)(2,1)S(1)}, u32[]{:S(2)}, u32[]{:S(2)}) %collective-permute-start.35) | collective-permute-done | bytes 196640 | tf_op jit(solution)/shard_map/ppermute | solution.py:69
  101.5 2.0 collective-permute-start.48
  106.2 1.9 collective-permute-start.37
  112.0 3.5 %collective-permute-done.38 = bf16[16,3072]{1,0:T(8,128)(2,1)S(1)} collective-permute-done((bf16[16,3072]{1,0:T(8,128)(2,1)S(1)}, bf16[16,3072]{1,0:T(8,128)(2,1)S(1)}, u32[]{:S(2)}, u32[]{:S(2)}) %collective-permute-start.38) | collective-permute-done | bytes 98336 | tf_op jit(solution)/shard_map/ppermute | solution.py:72
  118.8 9.9 %fusion.46 = (bf16[256,1536]{1,0:T(8,128)(2,1)}, f32[256,1536]{1,0:T(8,128)S(1)}) fusion(bf16[256,6144]{1,0:T(8,128)(2,1)S(1)} %get-tuple-element.39, bf16[6144,1536]{1,0:T(8,128)(2,1)} %param.7), kind=kOutput, calls=%fused_computation.187 | convolution fusion | flops 4832231424 | bytes 24379392 | tf_op jit(solution)/shard_map/dot_general | solution.py:123
  132.9 9.9 %fusion.47 = (bf16[256,1536]{1,0:T(8,128)(2,1)S(1)}, f32[256,1536]{1,0:T(8,128)S(1)}) fusion(bf16[256,6144]{1,0:T(8,128)(2,1)} %get-tuple-element.35, bf16[1536,6144]{1,0:T(8,128)(2,1)} %param.9), kind=kOutput, calls=%fused_computation.188 | convolution fusion | flops 4832231424 | bytes 24379392 | tf_op jit(solution)/shard_map/dot_general | solution.py:23
  143.4 5.9 %collective-permute-done.52 = bf16[256,1536]{1,0:T(8,128)(2,1)S(1)} collective-permute-done((bf16[256,1536]{1,0:T(8,128)(2,1)}, bf16[256,1536]{1,0:T(8,128)(2,1)S(1)}, u32[]{:S(2)}, u32[]{:S(2)}) %collective-permute-start.52) | collective-permute-done | bytes 786464 | tf_op jit(solution)/shard_map/ppermute | solution.py:78
  149.4 15.9 %collective-permute-done.41 = bf16[256,1536]{1,0:T(8,128)(2,1)S(1)} collective-permute-done((bf16[256,1536]{1,0:T(8,128)(2,1)S(1)}, bf16[256,1536]{1,0:T(8,128)(2,1)S(1)}, u32[]{:S(2)}, u32[]{:S(2)}) %collective-permute-start.41) | collective-permute-done | bytes 786464 | tf_op jit(solution)/shard_map/ppermute | solution.py:78
  165.3 3.8 %convert_reduce_fusion.1 = (f32[1536]{0:T(1024)S(1)}, bf16[256,1536]{1,0:T(8,128)(2,1)S(1)}, bf16[256,1536]{1,0:T(8,128)(2,1)}, bf16[256,1536]{1,0:T(8,128)(2,1)...) fusion(f32[1536]{0:T(1024)S(1)} %copy-done.6, f32[256,1536]{1,0:T(8,128)S(1)} %get-tuple-element.142, ...), kind=kLoop, calls=%fused_computation.31 | loop fusion | flops 22017024 | bytes 12601344 | tf_op jit(solution)/shard_map/reduce_sum | solution.py:140
  169.1 9.6 %fusion.48 = f32[256,6144]{1,0:T(8,128)S(1)} fusion(bf16[256,1536]{1,0:T(8,128)(2,1)S(1)} %get-tuple-element.7, bf16[6144,1536]{1,0:T(8,128)(2,1)} %param.7), kind=kOutput, calls=%fused_computation.189 | convolution fusion | flops 4831838208 | bytes 25952256 | tf_op jit(solution)/shard_map/dot_general | solution.py:23
  181.7 9.0 %fusion.49 = f32[256,6144]{1,0:T(8,128)S(1)} fusion(bf16[256,1536]{1,0:T(8,128)(2,1)S(1)} %get-tuple-element.140, bf16[6144,1536]{1,0:T(8,128)(2,1)} %param.7), kind=kOutput, calls=%fused_computation.190 | convolution fusion | flops 4831838208 | bytes 25952256 | tf_op jit(solution)/shard_map/dot_general | solution.py:23
  192.1 16.3 %convolution_convert_fusion.1 = bf16[6144,1536]{1,0:T(8,128)(2,1)} fusion(bf16[512,6144]{1,0:T(8,128)(2,1)} %get-tuple-element.38, bf16[256,1536]{1,0:T(8,128)(2,1)} %copy-done.2, bf16[256,1536]{1,0:T(8,128)(2,1)} %copy-done.1), kind=kOutput, calls=%fused_computation.1 | convolution fusion | flops 9676259328 | bytes 26738688 | tf_op jit(solution)/shard_map/dot_general | solution.py:29
  209.0 16.3 %convolution_convert_fusion = bf16[1536,6144]{1,0:T(8,128)(2,1)} fusion(bf16[512,6144]{1,0:T(8,128)(2,1)} %get-tuple-element.34, bf16[256,1536]{1,0:T(8,128)(2,1)} %get-tuple-element.138, bf16[256,1536]{1,0:T(8,128)(2,1)} %get-tuple-element.20), kind=kOutput, calls=%fused_computation | convolution fusion | flops 9676259328 | bytes 26738688 | tf_op jit(solution)/shard_map/dot_general | solution.py:29
  225.3 2.8 %fusion.40 = (bf16[128,6144]{1,0:T(8,128)(2,1)S(1)}, f32[128,6144]{1,0:T(8,128)S(1)}) fusion(bf16[128,6144]{1,0:T(8,128)(2,1)} %collective-permute-done.22, f32[256,6144]{1,0:T(8,128)} %copy-done), kind=kLoop, calls=%fused_computation.181 | loop fusion | flops 2359296 | bytes 9437184 | tf_op jit(solution)/shard_map/convert.12
  234.0 1.7 collective-permute-done.54
  236.1 5.4 %collective-permute-done.24 = bf16[16,6144]{1,0:T(8,128)(2,1)S(1)} collective-permute-done((bf16[16,6144]{1,0:T(8,128)(2,1)S(1)}, bf16[16,6144]{1,0:T(8,128)(2,1)S(1)}, u32[]{:S(2)}, u32[]{:S(2)}) %collective-permute-start.24) | collective-permute-done | bytes 196640 | tf_op jit(solution)/shard_map/ppermute | solution.py:72
  241.9 1.7 collective-permute-start.28
  243.7 2.1 collective-permute-done.55
  246.1 1.7 collective-permute-start.59
  247.9 2.1 collective-permute-done.25
  250.3 1.7 collective-permute-start.29
  252.1 2.1 collective-permute-done.56
  254.6 1.7 collective-permute-start.60
  257.3 1.9 collective-permute-start.30
  259.2 3.2 %collective-permute-done.60 = bf16[16,6144]{1,0:T(8,128)(2,1)S(1)} collective-permute-done((bf16[16,6144]{1,0:T(8,128)(2,1)S(1)}, bf16[16,6144]{1,0:T(8,128)(2,1)S(1)}, u32[]{:S(2)}, u32[]{:S(2)}) %collective-permute-start.60) | collective-permute-done | bytes 196640 | tf_op jit(solution)/shard_map/ppermute | solution.py:69
  262.4 1.8 collective-permute-start.61
  264.2 2.3 collective-permute-done.30
  266.6 2.0 collective-permute-done.61
  (177 shorter events, 62.9 us)
Async XLA Ops:
  1.6 8.8 %collective-permute-start.12 = (bf16[16,6144]{1,0:T(8,128)(2,1)S(1)}, bf16[16,6144]{1,0:T(8,128)(2,1)S(1)}, u32[]{:S(2)}, u32[]{:S(2)}) collective-permute-start(bf16[16,6144]{1,0:T(8,128)(2,1)S(1)} %get-tuple-element.57), channel_id=1, source_target_pairs={{8,0},{9,1},{16,8},{17,9},{24,16},{25,17},{26,24},{27,25},{18,26},... | collective-permute-start | bytes 589832 | tf_op jit(solution)/shard_map/ppermute | solution.py:72
  4.6 7.8 %collective-permute-start.11 = (bf16[16,6144]{1,0:T(8,128)(2,1)S(1)}, bf16[16,6144]{1,0:T(8,128)(2,1)S(1)}, u32[]{:S(2)}, u32[]{:S(2)}) collective-permute-start(bf16[16,6144]{1,0:T(8,128)(2,1)S(1)} %get-tuple-element.57), channel_id=1, source_target_pairs={{0,8},{1,9},{8,16},{9,17},{16,24},{17,25},{24,26},{25,27},{26,18},... | collective-permute-start | bytes 589832 | tf_op jit(solution)/shard_map/ppermute | solution.py:69
  5.7 8.9 %collective-permute-start.1 = (bf16[16,6144]{1,0:T(8,128)(2,1)S(1)}, bf16[16,6144]{1,0:T(8,128)(2,1)S(1)}, u32[]{:S(2)}, u32[]{:S(2)}) collective-permute-start(bf16[16,6144]{1,0:T(8,128)(2,1)S(1)} %get-tuple-element.49), channel_id=1, source_target_pairs={{8,0},{9,1},{16,8},{17,9},{24,16},{25,17},{26,24},{27,25},{18,26},... | collective-permute-start | bytes 589832 | tf_op jit(solution)/shard_map/ppermute | solution.py:72
  7.7 9.0 %collective-permute-start = (bf16[16,6144]{1,0:T(8,128)(2,1)S(1)}, bf16[16,6144]{1,0:T(8,128)(2,1)S(1)}, u32[]{:S(2)}, u32[]{:S(2)}) collective-permute-start(bf16[16,6144]{1,0:T(8,128)(2,1)S(1)} %get-tuple-element.49), channel_id=1, source_target_pairs={{0,8},{1,9},{8,16},{9,17},{16,24},{17,25},{24,26},{25,27},{26,18},... | collective-permute-start | bytes 589832 | tf_op jit(solution)/shard_map/ppermute | solution.py:69
  10.4 10.5 %collective-permute-start.14 = (bf16[16,6144]{1,0:T(8,128)(2,1)S(1)}, bf16[16,6144]{1,0:T(8,128)(2,1)S(1)}, u32[]{:S(2)}, u32[]{:S(2)}) collective-permute-start(bf16[16,6144]{1,0:T(8,128)(2,1)S(1)} %collective-permute-done.12), channel_id=1, source_target_pairs={{8,0},{9,1},{16,8},{17,9},{24,16},{25,17},{26,24},{27,25},{18,26},... | collective-permute-start | bytes 589832 | tf_op jit(solution)/shard_map/ppermute | solution.py:72
  12.5 8.4 %collective-permute-start.13 = (bf16[16,6144]{1,0:T(8,128)(2,1)S(1)}, bf16[16,6144]{1,0:T(8,128)(2,1)S(1)}, u32[]{:S(2)}, u32[]{:S(2)}) collective-permute-start(bf16[16,6144]{1,0:T(8,128)(2,1)S(1)} %collective-permute-done.11), channel_id=1, source_target_pairs={{0,8},{1,9},{8,16},{9,17},{16,24},{17,25},{24,26},{25,27},{26,18},... | collective-permute-start | bytes 589832 | tf_op jit(solution)/shard_map/ppermute | solution.py:69
  14.6 9.0 %collective-permute-start.3 = (bf16[16,6144]{1,0:T(8,128)(2,1)S(1)}, bf16[16,6144]{1,0:T(8,128)(2,1)S(1)}, u32[]{:S(2)}, u32[]{:S(2)}) collective-permute-start(bf16[16,6144]{1,0:T(8,128)(2,1)S(1)} %collective-permute-done.1), channel_id=1, source_target_pairs={{8,0},{9,1},{16,8},{17,9},{24,16},{25,17},{26,24},{27,25},{18,26},... | collective-permute-start | bytes 589832 | tf_op jit(solution)/shard_map/ppermute | solution.py:72
  16.7 7.0 %collective-permute-start.2 = (bf16[16,6144]{1,0:T(8,128)(2,1)S(1)}, bf16[16,6144]{1,0:T(8,128)(2,1)S(1)}, u32[]{:S(2)}, u32[]{:S(2)}) collective-permute-start(bf16[16,6144]{1,0:T(8,128)(2,1)S(1)} %collective-permute-done), channel_id=1, source_target_pairs={{0,8},{1,9},{8,16},{9,17},{16,24},{17,25},{24,26},{25,27},{26,18},... | collective-permute-start | bytes 589832 | tf_op jit(solution)/shard_map/ppermute | solution.py:69
  21.0 20.4 %collective-permute-start.19 = (bf16[80,6144]{1,0:T(8,128)(2,1)S(1)}, bf16[80,6144]{1,0:T(8,128)(2,1)S(1)}, u32[]{:S(2)}, u32[]{:S(2)}) collective-permute-start(bf16[80,6144]{1,0:T(8,128)(2,1)S(1)} %get-tuple-element.112), channel_id=1, source_target_pairs={{0,1},{1,0},{2,3},{3,2},{4,5},{5,4},{6,7},{7,6},{8,9},{9,8},{10,11... | collective-permute-start | bytes 2949128 | tf_op jit(solution)/shard_map/ppermute | solution.py:75
  21.1 7.8 %collective-permute-start.16 = (bf16[16,6144]{1,0:T(8,128)(2,1)S(1)}, bf16[16,6144]{1,0:T(8,128)(2,1)S(1)}, u32[]{:S(2)}, u32[]{:S(2)}) collective-permute-start(bf16[16,6144]{1,0:T(8,128)(2,1)S(1)} %collective-permute-done.14), channel_id=1, source_target_pairs={{8,0},{9,1},{16,8},{17,9},{24,16},{25,17},{26,24},{27,25},{18,26},... | collective-permute-start | bytes 589832 | tf_op jit(solution)/shard_map/ppermute | solution.py:72
  22.7 7.0 %collective-permute-start.15 = (bf16[16,6144]{1,0:T(8,128)(2,1)S(1)}, bf16[16,6144]{1,0:T(8,128)(2,1)S(1)}, u32[]{:S(2)}, u32[]{:S(2)}) collective-permute-start(bf16[16,6144]{1,0:T(8,128)(2,1)S(1)} %collective-permute-done.13), channel_id=1, source_target_pairs={{0,8},{1,9},{8,16},{9,17},{16,24},{17,25},{24,26},{25,27},{26,18},... | collective-permute-start | bytes 589832 | tf_op jit(solution)/shard_map/ppermute | solution.py:69
  23.7 20.6 %collective-permute-start.8 = (bf16[80,6144]{1,0:T(8,128)(2,1)S(1)}, bf16[80,6144]{1,0:T(8,128)(2,1)S(1)}, u32[]{:S(2)}, u32[]{:S(2)}) collective-permute-start(bf16[80,6144]{1,0:T(8,128)(2,1)S(1)} %get-tuple-element.80), channel_id=1, source_target_pairs={{0,1},{1,0},{2,3},{3,2},{4,5},{5,4},{6,7},{7,6},{8,9},{9,8},{10,11... | collective-permute-start | bytes 2949128 | tf_op jit(solution)/shard_map/ppermute | solution.py:75
  23.8 9.2 %collective-permute-start.5 = (bf16[16,6144]{1,0:T(8,128)(2,1)S(1)}, bf16[16,6144]{1,0:T(8,128)(2,1)S(1)}, u32[]{:S(2)}, u32[]{:S(2)}) collective-permute-start(bf16[16,6144]{1,0:T(8,128)(2,1)S(1)} %collective-permute-done.3), channel_id=1, source_target_pairs={{8,0},{9,1},{16,8},{17,9},{24,16},{25,17},{26,24},{27,25},{18,26},... | collective-permute-start | bytes 589832 | tf_op jit(solution)/shard_map/ppermute | solution.py:72
  28.8 6.0 %collective-permute-start.4 = (bf16[16,6144]{1,0:T(8,128)(2,1)S(1)}, bf16[16,6144]{1,0:T(8,128)(2,1)S(1)}, u32[]{:S(2)}, u32[]{:S(2)}) collective-permute-start(bf16[16,6144]{1,0:T(8,128)(2,1)S(1)} %collective-permute-done.2), channel_id=1, source_target_pairs={{0,8},{1,9},{8,16},{9,17},{16,24},{17,25},{24,26},{25,27},{26,18},... | collective-permute-start | bytes 589832 | tf_op jit(solution)/shard_map/ppermute | solution.py:69
  29.7 6.8 %collective-permute-start.18 = (bf16[16,3072]{1,0:T(8,128)(2,1)S(1)}, bf16[16,3072]{1,0:T(8,128)(2,1)S(1)}, u32[]{:S(2)}, u32[]{:S(2)}) collective-permute-start(bf16[16,3072]{1,0:T(8,128)(2,1)S(1)} %slice.151), channel_id=1, source_target_pairs={{8,0},{9,1},{16,8},{17,9},{24,16},{25,17},{26,24},{27,25},{18,26},... | collective-permute-start | bytes 294920 | tf_op jit(solution)/shard_map/ppermute | solution.py:72
  42.3 27.4 %collective-permute-start.43 = (bf16[16,6144]{1,0:T(8,128)(2,1)S(1)}, bf16[16,6144]{1,0:T(8,128)(2,1)S(1)}, u32[]{:S(2)}, u32[]{:S(2)}) collective-permute-start(bf16[16,6144]{1,0:T(8,128)(2,1)S(1)} %get-tuple-element.53), channel_id=1, source_target_pairs={{8,0},{9,1},{16,8},{17,9},{24,16},{25,17},{26,24},{27,25},{18,26},... | collective-permute-start | bytes 589832 | tf_op jit(solution)/shard_map/ppermute | solution.py:72
  43.9 26.3 %collective-permute-start.42 = (bf16[16,6144]{1,0:T(8,128)(2,1)S(1)}, bf16[16,6144]{1,0:T(8,128)(2,1)S(1)}, u32[]{:S(2)}, u32[]{:S(2)}) collective-permute-start(bf16[16,6144]{1,0:T(8,128)(2,1)S(1)} %get-tuple-element.53), channel_id=1, source_target_pairs={{0,8},{1,9},{8,16},{9,17},{16,24},{17,25},{24,26},{25,27},{26,18},... | collective-permute-start | bytes 589832 | tf_op jit(solution)/shard_map/ppermute | solution.py:69
  45.5 27.8 %collective-permute-start.32 = (bf16[16,6144]{1,0:T(8,128)(2,1)S(1)}, bf16[16,6144]{1,0:T(8,128)(2,1)S(1)}, u32[]{:S(2)}, u32[]{:S(2)}) collective-permute-start(bf16[16,6144]{1,0:T(8,128)(2,1)S(1)} %get-tuple-element.45), channel_id=1, source_target_pairs={{8,0},{9,1},{16,8},{17,9},{24,16},{25,17},{26,24},{27,25},{18,26},... | collective-permute-start | bytes 589832 | tf_op jit(solution)/shard_map/ppermute | solution.py:72
  47.1 26.6 %collective-permute-start.31 = (bf16[16,6144]{1,0:T(8,128)(2,1)S(1)}, bf16[16,6144]{1,0:T(8,128)(2,1)S(1)}, u32[]{:S(2)}, u32[]{:S(2)}) collective-permute-start(bf16[16,6144]{1,0:T(8,128)(2,1)S(1)} %get-tuple-element.45), channel_id=1, source_target_pairs={{0,8},{1,9},{8,16},{9,17},{16,24},{17,25},{24,26},{25,27},{26,18},... | collective-permute-start | bytes 589832 | tf_op jit(solution)/shard_map/ppermute | solution.py:69
  57.5 85.9 %collective-permute-start.21 = (bf16[256,1536]{1,0:T(8,128)(2,1)S(1)}, bf16[256,1536]{1,0:T(8,128)(2,1)S(1)}, u32[]{:S(2)}, u32[]{:S(2)}) collective-permute-start(bf16[256,1536]{1,0:T(8,128)(2,1)S(1)} %get-tuple-element.141), channel_id=1, source_target_pairs={{0,4},{4,0},{1,5},{5,1},{2,6},{6,2},{3,7},{7,3},{8,12},{12,8},{9,1... | collective-permute-start | bytes 2359304 | tf_op jit(solution)/shard_map/ppermute | solution.py:78
  69.7 73.7 %collective-permute-start.10 = (bf16[256,1536]{1,0:T(8,128)(2,1)}, bf16[256,1536]{1,0:T(8,128)(2,1)S(1)}, u32[]{:S(2)}, u32[]{:S(2)}) collective-permute-start(bf16[256,1536]{1,0:T(8,128)(2,1)} %get-tuple-element.143), channel_id=1, source_target_pairs={{0,4},{4,0},{1,5},{5,1},{2,6},{6,2},{3,7},{7,3},{8,12},{12,8},{9,1... | collective-permute-start | bytes 2359304 | tf_op jit(solution)/shard_map/ppermute | solution.py:78
  70.3 9.8 %collective-permute-start.45 = (bf16[16,6144]{1,0:T(8,128)(2,1)S(1)}, bf16[16,6144]{1,0:T(8,128)(2,1)S(1)}, u32[]{:S(2)}, u32[]{:S(2)}) collective-permute-start(bf16[16,6144]{1,0:T(8,128)(2,1)S(1)} %collective-permute-done.43), channel_id=1, source_target_pairs={{8,0},{9,1},{16,8},{17,9},{24,16},{25,17},{26,24},{27,25},{18,26},... | collective-permute-start | bytes 589832 | tf_op jit(solution)/shard_map/ppermute | solution.py:72
  73.3 5.7 %collective-permute-start.44 = (bf16[16,6144]{1,0:T(8,128)(2,1)S(1)}, bf16[16,6144]{1,0:T(8,128)(2,1)S(1)}, u32[]{:S(2)}, u32[]{:S(2)}) collective-permute-start(bf16[16,6144]{1,0:T(8,128)(2,1)S(1)} %collective-permute-done.42), channel_id=1, source_target_pairs={{0,8},{1,9},{8,16},{9,17},{16,24},{17,25},{24,26},{25,27},{26,18},... | collective-permute-start | bytes 589832 | tf_op jit(solution)/shard_map/ppermute | solution.py:69
  73.7 13.2 %collective-permute-start.34 = (bf16[16,6144]{1,0:T(8,128)(2,1)S(1)}, bf16[16,6144]{1,0:T(8,128)(2,1)S(1)}, u32[]{:S(2)}, u32[]{:S(2)}) collective-permute-start(bf16[16,6144]{1,0:T(8,128)(2,1)S(1)} %collective-permute-done.32), channel_id=1, source_target_pairs={{8,0},{9,1},{16,8},{17,9},{24,16},{25,17},{26,24},{27,25},{18,26},... | collective-permute-start | bytes 589832 | tf_op jit(solution)/shard_map/ppermute | solution.py:72
  80.8 35.3 %collective-permute-start.50 = (bf16[80,6144]{1,0:T(8,128)(2,1)S(1)}, bf16[80,6144]{1,0:T(8,128)(2,1)S(1)}, u32[]{:S(2)}, u32[]{:S(2)}) collective-permute-start(bf16[80,6144]{1,0:T(8,128)(2,1)S(1)} %get-tuple-element.96), channel_id=1, source_target_pairs={{0,1},{1,0},{2,3},{3,2},{4,5},{5,4},{6,7},{7,6},{8,9},{9,8},{10,11... | collective-permute-start | bytes 2949128 | tf_op jit(solution)/shard_map/ppermute | solution.py:75
  84.6 9.3 %collective-permute-start.47 = (bf16[16,6144]{1,0:T(8,128)(2,1)S(1)}, bf16[16,6144]{1,0:T(8,128)(2,1)S(1)}, u32[]{:S(2)}, u32[]{:S(2)}) collective-permute-start(bf16[16,6144]{1,0:T(8,128)(2,1)S(1)} %collective-permute-done.45), channel_id=1, source_target_pairs={{8,0},{9,1},{16,8},{17,9},{24,16},{25,17},{26,24},{27,25},{18,26},... | collective-permute-start | bytes 589832 | tf_op jit(solution)/shard_map/ppermute | solution.py:72
  92.6 8.9 %collective-permute-start.36 = (bf16[16,6144]{1,0:T(8,128)(2,1)S(1)}, bf16[16,6144]{1,0:T(8,128)(2,1)S(1)}, u32[]{:S(2)}, u32[]{:S(2)}) collective-permute-start(bf16[16,6144]{1,0:T(8,128)(2,1)S(1)} %collective-permute-done.34), channel_id=1, source_target_pairs={{8,0},{9,1},{16,8},{17,9},{24,16},{25,17},{26,24},{27,25},{18,26},... | collective-permute-start | bytes 589832 | tf_op jit(solution)/shard_map/ppermute | solution.py:72
  93.9 6.7 %collective-permute-start.35 = (bf16[16,6144]{1,0:T(8,128)(2,1)S(1)}, bf16[16,6144]{1,0:T(8,128)(2,1)S(1)}, u32[]{:S(2)}, u32[]{:S(2)}) collective-permute-start(bf16[16,6144]{1,0:T(8,128)(2,1)S(1)} %collective-permute-done.33), channel_id=1, source_target_pairs={{0,8},{1,9},{8,16},{9,17},{16,24},{17,25},{24,26},{25,27},{26,18},... | collective-permute-start | bytes 589832 | tf_op jit(solution)/shard_map/ppermute | solution.py:69
  105.2 25.0 %collective-permute-start.39 = (bf16[80,6144]{1,0:T(8,128)(2,1)S(1)}, bf16[80,6144]{1,0:T(8,128)(2,1)S(1)}, u32[]{:S(2)}, u32[]{:S(2)}) collective-permute-start(bf16[80,6144]{1,0:T(8,128)(2,1)S(1)} %get-tuple-element.64), channel_id=1, source_target_pairs={{0,1},{1,0},{2,3},{3,2},{4,5},{5,4},{6,7},{7,6},{8,9},{9,8},{10,11... | collective-permute-start | bytes 2949128 | tf_op jit(solution)/shard_map/ppermute | solution.py:75
  116.2 15.5 %collective-permute-start.40 = (bf16[48,6144]{1,0:T(8,128)(2,1)S(1)}, bf16[48,6144]{1,0:T(8,128)(2,1)S(1)}, u32[]{:S(2)}, u32[]{:S(2)}) collective-permute-start(bf16[48,6144]{1,0:T(8,128)(2,1)S(1)} %maximum_maximum_fusion.2), channel_id=1, source_target_pairs={{0,1},{1,0},{2,3},{3,2},{4,5},{5,4},{6,7},{7,6},{8,9},{9,8},{10,11... | collective-permute-start | bytes 1769480 | tf_op jit(solution)/shard_map/ppermute | solution.py:75
  128.7 20.6 %collective-permute-start.52 = (bf16[256,1536]{1,0:T(8,128)(2,1)}, bf16[256,1536]{1,0:T(8,128)(2,1)S(1)}, u32[]{:S(2)}, u32[]{:S(2)}) collective-permute-start(bf16[256,1536]{1,0:T(8,128)(2,1)} %get-tuple-element.145), channel_id=1, source_target_pairs={{0,4},{4,0},{1,5},{5,1},{2,6},{6,2},{3,7},{7,3},{8,12},{12,8},{9,1... | collective-permute-start | bytes 2359304 | tf_op jit(solution)/shard_map/ppermute | solution.py:78
  142.8 22.5 %collective-permute-start.41 = (bf16[256,1536]{1,0:T(8,128)(2,1)S(1)}, bf16[256,1536]{1,0:T(8,128)(2,1)S(1)}, u32[]{:S(2)}, u32[]{:S(2)}) collective-permute-start(bf16[256,1536]{1,0:T(8,128)(2,1)S(1)} %get-tuple-element.147), channel_id=1, source_target_pairs={{0,4},{4,0},{1,5},{5,1},{2,6},{6,2},{3,7},{7,3},{8,12},{12,8},{9,1... | collective-permute-start | bytes 2359304 | tf_op jit(solution)/shard_map/ppermute | solution.py:78
  180.2 45.1 %collective-permute-start.22 = (bf16[128,6144]{1,0:T(8,128)(2,1)}, bf16[128,6144]{1,0:T(8,128)(2,1)}, u32[]{:S(2)}, u32[]{:S(2)}) collective-permute-start(bf16[128,6144]{1,0:T(8,128)(2,1)} %slice.241), channel_id=1, source_target_pairs={{0,1},{1,0},{2,3},{3,2},{4,5},{5,4},{6,7},{7,6},{8,9},{9,8},{10,11... | collective-permute-start | bytes 4718600 | tf_op jit(solution)/shard_map/ppermute | solution.py:75
  192.1 38.2 %collective-permute-start.53 = (bf16[128,6144]{1,0:T(8,128)(2,1)}, bf16[128,6144]{1,0:T(8,128)(2,1)S(1)}, u32[]{:S(2)}, u32[]{:S(2)}) collective-permute-start(bf16[128,6144]{1,0:T(8,128)(2,1)} %slice.240), channel_id=1, source_target_pairs={{0,1},{1,0},{2,3},{3,2},{4,5},{5,4},{6,7},{7,6},{8,9},{9,8},{10,11... | collective-permute-start | bytes 4718600 | tf_op jit(solution)/shard_map/ppermute | solution.py:75
  228.7 7.4 %collective-permute-start.27 = (bf16[16,3072]{1,0:T(8,128)(2,1)S(1)}, bf16[16,3072]{1,0:T(8,128)(2,1)S(1)}, u32[]{:S(2)}, u32[]{:S(2)}) collective-permute-start(bf16[16,3072]{1,0:T(8,128)(2,1)S(1)} %get-tuple-element.23), channel_id=1, source_target_pairs={{0,8},{1,9},{8,16},{9,17},{16,24},{17,25},{24,26},{25,27},{26,18},... | collective-permute-start | bytes 294920 | tf_op jit(solution)/shard_map/ppermute | solution.py:69
  231.3 12.4 %collective-permute-start.58 = (bf16[16,3072]{1,0:T(8,128)(2,1)S(1)}, bf16[16,3072]{1,0:T(8,128)(2,1)S(1)}, u32[]{:S(2)}, u32[]{:S(2)}) collective-permute-start(bf16[16,3072]{1,0:T(8,128)(2,1)S(1)} %get-tuple-element.25), channel_id=1, source_target_pairs={{0,8},{1,9},{8,16},{9,17},{16,24},{17,25},{24,26},{25,27},{26,18},... | collective-permute-start | bytes 294920 | tf_op jit(solution)/shard_map/ppermute | solution.py:69
  233.7 7.8 %collective-permute-start.24 = (bf16[16,6144]{1,0:T(8,128)(2,1)S(1)}, bf16[16,6144]{1,0:T(8,128)(2,1)S(1)}, u32[]{:S(2)}, u32[]{:S(2)}) collective-permute-start(bf16[16,6144]{1,0:T(8,128)(2,1)S(1)} %fusion.31), channel_id=1, source_target_pairs={{8,0},{9,1},{16,8},{17,9},{24,16},{25,17},{26,24},{27,25},{18,26},... | collective-permute-start | bytes 589832 | tf_op jit(solution)/shard_map/ppermute | solution.py:72
  235.8 9.9 %collective-permute-start.55 = (bf16[16,6144]{1,0:T(8,128)(2,1)S(1)}, bf16[16,6144]{1,0:T(8,128)(2,1)S(1)}, u32[]{:S(2)}, u32[]{:S(2)}) collective-permute-start(bf16[16,6144]{1,0:T(8,128)(2,1)S(1)} %fusion.23), channel_id=1, source_target_pairs={{8,0},{9,1},{16,8},{17,9},{24,16},{25,17},{26,24},{27,25},{18,26},... | collective-permute-start | bytes 589832 | tf_op jit(solution)/shard_map/ppermute | solution.py:72
  241.6 8.4 %collective-permute-start.25 = (bf16[16,6144]{1,0:T(8,128)(2,1)S(1)}, bf16[16,6144]{1,0:T(8,128)(2,1)S(1)}, u32[]{:S(2)}, u32[]{:S(2)}) collective-permute-start(bf16[16,6144]{1,0:T(8,128)(2,1)S(1)} %get-tuple-element.14), channel_id=1, source_target_pairs={{8,0},{9,1},{16,8},{17,9},{24,16},{25,17},{26,24},{27,25},{18,26},... | collective-permute-start | bytes 589832 | tf_op jit(solution)/shard_map/ppermute | solution.py:72
  241.9 8.0 %collective-permute-start.28 = (bf16[16,6144]{1,0:T(8,128)(2,1)S(1)}, bf16[16,6144]{1,0:T(8,128)(2,1)S(1)}, u32[]{:S(2)}, u32[]{:S(2)}) collective-permute-start(bf16[16,6144]{1,0:T(8,128)(2,1)S(1)} %get-tuple-element.15), channel_id=1, source_target_pairs={{0,8},{1,9},{8,16},{9,17},{16,24},{17,25},{24,26},{25,27},{26,18},... | collective-permute-start | bytes 589832 | tf_op jit(solution)/shard_map/ppermute | solution.py:69
  245.8 8.4 %collective-permute-start.56 = (bf16[16,6144]{1,0:T(8,128)(2,1)S(1)}, bf16[16,6144]{1,0:T(8,128)(2,1)S(1)}, u32[]{:S(2)}, u32[]{:S(2)}) collective-permute-start(bf16[16,6144]{1,0:T(8,128)(2,1)S(1)} %get-tuple-element.18), channel_id=1, source_target_pairs={{8,0},{9,1},{16,8},{17,9},{24,16},{25,17},{26,24},{27,25},{18,26},... | collective-permute-start | bytes 589832 | tf_op jit(solution)/shard_map/ppermute | solution.py:72
  246.1 8.0 %collective-permute-start.59 = (bf16[16,6144]{1,0:T(8,128)(2,1)S(1)}, bf16[16,6144]{1,0:T(8,128)(2,1)S(1)}, u32[]{:S(2)}, u32[]{:S(2)}) collective-permute-start(bf16[16,6144]{1,0:T(8,128)(2,1)S(1)} %get-tuple-element.19), channel_id=1, source_target_pairs={{0,8},{1,9},{8,16},{9,17},{16,24},{17,25},{24,26},{25,27},{26,18},... | collective-permute-start | bytes 589832 | tf_op jit(solution)/shard_map/ppermute | solution.py:69
  250.0 14.2 %collective-permute-start.26 = (bf16[16,6144]{1,0:T(8,128)(2,1)S(1)}, bf16[16,6144]{1,0:T(8,128)(2,1)S(1)}, u32[]{:S(2)}, u32[]{:S(2)}) collective-permute-start(bf16[16,6144]{1,0:T(8,128)(2,1)S(1)} %get-tuple-element.12), channel_id=1, source_target_pairs={{8,0},{9,1},{16,8},{17,9},{24,16},{25,17},{26,24},{27,25},{18,26},... | collective-permute-start | bytes 589832 | tf_op jit(solution)/shard_map/ppermute | solution.py:72
  250.3 7.0 %collective-permute-start.29 = (bf16[16,6144]{1,0:T(8,128)(2,1)S(1)}, bf16[16,6144]{1,0:T(8,128)(2,1)S(1)}, u32[]{:S(2)}, u32[]{:S(2)}) collective-permute-start(bf16[16,6144]{1,0:T(8,128)(2,1)S(1)} %get-tuple-element.13), channel_id=1, source_target_pairs={{0,8},{1,9},{8,16},{9,17},{16,24},{17,25},{24,26},{25,27},{26,18},... | collective-permute-start | bytes 589832 | tf_op jit(solution)/shard_map/ppermute | solution.py:69
  254.2 12.4 %collective-permute-start.57 = (bf16[16,6144]{1,0:T(8,128)(2,1)S(1)}, bf16[16,6144]{1,0:T(8,128)(2,1)S(1)}, u32[]{:S(2)}, u32[]{:S(2)}) collective-permute-start(bf16[16,6144]{1,0:T(8,128)(2,1)S(1)} %get-tuple-element.16), channel_id=1, source_target_pairs={{8,0},{9,1},{16,8},{17,9},{24,16},{25,17},{26,24},{27,25},{18,26},... | collective-permute-start | bytes 589832 | tf_op jit(solution)/shard_map/ppermute | solution.py:72
  254.6 7.8 %collective-permute-start.60 = (bf16[16,6144]{1,0:T(8,128)(2,1)S(1)}, bf16[16,6144]{1,0:T(8,128)(2,1)S(1)}, u32[]{:S(2)}, u32[]{:S(2)}) collective-permute-start(bf16[16,6144]{1,0:T(8,128)(2,1)S(1)} %get-tuple-element.17), channel_id=1, source_target_pairs={{0,8},{1,9},{8,16},{9,17},{16,24},{17,25},{24,26},{25,27},{26,18},... | collective-permute-start | bytes 589832 | tf_op jit(solution)/shard_map/ppermute | solution.py:69
  257.3 9.2 %collective-permute-start.30 = (bf16[16,6144]{1,0:T(8,128)(2,1)S(1)}, bf16[16,6144]{1,0:T(8,128)(2,1)S(1)}, u32[]{:S(2)}, u32[]{:S(2)}) collective-permute-start(bf16[16,6144]{1,0:T(8,128)(2,1)S(1)} %fusion.30), channel_id=1, source_target_pairs={{0,8},{1,9},{8,16},{9,17},{16,24},{17,25},{24,26},{25,27},{26,18},... | collective-permute-start | bytes 589832 | tf_op jit(solution)/shard_map/ppermute | solution.py:69
  262.4 6.2 %collective-permute-start.61 = (bf16[16,6144]{1,0:T(8,128)(2,1)S(1)}, bf16[16,6144]{1,0:T(8,128)(2,1)S(1)}, u32[]{:S(2)}, u32[]{:S(2)}) collective-permute-start(bf16[16,6144]{1,0:T(8,128)(2,1)S(1)} %fusion.22), channel_id=1, source_target_pairs={{0,8},{1,9},{8,16},{9,17},{16,24},{17,25},{24,26},{25,27},{26,18},... | collective-permute-start | bytes 589832 | tf_op jit(solution)/shard_map/ppermute | solution.py:69
  (23 other events, 136.6 us)

commit v2 on v0

v2 whole, which is shorter than its diff:
```python
import jax
import jax.numpy as jnp
from jax import lax
from jax.experimental import pallas as pl
from jax.experimental.pallas import tpu as pltpu
from jax.sharding import PartitionSpec as P

tanh_scale = 0.7978845608028654
cubic_coef = 0.044715
ROWS = ("pipe", "tensor")
bf16, f32 = jnp.bfloat16, jnp.float32


def gelu_pair(value):
    inner = tanh_scale * (value + cubic_coef * value * value * value)
    tangent = jnp.tanh(inner)
    result = 0.5 * value * (1.0 + tangent)
    slope = 0.5 * (1.0 + tangent) + 0.5 * value * (1.0 - tangent * tangent) * tanh_scale * (
        1.0 + 3.0 * cubic_coef * value * value
    )
    return (result, slope)


def times_transpose(left, right):
    return lax.dot_general(
        left, right, (((1,), (1,)), ((), ())), preferred_element_type=f32
    )


def over_rows(left, right):
    return lax.dot_general(
        left, right, (((0,), (0,)), ((), ())), preferred_element_type=f32
    )


def shards_plain(tokens, out_grad, w_in, b_in, w_out):
    tok_all, grad_all = (
        lax.all_gather(tokens, ROWS, axis=0, tiled=True),
        lax.all_gather(out_grad, ROWS, axis=0, tiled=True),
    )
    proj_part = jnp.dot(tok_all, w_in, preferred_element_type=f32)
    signal_part = times_transpose(grad_all, w_out)
    projected = lax.psum(proj_part, "dp") + b_in
    active_f, derivative = gelu_pair(projected)
    activated = active_f.astype(bf16)
    back_signal = lax.psum(signal_part, "dp")
    proj_grad = (back_signal * derivative).astype(bf16)
    w_out_grad = over_rows(activated, grad_all).astype(bf16)
    w_in_grad = over_rows(tok_all, proj_grad).astype(bf16)
    b_in_grad = jnp.sum(proj_grad.astype(f32), axis=0)
    in_total = lax.psum_scatter(
        times_transpose(proj_grad, w_in), ROWS, scatter_dimension=0, tiled=True
    )
    return (in_total.astype(bf16), w_in_grad, w_out_grad, b_in_grad)


class Links:
    def __init__(self, pipe, tensor):
        lines = tensor // 2
        chips = []
        for y in range(lines):
            order = range(pipe) if y % 2 == 0 else range(pipe - 1, -1, -1)
            chips += [z * tensor + y * 2 for z in order]
        self.far = len(chips) // 2
        pairs = list(zip(chips, chips[1:] + chips[:1]))
        self.ring = [(a, b) for a, b in pairs] + [(b + 1, a + 1) for a, b in pairs]
        self.core = [(t, t ^ 1) for t in range(tensor)]

    def onward(self, x):
        return lax.ppermute(x, ROWS, self.ring)

    def sibling(self, x):
        return lax.ppermute(x, "tensor", self.core)

    def across(self, x):
        return lax.ppermute(x, "dp", [(0, 1), (1, 0)])


def over_rows_tiles(lefts, rights, into, first, count, tile):
    m, n = lefts[0].shape[1], rights[0].shape[1]
    parts = len(lefts)

    def kernel(*refs):
        ls, rs, o_ref = refs[:parts], refs[parts : 2 * parts], refs[-1]
        o_ref[...] = sum(over_rows(l[...], r[...]) for l, r in zip(ls, rs)).astype(bf16)

    depth = [l.shape[0] for l in lefts]
    in_specs = [pl.BlockSpec((k, tile), lambda i: (0, first + i)) for k in depth]
    in_specs += [pl.BlockSpec((k, n), lambda i: (0, 0)) for k in depth]
    args = list(lefts) + list(rights)
    alias = {}
    if into is not None:
        alias = {len(args): 0}
        args.append(into)
        in_specs.append(pl.BlockSpec(memory_space=pl.ANY))
    return pl.pallas_call(
        kernel,
        grid=(count,),
        in_specs=in_specs,
        out_specs=pl.BlockSpec((tile, n), lambda i: (first + i, 0)),
        out_shape=jax.ShapeDtypeStruct((m, n), bf16),
        input_output_aliases=alias,
        compiler_params=pltpu.CompilerParams(vmem_limit_bytes=40 << 20),
        cost_estimate=pl.CostEstimate(
            flops=2 * sum(depth) * count * tile * n,
            bytes_accessed=2 * (sum(depth) * (count * tile + n) + count * tile * n),
            transcendentals=0,
        ),
    )(*args)


def after(x, *others):
    return lax.optimization_barrier((x, others))[0]


def shards_ring(links, tokens, out_grad, w_in, b_in, w_out):
    far = links.far
    step = tokens.shape[0] // 2
    cat = jnp.concatenate

    def together(send, blocks):
        sizes = [b.shape[0] for b in blocks]
        got = send(cat(blocks))
        return [got[sum(sizes[:i]) : sum(sizes[: i + 1])] for i in range(len(sizes))]

    def apart(send, blocks):
        return [send(b) for b in blocks]

    def gather(chips, move, waits):
        got = {0: chips}
        for d in range(1, far + 1):
            out = got[d - 1]
            if d == far:
                out = [b[:step] for b in out]
            wait = waits(d, got)
            if wait is not None:
                out = after(out, wait)
            got[d] = move(links.onward, out)
        rows = []
        for i in range(len(chips)):
            early = cat([got[d][i] for d in range(1, far - 1)])
            late = cat([got[d][i] for d in range(far - 1, far + 1)])
            mine, theirs = chips[i][:step], chips[i][step:]
            others = [links.sibling(early), links.sibling(late)]
            rows.append(cat([mine, *others, theirs, early, late]))
        return rows, got

    def other_half(own):
        return links.across(own.astype(bf16))

    def project(rows):
        return jnp.dot(rows, w_in, preferred_element_type=f32)

    def signals(rows):
        return times_transpose(rows, w_out)

    def activate(p, p_other):
        return gelu_pair(p + p_other.astype(f32) + b_in)

    def backprop(s, s_other, derivative):
        pg = ((s + s_other.astype(f32)) * derivative).astype(bf16)
        return pg, jnp.sum(pg.astype(f32), axis=0)

    tok_sib, grad_sib = links.sibling(tokens), links.sibling(out_grad)
    chunk = lambda x, y, k: cat([x[k * step : (k + 1) * step], y[k * step : (k + 1) * step]])
    chips = [[chunk(tokens, tok_sib, k), chunk(out_grad, grad_sib, k)] for k in range(2)]

    (tok1, grad1), got1 = gather(chips[0], apart, lambda *_: None)
    done = {}

    def waits(d, got):
        if d == 1:
            return got1[far - 1]
        if d == 2:
            done["p"] = project(tok1)
            return done["p"]
        if d == 3:
            done["s"] = signals(after(grad1, got[1], done["p"]))
            done["px"] = other_half(after(done["p"], got[1]))
            return done["s"]
        return done["px"]

    (tok2, grad2), got2 = gather(chips[1], together, waits)
    s1x = after(other_half(done["s"]), got2[far])
    p2 = project(tok2)
    act1, slope1 = activate(done["p"], done["px"])
    pg1, sum1 = backprop(done["s"], s1x, slope1)
    act1, pg1, sum1 = lax.optimization_barrier((act1.astype(bf16), pg1, sum1))
    s2 = signals(after(grad2, pg1, p2))
    parts = lambda x: [x[: 8 * step], x[8 * step :]]
    p2x, s2x = [[other_half(h) for h in parts(x)] for x in (p2, s2)]

    def own_sums(pg, beside=None):
        partial = times_transpose(pg, w_in)
        if beside is not None:
            partial, beside = lax.optimization_barrier((partial, beside))
        theirs = links.sibling(partial.astype(bf16)[8 * step :])
        return partial, partial[: 8 * step] + theirs.astype(f32), beside

    def scatter(own, beside):
        running = own[(2 * far - 1) * step :].astype(bf16)
        for n, d in enumerate(range(far - 1, -1, -1)):
            work = beside(n, running)
            running = links.onward(running)
            if d == 0:
                ours = own[:step] + running[step:].astype(f32)
                return (ours + links.sibling(running[:step]).astype(f32)).astype(bf16), work
            here = own[(2 * d - 1) * step : (2 * d + 1) * step]
            if n == 0:
                first = here[:step] + running.astype(f32)
                running = cat([first.astype(bf16), here[step:].astype(bf16)])
            else:
                running = (here + running.astype(f32)).astype(bf16)
            if work is not None:
                running = after(running, work)

    part1, own1, p2x[1] = own_sums(after(pg1, s2, p2x[0]), p2x[1])
    act2, slope2 = activate(p2, cat(p2x))
    act2, slope2 = lax.optimization_barrier((act2.astype(bf16), slope2))
    made = {}

    def beside1(n, ready):
        if n == 3:
            pg2, made["sum2"] = backprop(s2, cat(after(s2x, ready, made["out"])), slope2)
            made["pg2"] = pg2
            made["part2"], made["own2"], _ = own_sums(pg2)
            return made["part2"]
        wait = made.get("part2", made.get("out", part1))
        a1, a2 = after((act1, act2), ready, wait)
        index = n
        made["out"] = over_rows_tiles(
            [a1, a2], [grad1, grad2], made.get("out"), 2 * index, 2, act1.shape[1] // 6
        )
        pairing = {0: 0, 3 - 1: 1}.get(n)
        if pairing is not None:
            made["out"], s2x[pairing] = lax.optimization_barrier((made["out"], s2x[pairing]))
        return made["out"]

    in1, _ = scatter(own1, beside1)

    def beside2(n, ready):
        if n == 3:
            return None
        t1, t2 = after((tok1, tok2), ready, made.get("in", made["out"]))
        made["in"] = over_rows_tiles(
            [t1, t2], [pg1, made["pg2"]], made.get("in"), 2 * n, 2, tokens.shape[1] // 6
        )
        return made["in"]

    in2, _ = scatter(made["own2"], beside2)
    return (cat([in1, in2]), made["in"], made["out"], sum1 + made["sum2"])


def solution(mesh):
    in_specs = (
        P(("pipe", "tensor"), "dp"),
        P(("pipe", "tensor"), "dp"),
        P("dp", ("pipe", "tensor")),
        P(("pipe", "tensor")),
        P(("pipe", "tensor"), "dp"),
    )
    out_specs = (
        P(("pipe", "tensor"), "dp"),
        P("dp", ("pipe", "tensor")),
        P(("pipe", "tensor"), "dp"),
        P(("pipe", "tensor")),
    )
    pipe, dp, tensor = (mesh.shape[a] for a in ("pipe", "dp", "tensor"))
    if dp == 2 and tensor == 4:
        links = Links(pipe, tensor)
        body = lambda *args: shards_ring(links, *args)
    else:
        body = shards_plain
    return jax.shard_map(body, mesh=mesh, in_specs=in_specs, out_specs=out_specs, check_vma=False)
```

time: 472 us -> 225 us (0.48)
  waiting for transfers between devices: 343 us -> 57.2 us
  starting transfers between devices: 0.34 us -> 42.9 us
  Pallas kernels: 0 us -> 32.8 us
  matrix products: 82.7 us -> 64.9 us
  local copies, waits for them, and re-layouts: 25.3 us -> 11.5 us
  between operations: 13.8 us -> 1.44 us
  other arithmetic: 6.64 us -> 13.6 us
    psum x1 -> x0, waiting for transfers between devices: 152 us -> none  [shards(): back_signal = lax.psum(signal_part, 'dp')]
    all_gather x2 -> x0, waiting for transfers between devices: 112 us -> none  [the longest x1 66.2 us: shards(): lax.all_gather(out_grad, ('pipe', 'tensor'), axis=0, tiled=True)]
    reduce_scatter x1 -> x0, waiting for transfers between devices: 77 us -> none  [shards(): lax.psum_scatter(times_transpose(proj_grad, w_in), ('pipe', 'tensor'), sc...]
    ppermute x0 -> x40, waiting for transfers between devices: none -> 57.2 us  [the longest x20 42.3 us: onward(): return lax.ppermute(x, ROWS, self.ring)]
    ppermute x0 -> x40, starting transfers between devices: none -> 42.9 us  [the longest x20 33.4 us: onward(): return lax.ppermute(x, ROWS, self.ring)]
    pallas_call x0 -> x6, Pallas kernels: none -> 32.8 us  [over_rows_tiles(): pl.pallas_call(kernel, grid=(count,), in_specs=in_specs, out_specs=pl.Blo...]
    dot_general x3 -> x2, matrix products: 49.5 us -> 20.4 us  [project(): return jnp.dot(rows, w_in, preferred_element_type=f32)]
    unnamed x5 -> x57, local copies, waits for them, and re-layouts: 25.3 us -> 5.02 us
  transfers between devices with their start and end apart: 4 -> 40, of which waited for: 4 -> 20; matrix products, arithmetic and copies ran while one was open for 16% -> 24% of each run, Pallas kernels for 0% -> 15%
where the time goes in v2:
time: 225 us; the launch traced here: 224 us
  matrix products  64.9 us (29%)
  waiting for transfers between devices  57.2 us (25%)
  starting transfers between devices  42.9 us (19%)
  Pallas kernels  32.8 us (15%)
  other arithmetic  13.6 us (6%)
  local copies, waits for them, and re-layouts  11.5 us (5%)
    dot_general x4, matrix products, times_transpose(): lax.dot_general(left, right, (((1,), (1,)), ((), ())), preferred_element_...  44.6 us
    ppermute x20, waiting for transfers between devices, onward(): return lax.ppermute(x, ROWS, self.ring)  42.3 us
    ppermute x20, starting transfers between devices, onward(): return lax.ppermute(x, ROWS, self.ring)  33.4 us
    pallas_call x6, Pallas kernels, over_rows_tiles(): pl.pallas_call(kernel, grid=(count,), in_specs=in_specs, out_specs=pl.Blo...  32.8 us
    dot_general x2, matrix products, project(): return jnp.dot(rows, w_in, preferred_element_type=f32)  20.4 us
    ppermute x6, waiting for transfers between devices, across(): return lax.ppermute(x, 'dp', [(0, 1), (1, 0)])  9.46 us
    ppermute x6, starting transfers between devices, across(): return lax.ppermute(x, 'dp', [(0, 1), (1, 0)])  7.03 us
    ppermute x14, waiting for transfers between devices, sibling(): return lax.ppermute(x, 'tensor', self.core)  5.47 us
  transfers between devices with their start and end apart: 40, of which 20 were waited for; matrix products, arithmetic and copies ran while one was open for 24% of the time, Pallas kernels for 15%

profile of v2, /device:TPU:0, one launch (start us, length us, event | category | flops | bytes accessed | tf_op | source)
XLA Modules:
  0.0 224.4 jit_solution(15010039007960451177)
XLA Ops:
  3.5 3.1 %collective-permute-start.1 = (bf16[32,6144]{1,0:T(8,128)(2,1)S(1)}, bf16[32,6144]{1,0:T(8,128)(2,1)S(1)}, u32[]{:S(2)}, u32[]{:S(2)}) collective-permute-start(bf16[32,6144]{1,0:T(8,128)(2,1)S(1)} %pad_maximum_fusion.12), channel_id=1, source_target_pairs={{0,8},{8,16},{16,24},{24,26},{26,18},{18,10},{10,2},{2,0},{9,1},{1... | collective-permute-start | bytes 1179656 | tf_op jit(solution)/shard_map/ppermute | solution.py:70
  6.6 1.6 collective-permute-start.8
  8.2 4.0 %collective-permute-done.1 = bf16[32,6144]{1,0:T(8,128)(2,1)S(1)} collective-permute-done((bf16[32,6144]{1,0:T(8,128)(2,1)S(1)}, bf16[32,6144]{1,0:T(8,128)(2,1)S(1)}, u32[]{:S(2)}, u32[]{:S(2)}) %collective-permute-start.1) | collective-permute-done | bytes 393248 | tf_op jit(solution)/shard_map/ppermute | solution.py:70
  12.2 2.1 collective-permute-start.2
  14.3 2.1 collective-permute-done.8
  16.4 2.1 collective-permute-start.9
  18.5 2.1 collective-permute-done.2
  20.7 2.1 collective-permute-start.4
  22.9 2.0 collective-permute-done.9
  24.9 2.1 collective-permute-start.10
  26.9 2.1 collective-permute-done.4
  29.1 2.1 collective-permute-start.5
  31.4 1.9 collective-permute-done.10
  33.3 2.1 collective-permute-start.14
  35.6 3.5 %collective-permute-done.14 = bf16[16,6144]{1,0:T(8,128)(2,1)S(1)} collective-permute-done((bf16[16,6144]{1,0:T(8,128)(2,1)S(1)}, bf16[16,6144]{1,0:T(8,128)(2,1)S(1)}, u32[]{:S(2)}, u32[]{:S(2)}) %collective-permute-start.14) | collective-permute-done | bytes 196640 | tf_op jit(solution)/shard_map/ppermute | solution.py:70
  39.4 1.7 collective-permute-done.15
  41.3 2.1 collective-permute-start.11
  43.6 10.2 %fusion.37 = f32[256,1536]{1,0:T(8,128)S(1)} fusion(bf16[256,6144]{1,0:T(8,128)(2,1)S(1)} %constant_dynamic-update-slice_fusion.refs_0_, bf16[6144,1536]{1,0:T(8,128)(2,1)} %param.7), kind=kOutput, calls=%fused_computation.111 | convolution fusion | flops 4831838208 | bytes 23592960 | tf_op jit(solution)/shard_map/dot_general | solution.py:152
  56.8 1.6 collective-permute-start.17
  59.8 10.5 %fusion.34 = (bf16[256,1536]{1,0:T(8,128)(2,1)}, f32[256,1536]{1,0:T(8,128)}) fusion(bf16[256,6144]{1,0:T(8,128)(2,1)S(1)} %constant_dynamic-update-slice_fusion.8.refs_2_, bf16[1536,6144]{1,0:T(8,128)(2,1)} %param.9), kind=kOutput, calls=%fused_computation.108 | convolution fusion | flops 4832231424 | bytes 24379392 | tf_op jit(solution)/shard_map/dot_general | solution.py:25
  71.0 1.6 collective-permute-start.18
  73.4 9.6 %collective-permute-done.18 = bf16[64,6144]{1,0:T(8,128)(2,1)S(1)} collective-permute-done((bf16[64,6144]{1,0:T(8,128)(2,1)S(1)}, bf16[64,6144]{1,0:T(8,128)(2,1)S(1)}, u32[]{:S(2)}, u32[]{:S(2)}) %collective-permute-start.18) | collective-permute-done | bytes 786464 | tf_op jit(solution)/shard_map/ppermute | solution.py:70
  83.1 1.8 collective-permute-start.19
  85.1 6.0 %collective-permute-done.19 = bf16[32,6144]{1,0:T(8,128)(2,1)S(1)} collective-permute-done((bf16[32,6144]{1,0:T(8,128)(2,1)S(1)}, bf16[32,6144]{1,0:T(8,128)(2,1)S(1)}, u32[]{:S(2)}, u32[]{:S(2)}) %collective-permute-start.19) | collective-permute-done | bytes 393248 | tf_op jit(solution)/shard_map/ppermute | solution.py:70
  91.9 2.5 %collective-permute-done.16 = bf16[256,1536]{1,0:T(8,128)(2,1)S(1)} collective-permute-done((bf16[256,1536]{1,0:T(8,128)(2,1)}, bf16[256,1536]{1,0:T(8,128)(2,1)S(1)}, u32[]{:S(2)}, u32[]{:S(2)}) %collective-permute-start.16) | collective-permute-done | bytes 786464 | tf_op jit(solution)/shard_map/ppermute | solution.py:76
  94.4 2.6 %convert_reduce_fusion.1 = (f32[1536]{0:T(1024)S(1)}, bf16[256,1536]{1,0:T(8,128)(2,1)S(1)}, bf16[256,1536]{1,0:T(8,128)(2,1)S(1)}) fusion(f32[1536]{0:T(1024)S(1)} %copy-done.16, f32[256,1536]{1,0:T(8,128)S(1)} %fusion.37, bf16[256,1536]{1,0:T(8,128)(2,1)} %collective-permute-done.12, f32[256,1536]{1,0:T(8,128)S(1)} %copy-done.10, ...), kind=kLoop, calls=%fused_computation.24 | loop fusion | flops 11008512 | bytes 6303744 | tf_op jit(solution)/shard_map/reduce_sum | solution.py:162
  98.5 10.2 %fusion.35 = (bf16[256,1536]{1,0:T(8,128)(2,1)S(1)}, f32[256,1536]{1,0:T(8,128)}) fusion(bf16[256,6144]{1,0:T(8,128)(2,1)S(1)} %get-tuple-element.89.refs_1_, bf16[6144,1536]{1,0:T(8,128)(2,1)} %param.7), kind=kOutput, calls=%fused_computation.109 | convolution fusion | flops 4832231424 | bytes 24379392 | tf_op jit(solution)/shard_map/dot_general | solution.py:152
  111.5 10.6 %fusion.36 = (bf16[256,1536]{1,0:T(8,128)(2,1)}, f32[256,1536]{1,0:T(8,128)}) fusion(bf16[256,6144]{1,0:T(8,128)(2,1)S(1)} %get-tuple-element.60.refs_3_, bf16[1536,6144]{1,0:T(8,128)(2,1)} %param.9), kind=kOutput, calls=%fused_computation.110 | convolution fusion | flops 4832231424 | bytes 24379392 | tf_op jit(solution)/shard_map/dot_general | solution.py:25
  122.1 5.7 %collective-permute-done.24 = bf16[128,1536]{1,0:T(8,128)(2,1)} collective-permute-done((bf16[128,1536]{1,0:T(8,128)(2,1)S(1)}, bf16[128,1536]{1,0:T(8,128)(2,1)}, u32[]{:S(2)}, u32[]{:S(2)}) %collective-permute-start.24) | collective-permute-done | bytes 393248 | tf_op jit(solution)/shard_map/ppermute | solution.py:76
  127.8 11.7 %fusion.38 = f32[256,6144]{1,0:T(8,128)} fusion(bf16[256,1536]{1,0:T(8,128)(2,1)S(1)} %get-tuple-element.61.refs_2_, bf16[6144,1536]{1,0:T(8,128)(2,1)} %param.7), kind=kOutput, calls=%fused_computation.112 | convolution fusion | flops 4831838208 | bytes 25952256 | tf_op jit(solution)/shard_map/dot_general | solution.py:25
  139.6 2.3 %slice.282 = bf16[128,6144]{1,0:T(8,128)(2,1)S(1)} slice(f32[256,6144]{1,0:T(8,128)} %fusion.38), slice={[128:256], [0:6144]} | slice | bytes 3145728 | tf_op jit(solution)/shard_map/slice | solution.py:197
  144.4 2.3 %fusion.11 = (f32[256,1536]{1,0:T(8,128)S(1)}, bf16[256,1536]{1,0:T(8,128)(2,1)S(1)}) fusion(f32[256,1536]{1,0:T(8,128)S(1)} %copy-done.12, f32[1536]{0:T(1024)S(1)} %copy-done.16, bf16[128,1536]{1,0:T(8,128)(2,1)} %copy-done.14, bf16[128,1536]{1,0:T(8,128)(2,1)} %collective-permute-done.24), kind=kLoop, calls=%fused_computation.19 | loop fusion | flops 9830400 | bytes 4724736 | tf_op jit(solution)/shard_map/add | solution.py:18
  148.0 5.4 %shard_map.84.refs_4_ = bf16[1536,6144]{1,0:T(8,128)(2,1)} custom-call(bf16[256,1536]{1,0:T(8,128)(2,1)S(1)} %get-tuple-element.73.refs_0_, bf16[256,1536]{1,0:T(8,128)(2,1)S(1)} %get-tuple-element.74.refs_1_, bf16[256,6144]{1,0:T(8,128)(2,1)S(1)} %constant_dynamic-update-slice_fusion.8.refs_2_, bf16[256,6144]{1,0:T(8,128)(2,1)S(1)} %get-tuple-element.60.refs_3_), custom_call_target="tpu_custom_call" | custom-call | flops 3221225472 | bytes 13107200 | tf_op jit(solution)/shard_map/pallas_call | solution.py:96
  156.8 5.4 %shard_map.85.refs_4_ = bf16[1536,6144]{1,0:T(8,128)(2,1)} custom-call(bf16[256,1536]{1,0:T(8,128)(2,1)S(1)} %get-tuple-element.73.refs_0_, bf16[256,1536]{1,0:T(8,128)(2,1)S(1)} %get-tuple-element.74.refs_1_, bf16[256,6144]{1,0:T(8,128)(2,1)S(1)} %constant_dynamic-update-slice_fusion.8.refs_2_, ...), custom_call_target="tpu_custom_call", output_to_operand_aliasing={{}: (4, {})} | custom-call | flops 3221225472 | bytes 13107200 | tf_op jit(solution)/shard_map/pallas_call | solution.py:96
  163.8 5.4 %shard_map.86 = bf16[1536,6144]{1,0:T(8,128)(2,1)} custom-call(bf16[256,1536]{1,0:T(8,128)(2,1)S(1)} %get-tuple-element.73.refs_0_, bf16[256,1536]{1,0:T(8,128)(2,1)S(1)} %get-tuple-element.74.refs_1_, bf16[256,6144]{1,0:T(8,128)(2,1)S(1)} %constant_dynamic-update-slice_fusion.8.refs_2_, ...), custom_call_target="tpu_custom_call", output_to_operand_aliasing={{}: (4, {})} | custom-call | flops 3221225472 | bytes 13107200 | tf_op jit(solution)/shard_map/pallas_call | solution.py:96
  169.2 2.0 collective-permute-done.30
  171.7 11.8 %fusion.39 = f32[256,6144]{1,0:T(8,128)} fusion(bf16[256,1536]{1,0:T(8,128)(2,1)S(1)} %get-tuple-element.93.refs_3_, bf16[6144,1536]{1,0:T(8,128)(2,1)} %param.7), kind=kOutput, calls=%fused_computation.113 | convolution fusion | flops 4831838208 | bytes 25952256 | tf_op jit(solution)/shard_map/dot_general | solution.py:25
  183.5 2.1 slice.281
  185.6 3.4 %collective-permute-done.34 = bf16[128,6144]{1,0:T(8,128)(2,1)S(1)} collective-permute-done((bf16[128,6144]{1,0:T(8,128)(2,1)S(1)}, bf16[128,6144]{1,0:T(8,128)(2,1)S(1)}, u32[]{:S(2)}, u32[]{:S(2)}) %collective-permute-start.34) | collective-permute-done | bytes 1572896 | tf_op jit(solution)/shard_map/ppermute | solution.py:73
  189.0 2.4 %fusion.22 = (bf16[128,6144]{1,0:T(8,128)(2,1)S(1)}, f32[128,6144]{1,0:T(8,128)S(1)}) fusion(bf16[128,6144]{1,0:T(8,128)(2,1)S(1)} %collective-permute-done.34, f32[256,6144]{1,0:T(8,128)} %fusion.39), kind=kLoop, calls=%fused_computation.97 | loop fusion | flops 2359296 | bytes 9437184 | tf_op jit(solution)/shard_map/convert.1
  191.9 5.5 %shard_map.87.refs_4_ = bf16[6144,1536]{1,0:T(8,128)(2,1)} custom-call(bf16[256,6144]{1,0:T(8,128)(2,1)S(1)} %copy-done.1, bf16[256,6144]{1,0:T(8,128)(2,1)S(1)} %get-tuple-element.89.refs_1_, bf16[256,1536]{1,0:T(8,128)(2,1)S(1)} %get-tuple-element.61.refs_2_, bf16[256,1536]{1,0:T(8,128)(2,1)S(1)} %get-tuple-element.93.refs_3_), custom_call_target="tpu_custom_call" | custom-call | flops 3221225472 | bytes 9961472 | tf_op jit(solution)/shard_map/pallas_call | solution.py:96
  197.5 1.8 collective-permute-start.36
  199.4 5.5 %shard_map.88.refs_4_ = bf16[6144,1536]{1,0:T(8,128)(2,1)} custom-call(bf16[256,6144]{1,0:T(8,128)(2,1)S(1)} %copy-done.1, bf16[256,6144]{1,0:T(8,128)(2,1)S(1)} %get-tuple-element.89.refs_1_, bf16[256,1536]{1,0:T(8,128)(2,1)S(1)} %get-tuple-element.61.refs_2_, bf16[256,1536]{1,0:T(8,128)(2,1)S(1)} %get-tuple-element.93.refs_3_, ...), custom_call_target="tpu_custom_call", output_to_operand_aliasing={{}: (4, {})} | custom-call | flops 3221225472 | bytes 9961472 | tf_op jit(solution)/shard_map/pallas_call | solution.py:96
  205.7 1.6 collective-permute-start.37
  208.4 5.5 %shard_map.89 = bf16[6144,1536]{1,0:T(8,128)(2,1)} custom-call(bf16[256,6144]{1,0:T(8,128)(2,1)S(1)} %copy-done.1, bf16[256,6144]{1,0:T(8,128)(2,1)S(1)} %get-tuple-element.89.refs_1_, bf16[256,1536]{1,0:T(8,128)(2,1)S(1)} %get-tuple-element.61.refs_2_, bf16[256,1536]{1,0:T(8,128)(2,1)S(1)} %get-tuple-element.93.refs_3_, ...), custom_call_target="tpu_custom_call", output_to_operand_aliasing={{}: (4, {})} | custom-call | flops 3221225472 | bytes 9961472 | tf_op jit(solution)/shard_map/pallas_call | solution.py:96
  214.0 2.2 collective-permute-start.38
  216.2 1.5 collective-permute-done.32
  218.5 3.5 %collective-permute-done.38 = bf16[32,6144]{1,0:T(8,128)(2,1)S(1)} collective-permute-done((bf16[32,6144]{1,0:T(8,128)(2,1)S(1)}, bf16[32,6144]{1,0:T(8,128)(2,1)S(1)}, u32[]{:S(2)}, u32[]{:S(2)}) %collective-permute-start.38) | collective-permute-done | bytes 393248 | tf_op jit(solution)/shard_map/ppermute | solution.py:70
  (155 shorter events, 29.9 us)
Async XLA Ops:
  0.6 2.8 %collective-permute-start = (bf16[32,6144]{1,0:T(8,128)(2,1)}, bf16[32,6144]{1,0:T(8,128)(2,1)S(1)}, u32[]{:S(2)}, u32[]{:S(2)}) collective-permute-start(bf16[32,6144]{1,0:T(8,128)(2,1)} %param.5), channel_id=1, source_target_pairs={{0,1},{1,0},{2,3},{3,2},{4,5},{5,4},{6,7},{7,6},{8,9},{9,8},{10,11... | collective-permute-start | bytes 1179656 | tf_op jit(solution)/shard_map/ppermute | solution.py:73
  1.1 5.4 %collective-permute-start.7 = (bf16[32,6144]{1,0:T(8,128)(2,1)}, bf16[32,6144]{1,0:T(8,128)(2,1)S(1)}, u32[]{:S(2)}, u32[]{:S(2)}) collective-permute-start(bf16[32,6144]{1,0:T(8,128)(2,1)} %param.6), channel_id=1, source_target_pairs={{0,1},{1,0},{2,3},{3,2},{4,5},{5,4},{6,7},{7,6},{8,9},{9,8},{10,11... | collective-permute-start | bytes 1179656 | tf_op jit(solution)/shard_map/ppermute | solution.py:73
  3.4 36.0 %copy-start.8 = (bf16[32,6144]{1,0:T(8,128)(2,1)}, bf16[32,6144]{1,0:T(8,128)(2,1)S(1)}, u32[]{:S(2)}) copy-start(bf16[32,6144]{1,0:T(8,128)(2,1)S(1)} %collective-permute-done) | copy-start | bytes 1179652
  3.5 8.8 %collective-permute-start.1 = (bf16[32,6144]{1,0:T(8,128)(2,1)S(1)}, bf16[32,6144]{1,0:T(8,128)(2,1)S(1)}, u32[]{:S(2)}, u32[]{:S(2)}) collective-permute-start(bf16[32,6144]{1,0:T(8,128)(2,1)S(1)} %pad_maximum_fusion.12), channel_id=1, source_target_pairs={{0,8},{8,16},{16,24},{24,26},{26,18},{18,10},{10,2},{2,0},{9,1},{1... | collective-permute-start | bytes 1179656 | tf_op jit(solution)/shard_map/ppermute | solution.py:70
  6.6 9.9 %collective-permute-start.8 = (bf16[32,6144]{1,0:T(8,128)(2,1)S(1)}, bf16[32,6144]{1,0:T(8,128)(2,1)S(1)}, u32[]{:S(2)}, u32[]{:S(2)}) collective-permute-start(bf16[32,6144]{1,0:T(8,128)(2,1)S(1)} %pad_maximum_fusion.15), channel_id=1, source_target_pairs={{0,8},{8,16},{16,24},{24,26},{26,18},{18,10},{10,2},{2,0},{9,1},{1... | collective-permute-start | bytes 1179656 | tf_op jit(solution)/shard_map/ppermute | solution.py:70
  12.2 8.4 %collective-permute-start.2 = (bf16[32,6144]{1,0:T(8,128)(2,1)S(1)}, bf16[32,6144]{1,0:T(8,128)(2,1)S(1)}, u32[]{:S(2)}, u32[]{:S(2)}) collective-permute-start(bf16[32,6144]{1,0:T(8,128)(2,1)S(1)} %collective-permute-done.1), channel_id=1, source_target_pairs={{0,8},{8,16},{16,24},{24,26},{26,18},{18,10},{10,2},{2,0},{9,1},{1... | collective-permute-start | bytes 1179656 | tf_op jit(solution)/shard_map/ppermute | solution.py:70
  16.4 8.4 %collective-permute-start.9 = (bf16[32,6144]{1,0:T(8,128)(2,1)S(1)}, bf16[32,6144]{1,0:T(8,128)(2,1)S(1)}, u32[]{:S(2)}, u32[]{:S(2)}) collective-permute-start(bf16[32,6144]{1,0:T(8,128)(2,1)S(1)} %collective-permute-done.8), channel_id=1, source_target_pairs={{0,8},{8,16},{16,24},{24,26},{26,18},{18,10},{10,2},{2,0},{9,1},{1... | collective-permute-start | bytes 1179656 | tf_op jit(solution)/shard_map/ppermute | solution.py:70
  20.7 8.4 %collective-permute-start.4 = (bf16[32,6144]{1,0:T(8,128)(2,1)S(1)}, bf16[32,6144]{1,0:T(8,128)(2,1)S(1)}, u32[]{:S(2)}, u32[]{:S(2)}) collective-permute-start(bf16[32,6144]{1,0:T(8,128)(2,1)S(1)} %collective-permute-done.2), channel_id=1, source_target_pairs={{0,8},{8,16},{16,24},{24,26},{26,18},{18,10},{10,2},{2,0},{9,1},{1... | collective-permute-start | bytes 1179656 | tf_op jit(solution)/shard_map/ppermute | solution.py:70
  22.8 16.4 %collective-permute-start.3 = (bf16[64,6144]{1,0:T(8,128)(2,1)S(1)}, bf16[64,6144]{1,0:T(8,128)(2,1)S(1)}, u32[]{:S(2)}, u32[]{:S(2)}) collective-permute-start(bf16[64,6144]{1,0:T(8,128)(2,1)S(1)} %pad_maximum_fusion), channel_id=1, source_target_pairs={{0,1},{1,0},{2,3},{3,2},{4,5},{5,4},{6,7},{7,6},{8,9},{9,8},{10,11... | collective-permute-start | bytes 2359304 | tf_op jit(solution)/shard_map/ppermute | solution.py:73
  24.9 8.4 %collective-permute-start.10 = (bf16[32,6144]{1,0:T(8,128)(2,1)S(1)}, bf16[32,6144]{1,0:T(8,128)(2,1)S(1)}, u32[]{:S(2)}, u32[]{:S(2)}) collective-permute-start(bf16[32,6144]{1,0:T(8,128)(2,1)S(1)} %collective-permute-done.9), channel_id=1, source_target_pairs={{0,8},{8,16},{16,24},{24,26},{26,18},{18,10},{10,2},{2,0},{9,1},{1... | collective-permute-start | bytes 1179656 | tf_op jit(solution)/shard_map/ppermute | solution.py:70
  29.1 6.3 %collective-permute-start.5 = (bf16[16,6144]{1,0:T(8,128)(2,1)S(1)}, bf16[16,6144]{1,0:T(8,128)(2,1)S(1)}, u32[]{:S(2)}, u32[]{:S(2)}) collective-permute-start(bf16[16,6144]{1,0:T(8,128)(2,1)S(1)} %slice.193), channel_id=1, source_target_pairs={{0,8},{8,16},{16,24},{24,26},{26,18},{18,10},{10,2},{2,0},{9,1},{1... | collective-permute-start | bytes 589832 | tf_op jit(solution)/shard_map/ppermute | solution.py:70
  31.3 7.9 %collective-permute-start.13 = (bf16[64,6144]{1,0:T(8,128)(2,1)S(1)}, bf16[64,6144]{1,0:T(8,128)(2,1)S(1)}, u32[]{:S(2)}, u32[]{:S(2)}) collective-permute-start(bf16[64,6144]{1,0:T(8,128)(2,1)S(1)} %pad_maximum_fusion.2), channel_id=1, source_target_pairs={{0,1},{1,0},{2,3},{3,2},{4,5},{5,4},{6,7},{7,6},{8,9},{9,8},{10,11... | collective-permute-start | bytes 2359304 | tf_op jit(solution)/shard_map/ppermute | solution.py:73
  33.3 5.7 %collective-permute-start.14 = (bf16[16,6144]{1,0:T(8,128)(2,1)S(1)}, bf16[16,6144]{1,0:T(8,128)(2,1)S(1)}, u32[]{:S(2)}, u32[]{:S(2)}) collective-permute-start(bf16[16,6144]{1,0:T(8,128)(2,1)S(1)} %slice.199), channel_id=1, source_target_pairs={{0,8},{8,16},{16,24},{24,26},{26,18},{18,10},{10,2},{2,0},{9,1},{1... | collective-permute-start | bytes 589832 | tf_op jit(solution)/shard_map/ppermute | solution.py:70
  35.5 3.8 %collective-permute-start.6 = (bf16[48,6144]{1,0:T(8,128)(2,1)S(1)}, bf16[48,6144]{1,0:T(8,128)(2,1)S(1)}, u32[]{:S(2)}, u32[]{:S(2)}) collective-permute-start(bf16[48,6144]{1,0:T(8,128)(2,1)S(1)} %pad_maximum_fusion.8), channel_id=1, source_target_pairs={{0,1},{1,0},{2,3},{3,2},{4,5},{5,4},{6,7},{7,6},{8,9},{9,8},{10,11... | collective-permute-start | bytes 1769480 | tf_op jit(solution)/shard_map/ppermute | solution.py:73
  39.1 2.1 collective-permute-start.15
  41.3 12.6 %collective-permute-start.11 = (bf16[64,6144]{1,0:T(8,128)(2,1)S(1)}, bf16[64,6144]{1,0:T(8,128)(2,1)S(1)}, u32[]{:S(2)}, u32[]{:S(2)}) collective-permute-start(bf16[64,6144]{1,0:T(8,128)(2,1)S(1)} %pad_maximum_fusion.1), channel_id=1, source_target_pairs={{0,8},{8,16},{16,24},{24,26},{26,18},{18,10},{10,2},{2,0},{9,1},{1... | collective-permute-start | bytes 2359304 | tf_op jit(solution)/shard_map/ppermute | solution.py:70
  43.6 10.2 %copy-start = (bf16[256,6144]{1,0:T(8,128)(2,1)}, bf16[256,6144]{1,0:T(8,128)(2,1)S(1)}, u32[]{:S(2)}) copy-start(bf16[256,6144]{1,0:T(8,128)(2,1)S(1)} %constant_dynamic-update-slice_fusion.refs_0_) | copy-start | bytes 9437188
  56.8 14.1 %collective-permute-start.17 = (bf16[64,6144]{1,0:T(8,128)(2,1)}, bf16[64,6144]{1,0:T(8,128)(2,1)S(1)}, u32[]{:S(2)}, u32[]{:S(2)}) collective-permute-start(bf16[64,6144]{1,0:T(8,128)(2,1)} %pad_maximum_fusion.3), channel_id=1, source_target_pairs={{0,8},{8,16},{16,24},{24,26},{26,18},{18,10},{10,2},{2,0},{9,1},{1... | collective-permute-start | bytes 2359304 | tf_op jit(solution)/shard_map/ppermute | solution.py:70
  58.3 24.7 %collective-permute-start.12 = (bf16[256,1536]{1,0:T(8,128)(2,1)}, bf16[256,1536]{1,0:T(8,128)(2,1)}, u32[]{:S(2)}, u32[]{:S(2)}) collective-permute-start(bf16[256,1536]{1,0:T(8,128)(2,1)} %convert_element_type.110), channel_id=1, source_target_pairs={{0,4},{4,0},{1,5},{5,1},{2,6},{6,2},{3,7},{7,3},{8,12},{12,8},{9,1... | collective-permute-start | bytes 2359304 | tf_op jit(solution)/shard_map/ppermute | solution.py:76
  70.3 24.1 %collective-permute-start.16 = (bf16[256,1536]{1,0:T(8,128)(2,1)}, bf16[256,1536]{1,0:T(8,128)(2,1)S(1)}, u32[]{:S(2)}, u32[]{:S(2)}) collective-permute-start(bf16[256,1536]{1,0:T(8,128)(2,1)} %get-tuple-element.141), channel_id=1, source_target_pairs={{0,4},{4,0},{1,5},{5,1},{2,6},{6,2},{3,7},{7,3},{8,12},{12,8},{9,1... | collective-permute-start | bytes 2359304 | tf_op jit(solution)/shard_map/ppermute | solution.py:76
  71.0 12.0 %collective-permute-start.18 = (bf16[64,6144]{1,0:T(8,128)(2,1)S(1)}, bf16[64,6144]{1,0:T(8,128)(2,1)S(1)}, u32[]{:S(2)}, u32[]{:S(2)}) collective-permute-start(bf16[64,6144]{1,0:T(8,128)(2,1)S(1)} %pad_maximum_fusion.4), channel_id=1, source_target_pairs={{0,8},{8,16},{16,24},{24,26},{26,18},{18,10},{10,2},{2,0},{9,1},{1... | collective-permute-start | bytes 2359304 | tf_op jit(solution)/shard_map/ppermute | solution.py:70
  72.7 12.3 %collective-permute-start.22 = (bf16[64,6144]{1,0:T(8,128)(2,1)S(1)}, bf16[64,6144]{1,0:T(8,128)(2,1)S(1)}, u32[]{:S(2)}, u32[]{:S(2)}) collective-permute-start(bf16[64,6144]{1,0:T(8,128)(2,1)S(1)} %pad_maximum_fusion.6), channel_id=1, source_target_pairs={{0,1},{1,0},{2,3},{3,2},{4,5},{5,4},{6,7},{7,6},{8,9},{9,8},{10,11... | collective-permute-start | bytes 2359304 | tf_op jit(solution)/shard_map/ppermute | solution.py:73
  72.8 12.2 %collective-permute-start.20 = (bf16[64,6144]{1,0:T(8,128)(2,1)S(1)}, bf16[64,6144]{1,0:T(8,128)(2,1)S(1)}, u32[]{:S(2)}, u32[]{:S(2)}) collective-permute-start(bf16[64,6144]{1,0:T(8,128)(2,1)S(1)} %pad_maximum_fusion.5), channel_id=1, source_target_pairs={{0,1},{1,0},{2,3},{3,2},{4,5},{5,4},{6,7},{7,6},{8,9},{9,8},{10,11... | collective-permute-start | bytes 2359304 | tf_op jit(solution)/shard_map/ppermute | solution.py:73
  83.1 8.0 %collective-permute-start.19 = (bf16[32,6144]{1,0:T(8,128)(2,1)S(1)}, bf16[32,6144]{1,0:T(8,128)(2,1)S(1)}, u32[]{:S(2)}, u32[]{:S(2)}) collective-permute-start(bf16[32,6144]{1,0:T(8,128)(2,1)S(1)} %pad_maximum_fusion.16), channel_id=1, source_target_pairs={{0,8},{8,16},{16,24},{24,26},{26,18},{18,10},{10,2},{2,0},{9,1},{1... | collective-permute-start | bytes 1179656 | tf_op jit(solution)/shard_map/ppermute | solution.py:70
  85.0 9.4 %copy-start.10 = (f32[256,1536]{1,0:T(8,128)S(1)}, f32[256,1536]{1,0:T(8,128)}, u32[]{:S(2)}) copy-start(f32[256,1536]{1,0:T(8,128)} %get-tuple-element.142) | copy-start | bytes 4718596
  85.0 9.4 %copy-start.16 = (f32[1536]{0:T(1024)S(1)}, f32[1536]{0:T(1024)}, u32[]{:S(2)}) copy-start(f32[1536]{0:T(1024)} %param.8) | copy-start | bytes 18436
  91.2 5.8 %collective-permute-start.23 = (bf16[48,6144]{1,0:T(8,128)(2,1)S(1)}, bf16[48,6144]{1,0:T(8,128)(2,1)S(1)}, u32[]{:S(2)}, u32[]{:S(2)}) collective-permute-start(bf16[48,6144]{1,0:T(8,128)(2,1)S(1)} %pad_maximum_fusion.11), channel_id=1, source_target_pairs={{0,1},{1,0},{2,3},{3,2},{4,5},{5,4},{6,7},{7,6},{8,9},{9,8},{10,11... | collective-permute-start | bytes 1769480 | tf_op jit(solution)/shard_map/ppermute | solution.py:73
  91.3 5.8 %collective-permute-start.21 = (bf16[48,6144]{1,0:T(8,128)(2,1)S(1)}, bf16[48,6144]{1,0:T(8,128)(2,1)S(1)}, u32[]{:S(2)}, u32[]{:S(2)}) collective-permute-start(bf16[48,6144]{1,0:T(8,128)(2,1)S(1)} %pad_maximum_fusion.10), channel_id=1, source_target_pairs={{0,1},{1,0},{2,3},{3,2},{4,5},{5,4},{6,7},{7,6},{8,9},{9,8},{10,11... | collective-permute-start | bytes 1769480 | tf_op jit(solution)/shard_map/ppermute | solution.py:73
  109.5 30.1 %collective-permute-start.25 = (bf16[128,1536]{1,0:T(8,128)(2,1)}, bf16[128,1536]{1,0:T(8,128)(2,1)S(1)}, u32[]{:S(2)}, u32[]{:S(2)}) collective-permute-start(bf16[128,1536]{1,0:T(8,128)(2,1)} %get-tuple-element.109), channel_id=1, source_target_pairs={{0,4},{4,0},{1,5},{5,1},{2,6},{6,2},{3,7},{7,3},{8,12},{12,8},{9,1... | collective-permute-start | bytes 1179656 | tf_op jit(solution)/shard_map/ppermute | solution.py:76
  111.0 16.9 %collective-permute-start.24 = (bf16[128,1536]{1,0:T(8,128)(2,1)S(1)}, bf16[128,1536]{1,0:T(8,128)(2,1)}, u32[]{:S(2)}, u32[]{:S(2)}) collective-permute-start(bf16[128,1536]{1,0:T(8,128)(2,1)S(1)} %get-tuple-element.110), channel_id=1, source_target_pairs={{0,4},{4,0},{1,5},{5,1},{2,6},{6,2},{3,7},{7,3},{8,12},{12,8},{9,1... | collective-permute-start | bytes 1179656 | tf_op jit(solution)/shard_map/ppermute | solution.py:76
  141.9 4.8 %collective-permute-start.26 = (bf16[128,6144]{1,0:T(8,128)(2,1)S(1)}, bf16[128,6144]{1,0:T(8,128)(2,1)S(1)}, u32[]{:S(2)}, u32[]{:S(2)}) collective-permute-start(bf16[128,6144]{1,0:T(8,128)(2,1)S(1)} %slice.282), channel_id=1, source_target_pairs={{0,1},{1,0},{2,3},{3,2},{4,5},{5,4},{6,7},{7,6},{8,9},{9,8},{10,11... | collective-permute-start | bytes 4718600 | tf_op jit(solution)/shard_map/ppermute | solution.py:73
  142.9 11.7 %collective-permute-start.28 = (bf16[128,1536]{1,0:T(8,128)(2,1)}, bf16[128,1536]{1,0:T(8,128)(2,1)S(1)}, u32[]{:S(2)}, u32[]{:S(2)}) collective-permute-start(bf16[128,1536]{1,0:T(8,128)(2,1)} %get-tuple-element.108), channel_id=1, source_target_pairs={{0,4},{4,0},{1,5},{5,1},{2,6},{6,2},{3,7},{7,3},{8,12},{12,8},{9,1... | collective-permute-start | bytes 1179656 | tf_op jit(solution)/shard_map/ppermute | solution.py:76
  147.2 24.0 %copy-start.2 = (f32[128,6144]{1,0:T(8,128)}, f32[128,6144]{1,0:T(8,128)S(1)}, u32[]{:S(2)}) copy-start(f32[128,6144]{1,0:T(8,128)S(1)} %get-tuple-element.97) | copy-start | bytes 9437188
  147.2 8.1 %copy-start.15 = (bf16[128,1536]{1,0:T(8,128)(2,1)S(1)}, bf16[128,1536]{1,0:T(8,128)(2,1)}, u32[]{:S(2)}) copy-start(bf16[128,1536]{1,0:T(8,128)(2,1)} %get-tuple-element.107) | copy-start | bytes 1179652
  147.2 7.4 %collective-permute-start.27 = (bf16[16,6144]{1,0:T(8,128)(2,1)S(1)}, bf16[16,6144]{1,0:T(8,128)(2,1)S(1)}, u32[]{:S(2)}, u32[]{:S(2)}) collective-permute-start(bf16[16,6144]{1,0:T(8,128)(2,1)S(1)} %get-tuple-element.106), channel_id=1, source_target_pairs={{0,8},{8,16},{16,24},{24,26},{26,18},{18,10},{10,2},{2,0},{9,1},{1... | collective-permute-start | bytes 589832 | tf_op jit(solution)/shard_map/ppermute | solution.py:70
  154.7 8.6 %collective-permute-start.29 = (bf16[32,6144]{1,0:T(8,128)(2,1)S(1)}, bf16[32,6144]{1,0:T(8,128)(2,1)S(1)}, u32[]{:S(2)}, u32[]{:S(2)}) collective-permute-start(bf16[32,6144]{1,0:T(8,128)(2,1)S(1)} %pad_maximum_fusion.17), channel_id=1, source_target_pairs={{0,8},{8,16},{16,24},{24,26},{26,18},{18,10},{10,2},{2,0},{9,1},{1... | collective-permute-start | bytes 1179656 | tf_op jit(solution)/shard_map/ppermute | solution.py:70
  155.3 13.9 %collective-permute-start.31 = (bf16[128,1536]{1,0:T(8,128)(2,1)S(1)}, bf16[128,1536]{1,0:T(8,128)(2,1)S(1)}, u32[]{:S(2)}, u32[]{:S(2)}) collective-permute-start(bf16[128,1536]{1,0:T(8,128)(2,1)S(1)} %copy-done.15), channel_id=1, source_target_pairs={{0,4},{4,0},{1,5},{5,1},{2,6},{6,2},{3,7},{7,3},{8,12},{12,8},{9,1... | collective-permute-start | bytes 1179656 | tf_op jit(solution)/shard_map/ppermute | solution.py:76
  163.4 7.9 %copy-start.11 = (f32[256,1536]{1,0:T(8,128)S(1)}, f32[256,1536]{1,0:T(8,128)}, u32[]{:S(2)}) copy-start(f32[256,1536]{1,0:T(8,128)} %get-tuple-element.146) | copy-start | bytes 4718596
  163.4 7.8 %collective-permute-start.30 = (bf16[32,6144]{1,0:T(8,128)(2,1)S(1)}, bf16[32,6144]{1,0:T(8,128)(2,1)S(1)}, u32[]{:S(2)}, u32[]{:S(2)}) collective-permute-start(bf16[32,6144]{1,0:T(8,128)(2,1)S(1)} %fusion.14), channel_id=1, source_target_pairs={{0,8},{8,16},{16,24},{24,26},{26,18},{18,10},{10,2},{2,0},{9,1},{1... | collective-permute-start | bytes 1179656 | tf_op jit(solution)/shard_map/ppermute | solution.py:70
  185.5 6.4 %copy-start.1 = (bf16[256,6144]{1,0:T(8,128)(2,1)S(1)}, bf16[256,6144]{1,0:T(8,128)(2,1)}, u32[]{:S(2)}) copy-start(bf16[256,6144]{1,0:T(8,128)(2,1)} %copy-done) | copy-start | bytes 9437188
  185.5 3.5 %collective-permute-start.34 = (bf16[128,6144]{1,0:T(8,128)(2,1)S(1)}, bf16[128,6144]{1,0:T(8,128)(2,1)S(1)}, u32[]{:S(2)}, u32[]{:S(2)}) collective-permute-start(bf16[128,6144]{1,0:T(8,128)(2,1)S(1)} %slice.281), channel_id=1, source_target_pairs={{0,1},{1,0},{2,3},{3,2},{4,5},{5,4},{6,7},{7,6},{8,9},{9,8},{10,11... | collective-permute-start | bytes 4718600 | tf_op jit(solution)/shard_map/ppermute | solution.py:73
  191.4 6.0 %collective-permute-start.35 = (bf16[16,6144]{1,0:T(8,128)(2,1)S(1)}, bf16[16,6144]{1,0:T(8,128)(2,1)S(1)}, u32[]{:S(2)}, u32[]{:S(2)}) collective-permute-start(bf16[16,6144]{1,0:T(8,128)(2,1)S(1)} %get-tuple-element.103), channel_id=1, source_target_pairs={{0,8},{8,16},{16,24},{24,26},{26,18},{18,10},{10,2},{2,0},{9,1},{1... | collective-permute-start | bytes 589832 | tf_op jit(solution)/shard_map/ppermute | solution.py:70
  197.5 8.1 %collective-permute-start.36 = (bf16[32,6144]{1,0:T(8,128)(2,1)S(1)}, bf16[32,6144]{1,0:T(8,128)(2,1)S(1)}, u32[]{:S(2)}, u32[]{:S(2)}) collective-permute-start(bf16[32,6144]{1,0:T(8,128)(2,1)S(1)} %pad_maximum_fusion.18), channel_id=1, source_target_pairs={{0,8},{8,16},{16,24},{24,26},{26,18},{18,10},{10,2},{2,0},{9,1},{1... | collective-permute-start | bytes 1179656 | tf_op jit(solution)/shard_map/ppermute | solution.py:70
  205.7 8.2 %collective-permute-start.37 = (bf16[32,6144]{1,0:T(8,128)(2,1)S(1)}, bf16[32,6144]{1,0:T(8,128)(2,1)S(1)}, u32[]{:S(2)}, u32[]{:S(2)}) collective-permute-start(bf16[32,6144]{1,0:T(8,128)(2,1)S(1)} %fusion.12), channel_id=1, source_target_pairs={{0,8},{8,16},{16,24},{24,26},{26,18},{18,10},{10,2},{2,0},{9,1},{1... | collective-permute-start | bytes 1179656 | tf_op jit(solution)/shard_map/ppermute | solution.py:70
  207.3 10.5 %collective-permute-start.32 = (bf16[32,6144]{1,0:T(8,128)(2,1)S(1)}, bf16[32,6144]{1,0:T(8,128)(2,1)S(1)}, u32[]{:S(2)}, u32[]{:S(2)}) collective-permute-start(bf16[32,6144]{1,0:T(8,128)(2,1)S(1)} %fusion.15), channel_id=1, source_target_pairs={{0,8},{8,16},{16,24},{24,26},{26,18},{18,10},{10,2},{2,0},{9,1},{1... | collective-permute-start | bytes 1179656 | tf_op jit(solution)/shard_map/ppermute | solution.py:70
  214.0 7.9 %collective-permute-start.38 = (bf16[32,6144]{1,0:T(8,128)(2,1)S(1)}, bf16[32,6144]{1,0:T(8,128)(2,1)S(1)}, u32[]{:S(2)}, u32[]{:S(2)}) collective-permute-start(bf16[32,6144]{1,0:T(8,128)(2,1)S(1)} %fusion.13), channel_id=1, source_target_pairs={{0,8},{8,16},{16,24},{24,26},{26,18},{18,10},{10,2},{2,0},{9,1},{1... | collective-permute-start | bytes 1179656 | tf_op jit(solution)/shard_map/ppermute | solution.py:70
  217.8 4.3 %collective-permute-start.33 = (bf16[16,6144]{1,0:T(8,128)(2,1)S(1)}, bf16[16,6144]{1,0:T(8,128)(2,1)S(1)}, u32[]{:S(2)}, u32[]{:S(2)}) collective-permute-start(bf16[16,6144]{1,0:T(8,128)(2,1)S(1)} %slice.220), channel_id=1, source_target_pairs={{0,1},{1,0},{2,3},{3,2},{4,5},{5,4},{6,7},{7,6},{8,9},{9,8},{10,11... | collective-permute-start | bytes 589832 | tf_op jit(solution)/shard_map/ppermute | solution.py:73
  222.0 1.5 collective-permute-start.39
  (9 other events, 26.4 us)

commit v3 on v2

--- a/solution.py
+++ b/solution.py
@@ -113,10 +113,41 @@
     return lax.optimization_barrier((x, others))[0]
 
 
+def back_rows(pg, w_in, tile):
+    rows, hidden = pg.shape
+    width = w_in.shape[0]
+    half = rows // 2
+
+    def kernel(pg_ref, w_ref, keep_ref, send_ref):
+        out = times_transpose(pg_ref[...], w_ref[...])
+        keep_ref[...] = out[:half]
+        send_ref[...] = out[half:].astype(bf16)
+
+    return pl.pallas_call(
+        kernel,
+        grid=(width // tile,),
+        in_specs=[
+            pl.BlockSpec((rows, hidden), lambda i: (0, 0)),
+            pl.BlockSpec((tile, hidden), lambda i: (i, 0)),
+        ],
+        out_specs=[pl.BlockSpec((half, tile), lambda i: (0, i))] * 2,
+        out_shape=[
+            jax.ShapeDtypeStruct((half, width), f32),
+            jax.ShapeDtypeStruct((half, width), bf16),
+        ],
+        compiler_params=pltpu.CompilerParams(vmem_limit_bytes=40 << 20),
+        cost_estimate=pl.CostEstimate(
+            flops=2 * rows * hidden * width,
+            bytes_accessed=2 * hidden * (rows + width) + 6 * half * width,
+            transcendentals=0,
+        ),
+    )(pg, w_in)
+
+
 def shards_ring(links, tokens, out_grad, w_in, b_in, w_out):
     far = links.far
     step = tokens.shape[0] // 2
-    cat = jnp.concatenate
+    cat, pair = jnp.concatenate, lambda *xs: lax.optimization_barrier(xs)
 
     def together(send, blocks):
         sizes = [b.shape[0] for b in blocks]
@@ -187,15 +218,9 @@
     pg1, sum1 = backprop(done["s"], s1x, slope1)
     act1, pg1, sum1 = lax.optimization_barrier((act1.astype(bf16), pg1, sum1))
     s2 = signals(after(grad2, pg1, p2))
-    parts = lambda x: [x[: 8 * step], x[8 * step :]]
-    p2x, s2x = [[other_half(h) for h in parts(x)] for x in (p2, s2)]
-
-    def own_sums(pg, beside=None):
-        partial = times_transpose(pg, w_in)
-        if beside is not None:
-            partial, beside = lax.optimization_barrier((partial, beside))
-        theirs = links.sibling(partial.astype(bf16)[8 * step :])
-        return partial, partial[: 8 * step] + theirs.astype(f32), beside
+    def own_sums(pg, *beside):
+        keep, send, *beside = pair(*back_rows(pg, w_in, w_in.shape[0] // 6), *beside)
+        return send, keep + links.sibling(send).astype(f32), beside
 
     def scatter(own, beside):
         running = own[(2 * far - 1) * step :].astype(bf16)
@@ -214,26 +239,33 @@
             if work is not None:
                 running = after(running, work)
 
-    part1, own1, p2x[1] = own_sums(after(pg1, s2, p2x[0]), p2x[1])
-    act2, slope2 = activate(p2, cat(p2x))
-    act2, slope2 = lax.optimization_barrier((act2.astype(bf16), slope2))
+    def pieces(x, n):
+        size = x.shape[0] // n
+        return [x[i * size : (i + 1) * size] for i in range(n)]
+
+    p2_a, p2_b = pieces(p2, 2)
+    s2, p2x_a = pair(s2, other_half(p2_a))
+    s2_first, *s2_rest = pieces(s2, 4)
+    part1, own1, (p2x_b, *s2x) = own_sums(
+        after(pg1, s2), other_half(after(p2_b, s2)), other_half(s2_first)
+    )
+    act2, slope2 = activate(p2, cat([p2x_a, p2x_b]))
+    act2, slope2 = pair(act2.astype(bf16), slope2)
     made = {}
 
     def beside1(n, ready):
         if n == 3:
-            pg2, made["sum2"] = backprop(s2, cat(after(s2x, ready, made["out"])), slope2)
+            pg2, made["sum2"] = backprop(s2, cat(after(s2x, ready)), slope2)
             made["pg2"] = pg2
             made["part2"], made["own2"], _ = own_sums(pg2)
             return made["part2"]
-        wait = made.get("part2", made.get("out", part1))
+        wait = made.get("out", part1)
         a1, a2 = after((act1, act2), ready, wait)
-        index = n
-        made["out"] = over_rows_tiles(
-            [a1, a2], [grad1, grad2], made.get("out"), 2 * index, 2, act1.shape[1] // 6
+        out = over_rows_tiles(
+            [a1, a2], [grad1, grad2], made.get("out"), 2 * n, 2, act1.shape[1] // 6
         )
-        pairing = {0: 0, 3 - 1: 1}.get(n)
-        if pairing is not None:
-            made["out"], s2x[pairing] = lax.optimization_barrier((made["out"], s2x[pairing]))
+        made["out"], more = pair(out, other_half(after(s2_rest[n], wait)))
+        s2x.append(more)
         return made["out"]
 
     in1, _ = scatter(own1, beside1)

time: 225 us -> 215 us (0.956)
  matrix products: 64.9 us -> 38.6 us
  Pallas kernels: 32.8 us -> 53.3 us
  waiting for transfers between devices: 57.2 us -> 51.3 us
  starting transfers between devices: 42.9 us -> 46.7 us
  other arithmetic: 13.6 us -> 11 us
    dot_general x4 -> x2, matrix products: 44.6 us -> 20.6 us  [times_transpose(): lax.dot_general(left, right, (((1,), (1,)), ((), ())), preferred_element_...]
    pallas_call x0 -> x2, Pallas kernels: none -> 20.7 us  [back_rows(): pl.pallas_call(kernel, grid=(width // tile,), in_specs=[pl.BlockSpec((row...]
    ppermute x6 -> x8, waiting for transfers between devices: 9.46 us -> 2.03 us  [across(): return lax.ppermute(x, 'dp', [(0, 1), (1, 0)])]
    ppermute x20, starting transfers between devices: 33.4 us -> 36.4 us  [onward(): return lax.ppermute(x, ROWS, self.ring)]
    slice x4 -> x2, local copies, waits for them, and re-layouts: 6.09 us -> 3.19 us  [pieces(): return [x[i * size:(i + 1) * size] for i in range(n)]]
    ppermute x14, waiting for transfers between devices: 5.47 us -> 8.17 us  [sibling(): return lax.ppermute(x, 'tensor', self.core)]
    dot_general x2, matrix products: 20.4 us -> 18 us  [project(): return jnp.dot(rows, w_in, preferred_element_type=f32)]
    unnamed x57 -> x63, local copies, waits for them, and re-layouts: 5.02 us -> 7.36 us
  transfers between devices with their start and end apart: 40 -> 42, of which waited for: 20 -> 21; matrix products, arithmetic and copies ran while one was open for 24% -> 19% of each run, Pallas kernels for 15% -> 20%
where the time goes in v3:
time: 215 us; the launch traced here: 214 us
  Pallas kernels  53.3 us (25%)
  waiting for transfers between devices  51.3 us (24%)
  starting transfers between devices  46.7 us (22%)
  matrix products  38.6 us (18%)
  local copies, waits for them, and re-layouts  12.1 us (6%)
  other arithmetic  11 us (5%)
    ppermute x20, waiting for transfers between devices, onward(): return lax.ppermute(x, ROWS, self.ring)  41.1 us
    ppermute x20, starting transfers between devices, onward(): return lax.ppermute(x, ROWS, self.ring)  36.4 us
    pallas_call x6, Pallas kernels, over_rows_tiles(): pl.pallas_call(kernel, grid=(count,), in_specs=in_specs, out_specs=pl.Blo...  32.7 us
    pallas_call x2, Pallas kernels, back_rows(): pl.pallas_call(kernel, grid=(width // tile,), in_specs=[pl.BlockSpec((row...  20.7 us
    dot_general x2, matrix products, times_transpose(): lax.dot_general(left, right, (((1,), (1,)), ((), ())), preferred_element_...  20.6 us
    dot_general x2, matrix products, project(): return jnp.dot(rows, w_in, preferred_element_type=f32)  18 us
    ppermute x14, waiting for transfers between devices, sibling(): return lax.ppermute(x, 'tensor', self.core)  8.17 us
    ppermute x8, starting transfers between devices, across(): return lax.ppermute(x, 'dp', [(0, 1), (1, 0)])  7.88 us
  transfers between devices with their start and end apart: 42, of which 21 were waited for; matrix products, arithmetic and copies ran while one was open for 19% of the time, Pallas kernels for 20%

profile of v3, /device:TPU:0, one launch (start us, length us, event | category | flops | bytes accessed | tf_op | source)
XLA Modules:
  0.0 214.3 jit_solution(5079554592627971910)
XLA Ops:
  3.5 3.1 %collective-permute-start.1 = (bf16[32,6144]{1,0:T(8,128)(2,1)S(1)}, bf16[32,6144]{1,0:T(8,128)(2,1)S(1)}, u32[]{:S(2)}, u32[]{:S(2)}) collective-permute-start(bf16[32,6144]{1,0:T(8,128)(2,1)S(1)} %pad_maximum_fusion.12), channel_id=1, source_target_pairs={{0,8},{8,16},{16,24},{24,26},{26,18},{18,10},{10,2},{2,0},{9,1},{1... | collective-permute-start | bytes 1179656 | tf_op jit(solution)/shard_map/ppermute | solution.py:70
  6.6 1.6 collective-permute-start.8
  8.2 4.0 %collective-permute-done.1 = bf16[32,6144]{1,0:T(8,128)(2,1)S(1)} collective-permute-done((bf16[32,6144]{1,0:T(8,128)(2,1)S(1)}, bf16[32,6144]{1,0:T(8,128)(2,1)S(1)}, u32[]{:S(2)}, u32[]{:S(2)}) %collective-permute-start.1) | collective-permute-done | bytes 393248 | tf_op jit(solution)/shard_map/ppermute | solution.py:70
  12.2 2.1 collective-permute-start.2
  14.3 2.1 collective-permute-done.8
  16.4 2.1 collective-permute-start.9
  18.5 2.1 collective-permute-done.2
  20.6 2.1 collective-permute-start.4
  22.9 2.0 collective-permute-done.9
  24.9 2.1 collective-permute-start.10
  26.9 2.1 collective-permute-done.4
  29.1 2.1 collective-permute-start.5
  31.4 1.9 collective-permute-done.10
  33.3 2.1 collective-permute-start.14
  35.6 3.5 %collective-permute-done.14 = bf16[16,6144]{1,0:T(8,128)(2,1)S(1)} collective-permute-done((bf16[16,6144]{1,0:T(8,128)(2,1)S(1)}, bf16[16,6144]{1,0:T(8,128)(2,1)S(1)}, u32[]{:S(2)}, u32[]{:S(2)}) %collective-permute-start.14) | collective-permute-done | bytes 196640 | tf_op jit(solution)/shard_map/ppermute | solution.py:70
  39.4 1.7 collective-permute-done.15
  41.3 2.1 collective-permute-start.11
  43.6 9.0 %fusion.35 = f32[256,1536]{1,0:T(8,128)S(1)} fusion(bf16[256,6144]{1,0:T(8,128)(2,1)S(1)} %constant_dynamic-update-slice_fusion.refs_0_, bf16[6144,1536]{1,0:T(8,128)(2,1)} %w_ref.3), kind=kOutput, calls=%fused_computation.109 | convolution fusion | flops 4831838208 | bytes 23592960 | tf_op jit(solution)/shard_map/dot_general | solution.py:183
  55.5 2.1 collective-permute-start.17
  57.5 1.5 collective-permute-start.12
  59.0 10.5 %fusion.34 = (bf16[256,1536]{1,0:T(8,128)(2,1)}, f32[256,1536]{1,0:T(8,128)}) fusion(bf16[256,6144]{1,0:T(8,128)(2,1)S(1)} %constant_dynamic-update-slice_fusion.8.refs_2_, bf16[1536,6144]{1,0:T(8,128)(2,1)} %param.9), kind=kOutput, calls=%fused_computation.108 | convolution fusion | flops 4832231424 | bytes 24379392 | tf_op jit(solution)/shard_map/dot_general | solution.py:25
  71.3 1.6 collective-permute-start.18
  73.7 9.7 %collective-permute-done.18 = bf16[64,6144]{1,0:T(8,128)(2,1)S(1)} collective-permute-done((bf16[64,6144]{1,0:T(8,128)(2,1)S(1)}, bf16[64,6144]{1,0:T(8,128)(2,1)S(1)}, u32[]{:S(2)}, u32[]{:S(2)}) %collective-permute-start.18) | collective-permute-done | bytes 786464 | tf_op jit(solution)/shard_map/ppermute | solution.py:70
  83.4 1.8 collective-permute-start.19
  85.5 6.0 %collective-permute-done.19 = bf16[32,6144]{1,0:T(8,128)(2,1)S(1)} collective-permute-done((bf16[32,6144]{1,0:T(8,128)(2,1)S(1)}, bf16[32,6144]{1,0:T(8,128)(2,1)S(1)}, u32[]{:S(2)}, u32[]{:S(2)}) %collective-permute-start.19) | collective-permute-done | bytes 393248 | tf_op jit(solution)/shard_map/ppermute | solution.py:70
  93.0 3.8 %convert_reduce_fusion.1 = (f32[1536]{0:T(1024)S(1)}, bf16[256,1536]{1,0:T(8,128)(2,1)}, bf16[256,1536]{1,0:T(8,128)(2,1)}) fusion(f32[1536]{0:T(1024)S(1)} %copy-done.19, f32[256,1536]{1,0:T(8,128)S(1)} %copy-done.4, bf16[256,1536]{1,0:T(8,128)(2,1)} %collective-permute-done.12, f32[256,1536]{1,0:T(8,128)S(1)} %copy-done.16, ...), kind=kLoop, calls=%fused_computation.22 | loop fusion | flops 11008512 | bytes 6303744 | tf_op jit(solution)/shard_map/reduce_sum | solution.py:193
  99.2 9.0 %fusion.36 = f32[256,1536]{1,0:T(8,128)S(1)} fusion(bf16[256,6144]{1,0:T(8,128)(2,1)S(1)} %get-tuple-element.121.refs_1_, bf16[6144,1536]{1,0:T(8,128)(2,1)} %w_ref.3), kind=kOutput, calls=%fused_computation.110 | convolution fusion | flops 4831838208 | bytes 23592960 | tf_op jit(solution)/shard_map/dot_general | solution.py:183
  110.3 1.5 collective-permute-start.24
  111.8 10.1 %fusion.37 = f32[256,1536]{1,0:T(8,128)} fusion(bf16[256,6144]{1,0:T(8,128)(2,1)S(1)} %get-tuple-element.76.refs_3_, bf16[1536,6144]{1,0:T(8,128)(2,1)} %param.9), kind=kOutput, calls=%fused_computation.111 | convolution fusion | flops 4831838208 | bytes 23592960 | tf_op jit(solution)/shard_map/dot_general | solution.py:25
  122.0 2.2 %fusion.26 = (bf16[64,1536]{1,0:T(8,128)(2,1)}, bf16[64,1536]{1,0:T(8,128)(2,1)}, bf16[64,1536]{1,0:T(8,128)(2,1)}, bf16[64,1536]{1,0:T(8,128)(2,1)S(1)}) fusion(f32[256,1536]{1,0:T(8,128)} %fusion.37), kind=kLoop, calls=%fused_computation.100 | loop fusion | bytes 1572864 | tf_op jit(solution)/shard_map/slice | solution.py:244
  127.4 10.4 %shard_map.84 = (f32[128,6144]{1,0:T(8,128)S(1)}, bf16[128,6144]{1,0:T(8,128)(2,1)S(1)}) custom-call(bf16[256,1536]{1,0:T(8,128)(2,1)S(1)} %copy-done, bf16[6144,1536]{1,0:T(8,128)(2,1)} %w_ref.3), custom_call_target="tpu_custom_call" | custom-call | flops 4831838208 | bytes 24379392 | tf_op jit(solution)/shard_map/pallas_call | solution.py:126
  140.4 1.7 collective-permute-done.27
  142.7 1.6 collective-permute-start.28
  144.3 5.4 %shard_map.85.refs_4_ = bf16[1536,6144]{1,0:T(8,128)(2,1)} custom-call(bf16[256,1536]{1,0:T(8,128)(2,1)S(1)} %copy-done.2, bf16[256,1536]{1,0:T(8,128)(2,1)S(1)} %get-tuple-element.99.refs_1_, bf16[256,6144]{1,0:T(8,128)(2,1)S(1)} %constant_dynamic-update-slice_fusion.8.refs_2_, bf16[256,6144]{1,0:T(8,128)(2,1)S(1)} %get-tuple-element.76.refs_3_), custom_call_target="tpu_custom_call" | custom-call | flops 3221225472 | bytes 13107200 | tf_op jit(solution)/shard_map/pallas_call | solution.py:96
  149.8 1.9 collective-permute-start.30
  152.3 5.4 %shard_map.86.refs_4_ = bf16[1536,6144]{1,0:T(8,128)(2,1)} custom-call(bf16[256,1536]{1,0:T(8,128)(2,1)S(1)} %copy-done.2, bf16[256,1536]{1,0:T(8,128)(2,1)S(1)} %get-tuple-element.99.refs_1_, bf16[256,6144]{1,0:T(8,128)(2,1)S(1)} %constant_dynamic-update-slice_fusion.8.refs_2_, ...), custom_call_target="tpu_custom_call", output_to_operand_aliasing={{}: (4, {})} | custom-call | flops 3221225472 | bytes 13107200 | tf_op jit(solution)/shard_map/pallas_call | solution.py:96
  158.0 1.5 collective-permute-start.32
  160.7 5.4 %shard_map.87 = bf16[1536,6144]{1,0:T(8,128)(2,1)} custom-call(bf16[256,1536]{1,0:T(8,128)(2,1)S(1)} %copy-done.2, bf16[256,1536]{1,0:T(8,128)(2,1)S(1)} %get-tuple-element.99.refs_1_, bf16[256,6144]{1,0:T(8,128)(2,1)S(1)} %constant_dynamic-update-slice_fusion.8.refs_2_, ...), custom_call_target="tpu_custom_call", output_to_operand_aliasing={{}: (4, {})} | custom-call | flops 3221225472 | bytes 13107200 | tf_op jit(solution)/shard_map/pallas_call | solution.py:96
  166.6 10.3 %shard_map.88 = (f32[128,6144]{1,0:T(8,128)S(1)}, bf16[128,6144]{1,0:T(8,128)(2,1)S(1)}) custom-call(bf16[256,1536]{1,0:T(8,128)(2,1)S(1)} %get-tuple-element.125.pg_ref.refs_3_, bf16[6144,1536]{1,0:T(8,128)(2,1)} %w_ref.3), custom_call_target="tpu_custom_call" | custom-call | flops 4831838208 | bytes 24379392 | tf_op jit(solution)/shard_map/pallas_call | solution.py:126
  177.0 3.4 %collective-permute-done.36 = bf16[128,6144]{1,0:T(8,128)(2,1)S(1)} collective-permute-done((bf16[128,6144]{1,0:T(8,128)(2,1)S(1)}, bf16[128,6144]{1,0:T(8,128)(2,1)S(1)}, u32[]{:S(2)}, u32[]{:S(2)}) %collective-permute-start.36) | collective-permute-done | bytes 1572896 | tf_op jit(solution)/shard_map/ppermute | solution.py:73
  182.1 5.5 %shard_map.89.refs_4_ = bf16[6144,1536]{1,0:T(8,128)(2,1)} custom-call(bf16[256,6144]{1,0:T(8,128)(2,1)S(1)} %constant_dynamic-update-slice_fusion.refs_0_, bf16[256,6144]{1,0:T(8,128)(2,1)S(1)} %get-tuple-element.121.refs_1_, bf16[256,1536]{1,0:T(8,128)(2,1)S(1)} %copy-done.1, bf16[256,1536]{1,0:T(8,128)(2,1)S(1)} %get-tuple-element.125.pg_ref.refs_3_), custom_call_target="tpu_custom_call" | custom-call | flops 3221225472 | bytes 9961472 | tf_op jit(solution)/shard_map/pallas_call | solution.py:96
  187.7 1.6 collective-permute-start.38
  189.3 5.5 %shard_map.90.refs_4_ = bf16[6144,1536]{1,0:T(8,128)(2,1)} custom-call(bf16[256,6144]{1,0:T(8,128)(2,1)S(1)} %constant_dynamic-update-slice_fusion.refs_0_, bf16[256,6144]{1,0:T(8,128)(2,1)S(1)} %get-tuple-element.121.refs_1_, bf16[256,1536]{1,0:T(8,128)(2,1)S(1)} %copy-done.1, ...), custom_call_target="tpu_custom_call", output_to_operand_aliasing={{}: (4, {})} | custom-call | flops 3221225472 | bytes 9961472 | tf_op jit(solution)/shard_map/pallas_call | solution.py:96
  195.7 1.6 collective-permute-start.39
  197.8 5.5 %shard_map.91 = bf16[6144,1536]{1,0:T(8,128)(2,1)} custom-call(bf16[256,6144]{1,0:T(8,128)(2,1)S(1)} %constant_dynamic-update-slice_fusion.refs_0_, bf16[256,6144]{1,0:T(8,128)(2,1)S(1)} %get-tuple-element.121.refs_1_, bf16[256,1536]{1,0:T(8,128)(2,1)S(1)} %copy-done.1, ...), custom_call_target="tpu_custom_call", output_to_operand_aliasing={{}: (4, {})} | custom-call | flops 3221225472 | bytes 9961472 | tf_op jit(solution)/shard_map/pallas_call | solution.py:96
  203.6 1.6 collective-permute-start.40
  205.2 2.5 %collective-permute-done.34 = bf16[32,6144]{1,0:T(8,128)(2,1)S(1)} collective-permute-done((bf16[32,6144]{1,0:T(8,128)(2,1)S(1)}, bf16[32,6144]{1,0:T(8,128)(2,1)S(1)}, u32[]{:S(2)}, u32[]{:S(2)}) %collective-permute-start.34) | collective-permute-done | bytes 393248 | tf_op jit(solution)/shard_map/ppermute | solution.py:70
  208.4 3.5 %collective-permute-done.40 = bf16[32,6144]{1,0:T(8,128)(2,1)S(1)} collective-permute-done((bf16[32,6144]{1,0:T(8,128)(2,1)S(1)}, bf16[32,6144]{1,0:T(8,128)(2,1)S(1)}, u32[]{:S(2)}, u32[]{:S(2)}) %collective-permute-start.40) | collective-permute-done | bytes 393248 | tf_op jit(solution)/shard_map/ppermute | solution.py:70
  (163 shorter events, 31.1 us)
Async XLA Ops:
  0.6 2.8 %collective-permute-start = (bf16[32,6144]{1,0:T(8,128)(2,1)}, bf16[32,6144]{1,0:T(8,128)(2,1)S(1)}, u32[]{:S(2)}, u32[]{:S(2)}) collective-permute-start(bf16[32,6144]{1,0:T(8,128)(2,1)} %param.5), channel_id=1, source_target_pairs={{0,1},{1,0},{2,3},{3,2},{4,5},{5,4},{6,7},{7,6},{8,9},{9,8},{10,11... | collective-permute-start | bytes 1179656 | tf_op jit(solution)/shard_map/ppermute | solution.py:73
  1.1 5.4 %collective-permute-start.7 = (bf16[32,6144]{1,0:T(8,128)(2,1)}, bf16[32,6144]{1,0:T(8,128)(2,1)S(1)}, u32[]{:S(2)}, u32[]{:S(2)}) collective-permute-start(bf16[32,6144]{1,0:T(8,128)(2,1)} %param.6), channel_id=1, source_target_pairs={{0,1},{1,0},{2,3},{3,2},{4,5},{5,4},{6,7},{7,6},{8,9},{9,8},{10,11... | collective-permute-start | bytes 1179656 | tf_op jit(solution)/shard_map/ppermute | solution.py:73
  3.4 36.0 %copy-start.14 = (bf16[32,6144]{1,0:T(8,128)(2,1)}, bf16[32,6144]{1,0:T(8,128)(2,1)S(1)}, u32[]{:S(2)}) copy-start(bf16[32,6144]{1,0:T(8,128)(2,1)S(1)} %collective-permute-done) | copy-start | bytes 1179652
  3.5 8.8 %collective-permute-start.1 = (bf16[32,6144]{1,0:T(8,128)(2,1)S(1)}, bf16[32,6144]{1,0:T(8,128)(2,1)S(1)}, u32[]{:S(2)}, u32[]{:S(2)}) collective-permute-start(bf16[32,6144]{1,0:T(8,128)(2,1)S(1)} %pad_maximum_fusion.12), channel_id=1, source_target_pairs={{0,8},{8,16},{16,24},{24,26},{26,18},{18,10},{10,2},{2,0},{9,1},{1... | collective-permute-start | bytes 1179656 | tf_op jit(solution)/shard_map/ppermute | solution.py:70
  6.5 34.7 %copy-start.12 = (bf16[32,6144]{1,0:T(8,128)(2,1)}, bf16[32,6144]{1,0:T(8,128)(2,1)S(1)}, u32[]{:S(2)}) copy-start(bf16[32,6144]{1,0:T(8,128)(2,1)S(1)} %collective-permute-done.7) | copy-start | bytes 1179652
  6.6 9.9 %collective-permute-start.8 = (bf16[32,6144]{1,0:T(8,128)(2,1)S(1)}, bf16[32,6144]{1,0:T(8,128)(2,1)S(1)}, u32[]{:S(2)}, u32[]{:S(2)}) collective-permute-start(bf16[32,6144]{1,0:T(8,128)(2,1)S(1)} %pad_maximum_fusion.15), channel_id=1, source_target_pairs={{0,8},{8,16},{16,24},{24,26},{26,18},{18,10},{10,2},{2,0},{9,1},{1... | collective-permute-start | bytes 1179656 | tf_op jit(solution)/shard_map/ppermute | solution.py:70
  12.2 8.4 %collective-permute-start.2 = (bf16[32,6144]{1,0:T(8,128)(2,1)S(1)}, bf16[32,6144]{1,0:T(8,128)(2,1)S(1)}, u32[]{:S(2)}, u32[]{:S(2)}) collective-permute-start(bf16[32,6144]{1,0:T(8,128)(2,1)S(1)} %collective-permute-done.1), channel_id=1, source_target_pairs={{0,8},{8,16},{16,24},{24,26},{26,18},{18,10},{10,2},{2,0},{9,1},{1... | collective-permute-start | bytes 1179656 | tf_op jit(solution)/shard_map/ppermute | solution.py:70
  16.4 8.4 %collective-permute-start.9 = (bf16[32,6144]{1,0:T(8,128)(2,1)S(1)}, bf16[32,6144]{1,0:T(8,128)(2,1)S(1)}, u32[]{:S(2)}, u32[]{:S(2)}) collective-permute-start(bf16[32,6144]{1,0:T(8,128)(2,1)S(1)} %collective-permute-done.8), channel_id=1, source_target_pairs={{0,8},{8,16},{16,24},{24,26},{26,18},{18,10},{10,2},{2,0},{9,1},{1... | collective-permute-start | bytes 1179656 | tf_op jit(solution)/shard_map/ppermute | solution.py:70
  20.6 8.4 %collective-permute-start.4 = (bf16[32,6144]{1,0:T(8,128)(2,1)S(1)}, bf16[32,6144]{1,0:T(8,128)(2,1)S(1)}, u32[]{:S(2)}, u32[]{:S(2)}) collective-permute-start(bf16[32,6144]{1,0:T(8,128)(2,1)S(1)} %collective-permute-done.2), channel_id=1, source_target_pairs={{0,8},{8,16},{16,24},{24,26},{26,18},{18,10},{10,2},{2,0},{9,1},{1... | collective-permute-start | bytes 1179656 | tf_op jit(solution)/shard_map/ppermute | solution.py:70
  22.8 16.4 %collective-permute-start.3 = (bf16[64,6144]{1,0:T(8,128)(2,1)S(1)}, bf16[64,6144]{1,0:T(8,128)(2,1)S(1)}, u32[]{:S(2)}, u32[]{:S(2)}) collective-permute-start(bf16[64,6144]{1,0:T(8,128)(2,1)S(1)} %pad_maximum_fusion), channel_id=1, source_target_pairs={{0,1},{1,0},{2,3},{3,2},{4,5},{5,4},{6,7},{7,6},{8,9},{9,8},{10,11... | collective-permute-start | bytes 2359304 | tf_op jit(solution)/shard_map/ppermute | solution.py:73
  24.9 8.4 %collective-permute-start.10 = (bf16[32,6144]{1,0:T(8,128)(2,1)S(1)}, bf16[32,6144]{1,0:T(8,128)(2,1)S(1)}, u32[]{:S(2)}, u32[]{:S(2)}) collective-permute-start(bf16[32,6144]{1,0:T(8,128)(2,1)S(1)} %collective-permute-done.9), channel_id=1, source_target_pairs={{0,8},{8,16},{16,24},{24,26},{26,18},{18,10},{10,2},{2,0},{9,1},{1... | collective-permute-start | bytes 1179656 | tf_op jit(solution)/shard_map/ppermute | solution.py:70
  29.1 6.3 %collective-permute-start.5 = (bf16[16,6144]{1,0:T(8,128)(2,1)S(1)}, bf16[16,6144]{1,0:T(8,128)(2,1)S(1)}, u32[]{:S(2)}, u32[]{:S(2)}) collective-permute-start(bf16[16,6144]{1,0:T(8,128)(2,1)S(1)} %slice.183), channel_id=1, source_target_pairs={{0,8},{8,16},{16,24},{24,26},{26,18},{18,10},{10,2},{2,0},{9,1},{1... | collective-permute-start | bytes 589832 | tf_op jit(solution)/shard_map/ppermute | solution.py:70
  31.3 7.9 %collective-permute-start.13 = (bf16[64,6144]{1,0:T(8,128)(2,1)S(1)}, bf16[64,6144]{1,0:T(8,128)(2,1)S(1)}, u32[]{:S(2)}, u32[]{:S(2)}) collective-permute-start(bf16[64,6144]{1,0:T(8,128)(2,1)S(1)} %pad_maximum_fusion.2), channel_id=1, source_target_pairs={{0,1},{1,0},{2,3},{3,2},{4,5},{5,4},{6,7},{7,6},{8,9},{9,8},{10,11... | collective-permute-start | bytes 2359304 | tf_op jit(solution)/shard_map/ppermute | solution.py:73
  33.3 5.7 %collective-permute-start.14 = (bf16[16,6144]{1,0:T(8,128)(2,1)S(1)}, bf16[16,6144]{1,0:T(8,128)(2,1)S(1)}, u32[]{:S(2)}, u32[]{:S(2)}) collective-permute-start(bf16[16,6144]{1,0:T(8,128)(2,1)S(1)} %slice.189), channel_id=1, source_target_pairs={{0,8},{8,16},{16,24},{24,26},{26,18},{18,10},{10,2},{2,0},{9,1},{1... | collective-permute-start | bytes 589832 | tf_op jit(solution)/shard_map/ppermute | solution.py:70
  35.5 3.8 %collective-permute-start.6 = (bf16[48,6144]{1,0:T(8,128)(2,1)S(1)}, bf16[48,6144]{1,0:T(8,128)(2,1)S(1)}, u32[]{:S(2)}, u32[]{:S(2)}) collective-permute-start(bf16[48,6144]{1,0:T(8,128)(2,1)S(1)} %pad_maximum_fusion.8), channel_id=1, source_target_pairs={{0,1},{1,0},{2,3},{3,2},{4,5},{5,4},{6,7},{7,6},{8,9},{9,8},{10,11... | collective-permute-start | bytes 1769480 | tf_op jit(solution)/shard_map/ppermute | solution.py:73
  39.1 2.1 collective-permute-start.15
  41.3 12.0 %collective-permute-start.11 = (bf16[64,6144]{1,0:T(8,128)(2,1)S(1)}, bf16[64,6144]{1,0:T(8,128)(2,1)S(1)}, u32[]{:S(2)}, u32[]{:S(2)}) collective-permute-start(bf16[64,6144]{1,0:T(8,128)(2,1)S(1)} %pad_maximum_fusion.1), channel_id=1, source_target_pairs={{0,8},{8,16},{16,24},{24,26},{26,18},{18,10},{10,2},{2,0},{9,1},{1... | collective-permute-start | bytes 2359304 | tf_op jit(solution)/shard_map/ppermute | solution.py:70
  55.5 14.6 %collective-permute-start.17 = (bf16[64,6144]{1,0:T(8,128)(2,1)}, bf16[64,6144]{1,0:T(8,128)(2,1)}, u32[]{:S(2)}, u32[]{:S(2)}) collective-permute-start(bf16[64,6144]{1,0:T(8,128)(2,1)} %pad_maximum_fusion.3), channel_id=1, source_target_pairs={{0,8},{8,16},{16,24},{24,26},{26,18},{18,10},{10,2},{2,0},{9,1},{1... | collective-permute-start | bytes 2359304 | tf_op jit(solution)/shard_map/ppermute | solution.py:70
  57.5 25.8 %collective-permute-start.12 = (bf16[256,1536]{1,0:T(8,128)(2,1)}, bf16[256,1536]{1,0:T(8,128)(2,1)}, u32[]{:S(2)}, u32[]{:S(2)}) collective-permute-start(bf16[256,1536]{1,0:T(8,128)(2,1)} %convert_element_type.114), channel_id=1, source_target_pairs={{0,4},{4,0},{1,5},{5,1},{2,6},{6,2},{3,7},{7,3},{8,12},{12,8},{9,1... | collective-permute-start | bytes 2359304 | tf_op jit(solution)/shard_map/ppermute | solution.py:76
  69.5 23.5 %collective-permute-start.16 = (bf16[256,1536]{1,0:T(8,128)(2,1)}, bf16[256,1536]{1,0:T(8,128)(2,1)S(1)}, u32[]{:S(2)}, u32[]{:S(2)}) collective-permute-start(bf16[256,1536]{1,0:T(8,128)(2,1)} %get-tuple-element.175), channel_id=1, source_target_pairs={{0,4},{4,0},{1,5},{5,1},{2,6},{6,2},{3,7},{7,3},{8,12},{12,8},{9,1... | collective-permute-start | bytes 2359304 | tf_op jit(solution)/shard_map/ppermute | solution.py:76
  71.3 12.0 %collective-permute-start.18 = (bf16[64,6144]{1,0:T(8,128)(2,1)S(1)}, bf16[64,6144]{1,0:T(8,128)(2,1)S(1)}, u32[]{:S(2)}, u32[]{:S(2)}) collective-permute-start(bf16[64,6144]{1,0:T(8,128)(2,1)S(1)} %pad_maximum_fusion.4), channel_id=1, source_target_pairs={{0,8},{8,16},{16,24},{24,26},{26,18},{18,10},{10,2},{2,0},{9,1},{1... | collective-permute-start | bytes 2359304 | tf_op jit(solution)/shard_map/ppermute | solution.py:70
  73.0 12.3 %collective-permute-start.22 = (bf16[64,6144]{1,0:T(8,128)(2,1)S(1)}, bf16[64,6144]{1,0:T(8,128)(2,1)S(1)}, u32[]{:S(2)}, u32[]{:S(2)}) collective-permute-start(bf16[64,6144]{1,0:T(8,128)(2,1)S(1)} %pad_maximum_fusion.6), channel_id=1, source_target_pairs={{0,1},{1,0},{2,3},{3,2},{4,5},{5,4},{6,7},{7,6},{8,9},{9,8},{10,11... | collective-permute-start | bytes 2359304 | tf_op jit(solution)/shard_map/ppermute | solution.py:73
  73.1 12.3 %collective-permute-start.20 = (bf16[64,6144]{1,0:T(8,128)(2,1)S(1)}, bf16[64,6144]{1,0:T(8,128)(2,1)S(1)}, u32[]{:S(2)}, u32[]{:S(2)}) collective-permute-start(bf16[64,6144]{1,0:T(8,128)(2,1)S(1)} %pad_maximum_fusion.5), channel_id=1, source_target_pairs={{0,1},{1,0},{2,3},{3,2},{4,5},{5,4},{6,7},{7,6},{8,9},{9,8},{10,11... | collective-permute-start | bytes 2359304 | tf_op jit(solution)/shard_map/ppermute | solution.py:73
  83.4 8.0 %collective-permute-start.19 = (bf16[32,6144]{1,0:T(8,128)(2,1)S(1)}, bf16[32,6144]{1,0:T(8,128)(2,1)S(1)}, u32[]{:S(2)}, u32[]{:S(2)}) collective-permute-start(bf16[32,6144]{1,0:T(8,128)(2,1)S(1)} %pad_maximum_fusion.16), channel_id=1, source_target_pairs={{0,8},{8,16},{16,24},{24,26},{26,18},{18,10},{10,2},{2,0},{9,1},{1... | collective-permute-start | bytes 1179656 | tf_op jit(solution)/shard_map/ppermute | solution.py:70
  85.3 7.7 %copy-start.4 = (f32[256,1536]{1,0:T(8,128)S(1)}, f32[256,1536]{1,0:T(8,128)}, u32[]{:S(2)}) copy-start(f32[256,1536]{1,0:T(8,128)} %copy-done.3) | copy-start | bytes 4718596
  91.5 5.2 %collective-permute-start.23 = (bf16[48,6144]{1,0:T(8,128)(2,1)S(1)}, bf16[48,6144]{1,0:T(8,128)(2,1)S(1)}, u32[]{:S(2)}, u32[]{:S(2)}) collective-permute-start(bf16[48,6144]{1,0:T(8,128)(2,1)S(1)} %pad_maximum_fusion.11), channel_id=1, source_target_pairs={{0,1},{1,0},{2,3},{3,2},{4,5},{5,4},{6,7},{7,6},{8,9},{9,8},{10,11... | collective-permute-start | bytes 1769480 | tf_op jit(solution)/shard_map/ppermute | solution.py:73
  91.7 5.2 %collective-permute-start.21 = (bf16[48,6144]{1,0:T(8,128)(2,1)S(1)}, bf16[48,6144]{1,0:T(8,128)(2,1)S(1)}, u32[]{:S(2)}, u32[]{:S(2)}) collective-permute-start(bf16[48,6144]{1,0:T(8,128)(2,1)S(1)} %pad_maximum_fusion.10), channel_id=1, source_target_pairs={{0,1},{1,0},{2,3},{3,2},{4,5},{5,4},{6,7},{7,6},{8,9},{9,8},{10,11... | collective-permute-start | bytes 1769480 | tf_op jit(solution)/shard_map/ppermute | solution.py:73
  110.3 11.6 %collective-permute-start.24 = (bf16[128,1536]{1,0:T(8,128)(2,1)}, bf16[128,1536]{1,0:T(8,128)(2,1)S(1)}, u32[]{:S(2)}, u32[]{:S(2)}) collective-permute-start(bf16[128,1536]{1,0:T(8,128)(2,1)} %get-tuple-element.144), channel_id=1, source_target_pairs={{0,4},{4,0},{1,5},{5,1},{2,6},{6,2},{3,7},{7,3},{8,12},{12,8},{9,1... | collective-permute-start | bytes 1179656 | tf_op jit(solution)/shard_map/ppermute | solution.py:76
  124.2 14.5 %collective-permute-start.25 = (bf16[128,1536]{1,0:T(8,128)(2,1)}, bf16[128,1536]{1,0:T(8,128)(2,1)S(1)}, u32[]{:S(2)}, u32[]{:S(2)}) collective-permute-start(bf16[128,1536]{1,0:T(8,128)(2,1)} %get-tuple-element.81), channel_id=1, source_target_pairs={{0,4},{4,0},{1,5},{5,1},{2,6},{6,2},{3,7},{7,3},{8,12},{12,8},{9,1... | collective-permute-start | bytes 1179656 | tf_op jit(solution)/shard_map/ppermute | solution.py:76
  124.7 14.0 %collective-permute-start.26 = (bf16[64,1536]{1,0:T(8,128)(2,1)S(1)}, bf16[64,1536]{1,0:T(8,128)(2,1)S(1)}, u32[]{:S(2)}, u32[]{:S(2)}) collective-permute-start(bf16[64,1536]{1,0:T(8,128)(2,1)S(1)} %get-tuple-element.140), channel_id=1, source_target_pairs={{0,4},{4,0},{1,5},{5,1},{2,6},{6,2},{3,7},{7,3},{8,12},{12,8},{9,1... | collective-permute-start | bytes 589832 | tf_op jit(solution)/shard_map/ppermute | solution.py:76
  127.4 11.9 %copy-start.7 = (f32[256,1536]{1,0:T(8,128)S(1)}, f32[256,1536]{1,0:T(8,128)}, u32[]{:S(2)}) copy-start(f32[256,1536]{1,0:T(8,128)} %copy-done.6) | copy-start | bytes 4718596
  138.7 3.4 %collective-permute-start.27 = (bf16[128,6144]{1,0:T(8,128)(2,1)S(1)}, bf16[128,6144]{1,0:T(8,128)(2,1)S(1)}, u32[]{:S(2)}, u32[]{:S(2)}) collective-permute-start(bf16[128,6144]{1,0:T(8,128)(2,1)S(1)} %get-tuple-element.83), channel_id=1, source_target_pairs={{0,1},{1,0},{2,3},{3,2},{4,5},{5,4},{6,7},{7,6},{8,9},{9,8},{10,11... | collective-permute-start | bytes 4718600 | tf_op jit(solution)/shard_map/ppermute | solution.py:73
  138.7 11.0 %collective-permute-start.29 = (bf16[64,1536]{1,0:T(8,128)(2,1)}, bf16[64,1536]{1,0:T(8,128)(2,1)S(1)}, u32[]{:S(2)}, u32[]{:S(2)}) collective-permute-start(bf16[64,1536]{1,0:T(8,128)(2,1)} %get-tuple-element.90), channel_id=1, source_target_pairs={{0,4},{4,0},{1,5},{5,1},{2,6},{6,2},{3,7},{7,3},{8,12},{12,8},{9,1... | collective-permute-start | bytes 589832 | tf_op jit(solution)/shard_map/ppermute | solution.py:76
  142.7 9.0 %copy-start.18 = (bf16[64,1536]{1,0:T(8,128)(2,1)S(1)}, bf16[64,1536]{1,0:T(8,128)(2,1)}, u32[]{:S(2)}) copy-start(bf16[64,1536]{1,0:T(8,128)(2,1)} %get-tuple-element.95) | copy-start | bytes 589828
  142.7 7.0 %collective-permute-start.28 = (bf16[16,6144]{1,0:T(8,128)(2,1)S(1)}, bf16[16,6144]{1,0:T(8,128)(2,1)S(1)}, u32[]{:S(2)}, u32[]{:S(2)}) collective-permute-start(bf16[16,6144]{1,0:T(8,128)(2,1)S(1)} %get-tuple-element.142), channel_id=1, source_target_pairs={{0,8},{8,16},{16,24},{24,26},{26,18},{18,10},{10,2},{2,0},{9,1},{1... | collective-permute-start | bytes 589832 | tf_op jit(solution)/shard_map/ppermute | solution.py:70
  149.8 8.2 %collective-permute-start.30 = (bf16[32,6144]{1,0:T(8,128)(2,1)S(1)}, bf16[32,6144]{1,0:T(8,128)(2,1)S(1)}, u32[]{:S(2)}, u32[]{:S(2)}) collective-permute-start(bf16[32,6144]{1,0:T(8,128)(2,1)S(1)} %pad_maximum_fusion.17), channel_id=1, source_target_pairs={{0,8},{8,16},{16,24},{24,26},{26,18},{18,10},{10,2},{2,0},{9,1},{1... | collective-permute-start | bytes 1179656 | tf_op jit(solution)/shard_map/ppermute | solution.py:70
  151.6 7.9 %copy-start.17 = (bf16[64,1536]{1,0:T(8,128)(2,1)S(1)}, bf16[64,1536]{1,0:T(8,128)(2,1)}, u32[]{:S(2)}) copy-start(bf16[64,1536]{1,0:T(8,128)(2,1)} %get-tuple-element.100) | copy-start | bytes 589828
  151.6 6.3 %collective-permute-start.31 = (bf16[64,1536]{1,0:T(8,128)(2,1)S(1)}, bf16[64,1536]{1,0:T(8,128)(2,1)S(1)}, u32[]{:S(2)}, u32[]{:S(2)}) collective-permute-start(bf16[64,1536]{1,0:T(8,128)(2,1)S(1)} %copy-done.18), channel_id=1, source_target_pairs={{0,4},{4,0},{1,5},{5,1},{2,6},{6,2},{3,7},{7,3},{8,12},{12,8},{9,1... | collective-permute-start | bytes 589832 | tf_op jit(solution)/shard_map/ppermute | solution.py:76
  158.0 8.1 %collective-permute-start.32 = (bf16[32,6144]{1,0:T(8,128)(2,1)S(1)}, bf16[32,6144]{1,0:T(8,128)(2,1)S(1)}, u32[]{:S(2)}, u32[]{:S(2)}) collective-permute-start(bf16[32,6144]{1,0:T(8,128)(2,1)S(1)} %fusion.14), channel_id=1, source_target_pairs={{0,8},{8,16},{16,24},{24,26},{26,18},{18,10},{10,2},{2,0},{9,1},{1... | collective-permute-start | bytes 1179656 | tf_op jit(solution)/shard_map/ppermute | solution.py:70
  159.5 6.6 %collective-permute-start.33 = (bf16[64,1536]{1,0:T(8,128)(2,1)S(1)}, bf16[64,1536]{1,0:T(8,128)(2,1)S(1)}, u32[]{:S(2)}, u32[]{:S(2)}) collective-permute-start(bf16[64,1536]{1,0:T(8,128)(2,1)S(1)} %copy-done.17), channel_id=1, source_target_pairs={{0,4},{4,0},{1,5},{5,1},{2,6},{6,2},{3,7},{7,3},{8,12},{12,8},{9,1... | collective-permute-start | bytes 589832 | tf_op jit(solution)/shard_map/ppermute | solution.py:76
  176.9 3.5 %collective-permute-start.36 = (bf16[128,6144]{1,0:T(8,128)(2,1)S(1)}, bf16[128,6144]{1,0:T(8,128)(2,1)S(1)}, u32[]{:S(2)}, u32[]{:S(2)}) collective-permute-start(bf16[128,6144]{1,0:T(8,128)(2,1)S(1)} %get-tuple-element.113), channel_id=1, source_target_pairs={{0,1},{1,0},{2,3},{3,2},{4,5},{5,4},{6,7},{7,6},{8,9},{9,8},{10,11... | collective-permute-start | bytes 4718600 | tf_op jit(solution)/shard_map/ppermute | solution.py:73
  180.9 6.8 %collective-permute-start.37 = (bf16[16,6144]{1,0:T(8,128)(2,1)S(1)}, bf16[16,6144]{1,0:T(8,128)(2,1)S(1)}, u32[]{:S(2)}, u32[]{:S(2)}) collective-permute-start(bf16[16,6144]{1,0:T(8,128)(2,1)S(1)} %get-tuple-element.135), channel_id=1, source_target_pairs={{0,8},{8,16},{16,24},{24,26},{26,18},{18,10},{10,2},{2,0},{9,1},{1... | collective-permute-start | bytes 589832 | tf_op jit(solution)/shard_map/ppermute | solution.py:70
  187.7 7.8 %collective-permute-start.38 = (bf16[32,6144]{1,0:T(8,128)(2,1)S(1)}, bf16[32,6144]{1,0:T(8,128)(2,1)S(1)}, u32[]{:S(2)}, u32[]{:S(2)}) collective-permute-start(bf16[32,6144]{1,0:T(8,128)(2,1)S(1)} %pad_maximum_fusion.18), channel_id=1, source_target_pairs={{0,8},{8,16},{16,24},{24,26},{26,18},{18,10},{10,2},{2,0},{9,1},{1... | collective-permute-start | bytes 1179656 | tf_op jit(solution)/shard_map/ppermute | solution.py:70
  195.7 7.8 %collective-permute-start.39 = (bf16[32,6144]{1,0:T(8,128)(2,1)S(1)}, bf16[32,6144]{1,0:T(8,128)(2,1)S(1)}, u32[]{:S(2)}, u32[]{:S(2)}) collective-permute-start(bf16[32,6144]{1,0:T(8,128)(2,1)S(1)} %fusion.12), channel_id=1, source_target_pairs={{0,8},{8,16},{16,24},{24,26},{26,18},{18,10},{10,2},{2,0},{9,1},{1... | collective-permute-start | bytes 1179656 | tf_op jit(solution)/shard_map/ppermute | solution.py:70
  197.2 10.5 %collective-permute-start.34 = (bf16[32,6144]{1,0:T(8,128)(2,1)S(1)}, bf16[32,6144]{1,0:T(8,128)(2,1)S(1)}, u32[]{:S(2)}, u32[]{:S(2)}) collective-permute-start(bf16[32,6144]{1,0:T(8,128)(2,1)S(1)} %fusion.15), channel_id=1, source_target_pairs={{0,8},{8,16},{16,24},{24,26},{26,18},{18,10},{10,2},{2,0},{9,1},{1... | collective-permute-start | bytes 1179656 | tf_op jit(solution)/shard_map/ppermute | solution.py:70
  203.6 8.3 %collective-permute-start.40 = (bf16[32,6144]{1,0:T(8,128)(2,1)S(1)}, bf16[32,6144]{1,0:T(8,128)(2,1)S(1)}, u32[]{:S(2)}, u32[]{:S(2)}) collective-permute-start(bf16[32,6144]{1,0:T(8,128)(2,1)S(1)} %fusion.13), channel_id=1, source_target_pairs={{0,8},{8,16},{16,24},{24,26},{26,18},{18,10},{10,2},{2,0},{9,1},{1... | collective-permute-start | bytes 1179656 | tf_op jit(solution)/shard_map/ppermute | solution.py:70
  207.7 4.3 %collective-permute-start.35 = (bf16[16,6144]{1,0:T(8,128)(2,1)S(1)}, bf16[16,6144]{1,0:T(8,128)(2,1)S(1)}, u32[]{:S(2)}, u32[]{:S(2)}) collective-permute-start(bf16[16,6144]{1,0:T(8,128)(2,1)S(1)} %slice.208), channel_id=1, source_target_pairs={{0,1},{1,0},{2,3},{3,2},{4,5},{5,4},{6,7},{7,6},{8,9},{9,8},{10,11... | collective-permute-start | bytes 589832 | tf_op jit(solution)/shard_map/ppermute | solution.py:73
  211.9 1.5 collective-permute-start.41
  (14 other events, 53.0 us)

commit v4 on v3

--- a/solution.py
+++ b/solution.py
@@ -149,44 +149,27 @@
     step = tokens.shape[0] // 2
     cat, pair = jnp.concatenate, lambda *xs: lax.optimization_barrier(xs)
 
-    def together(send, blocks):
-        sizes = [b.shape[0] for b in blocks]
-        got = send(cat(blocks))
-        return [got[sum(sizes[:i]) : sum(sizes[: i + 1])] for i in range(len(sizes))]
-
-    def apart(send, blocks):
-        return [send(b) for b in blocks]
-
-    def gather(chips, move, waits):
-        got = {0: chips}
-        for d in range(1, far + 1):
-            out = got[d - 1]
-            if d == far:
-                out = [b[:step] for b in out]
-            wait = waits(d, got)
-            if wait is not None:
-                out = after(out, wait)
-            got[d] = move(links.onward, out)
-        rows = []
-        for i in range(len(chips)):
-            early = cat([got[d][i] for d in range(1, far - 1)])
-            late = cat([got[d][i] for d in range(far - 1, far + 1)])
-            mine, theirs = chips[i][:step], chips[i][step:]
-            others = [links.sibling(early), links.sibling(late)]
-            rows.append(cat([mine, *others, theirs, early, late]))
-        return rows, got
+    def onward(block, d, *others):
+        if d == far:
+            block = block[:step]
+        return links.onward(after(block, *others) if others else block)
+
+    def rows_of(got):
+        early, late = cat(got[1 : far - 1]), cat(got[far - 1 :])
+        others = [links.sibling(early), links.sibling(late)]
+        return cat([got[0][:step], *others, got[0][step:], early, late])
 
     def other_half(own):
         return links.across(own.astype(bf16))
 
-    def project(rows):
-        return jnp.dot(rows, w_in, preferred_element_type=f32)
-
-    def signals(rows):
-        return times_transpose(rows, w_out)
-
-    def activate(p, p_other):
-        return gelu_pair(p + p_other.astype(f32) + b_in)
+    def project(rows, cols=slice(None)):
+        return jnp.dot(rows, w_in[:, cols], preferred_element_type=f32)
+
+    def signals(rows, cols=slice(None)):
+        return times_transpose(rows, w_out[cols])
+
+    def activate(p, p_other, cols=slice(None)):
+        return gelu_pair(p + p_other.astype(f32) + b_in[cols])
 
     def backprop(s, s_other, derivative):
         pg = ((s + s_other.astype(f32)) * derivative).astype(bf16)
@@ -194,30 +177,39 @@
 
     tok_sib, grad_sib = links.sibling(tokens), links.sibling(out_grad)
     chunk = lambda x, y, k: cat([x[k * step : (k + 1) * step], y[k * step : (k + 1) * step]])
-    chips = [[chunk(tokens, tok_sib, k), chunk(out_grad, grad_sib, k)] for k in range(2)]
-
-    (tok1, grad1), got1 = gather(chips[0], apart, lambda *_: None)
-    done = {}
-
-    def waits(d, got):
-        if d == 1:
-            return got1[far - 1]
-        if d == 2:
-            done["p"] = project(tok1)
-            return done["p"]
-        if d == 3:
-            done["s"] = signals(after(grad1, got[1], done["p"]))
-            done["px"] = other_half(after(done["p"], got[1]))
-            return done["s"]
-        return done["px"]
-
-    (tok2, grad2), got2 = gather(chips[1], together, waits)
-    s1x = after(other_half(done["s"]), got2[far])
-    p2 = project(tok2)
-    act1, slope1 = activate(done["p"], done["px"])
-    pg1, sum1 = backprop(done["s"], s1x, slope1)
-    act1, pg1, sum1 = lax.optimization_barrier((act1.astype(bf16), pg1, sum1))
-    s2 = signals(after(grad2, pg1, p2))
+    toks, grads = [
+        [[chunk(x, y, k)] for k in range(2)] for x, y in ((tokens, tok_sib), (out_grad, grad_sib))
+    ]
+
+    for d in range(1, far + 1):
+        toks[0].append(onward(toks[0][-1], d))
+        grads[0].append(onward(grads[0][-1], d))
+    tok1, grad1 = rows_of(toks[0]), rows_of(grads[0])
+
+    t, g = toks[1], grads[1]
+    halves = [slice(0, w_in.shape[1] // 2), slice(w_in.shape[1] // 2, None)]
+    t.append(onward(t[0], 1, toks[0][far - 1]))
+    g.append(onward(g[0], 1, grads[0][far - 1]))
+    p1, t[1], g[1] = pair(project(tok1), t[1], g[1])
+    t.append(onward(t[1], 2))
+    g.append(onward(g[1], 2))
+    for d in range(3, far):
+        t.append(onward(t[-1], d))
+    p1x = other_half(p1)
+    s_a, g[2], t[far - 1] = pair(signals(after(grad1, t[2], p1), halves[0]), g[2], t[far - 1])
+    for d in range(3, far):
+        g.append(onward(g[-1], d))
+    t.append(onward(t[-1], far))
+    s_b, g[far - 1], t[far] = pair(signals(after(grad1, s_a), halves[1]), g[far - 1], t[far])
+    s_ax, s_bx = other_half(s_a), other_half(s_b)
+    g.append(onward(g[-1], far))
+    tok2, grad2 = rows_of(t), rows_of(g)
+    p2, s_ax = pair(project(tok2), s_ax)
+    s2 = signals(after(grad2, p2))
+    act1, slope1 = activate(p1, p1x)
+    pg1, sum1 = backprop(cat([s_a, s_b], axis=1), cat([s_ax, s_bx], axis=1), slope1)
+    act1, pg1, sum1 = pair(act1.astype(bf16), pg1, sum1)
+
     def own_sums(pg, *beside):
         keep, send, *beside = pair(*back_rows(pg, w_in, w_in.shape[0] // 6), *beside)
         return send, keep + links.sibling(send).astype(f32), beside
@@ -245,7 +237,8 @@
 
     p2_a, p2_b = pieces(p2, 2)
     s2, p2x_a = pair(s2, other_half(p2_a))
-    s2_first, *s2_rest = pieces(s2, 4)
+    cuts = (0, 4 * step, 10 * step, 16 * step)
+    s2_first, *s2_rest = [s2[a:b] for a, b in zip(cuts, cuts[1:])]
     part1, own1, (p2x_b, *s2x) = own_sums(
         after(pg1, s2), other_half(after(p2_b, s2)), other_half(s2_first)
     )
@@ -254,21 +247,26 @@
     made = {}
 
     def beside1(n, ready):
-        if n == 3:
+        if n == 2:
             pg2, made["sum2"] = backprop(s2, cat(after(s2x, ready)), slope2)
             made["pg2"] = pg2
-            made["part2"], made["own2"], _ = own_sums(pg2)
-            return made["part2"]
-        wait = made.get("out", part1)
+            made["keep"], made["send"] = pair(*back_rows(pg2, w_in, w_in.shape[0] // 6))
+            made["theirs"] = links.sibling(made["send"])
+            return made["send"]
+        wait = made.get("send", made.get("out", part1))
         a1, a2 = after((act1, act2), ready, wait)
         out = over_rows_tiles(
-            [a1, a2], [grad1, grad2], made.get("out"), 2 * n, 2, act1.shape[1] // 6
+            [a1, a2], [grad1, grad2], made.get("out"), 2 * min(n, 2), 2, act1.shape[1] // 6
         )
-        made["out"], more = pair(out, other_half(after(s2_rest[n], wait)))
-        s2x.append(more)
+        if n == 3:
+            made["out"], made["theirs"] = pair(out, made["theirs"])
+        else:
+            made["out"], more = pair(out, other_half(after(s2_rest[n], wait)))
+            s2x.append(more)
         return made["out"]
 
     in1, _ = scatter(own1, beside1)
+    own2 = made["keep"] + made["theirs"].astype(f32)
 
     def beside2(n, ready):
         if n == 3:
@@ -279,7 +277,7 @@
         )
         return made["in"]
 
-    in2, _ = scatter(made["own2"], beside2)
+    in2, _ = scatter(own2, beside2)
     return (cat([in1, in2]), made["in"], made["out"], sum1 + made["sum2"])
 
 

time: 215 us -> 202 us (0.940)
  waiting for transfers between devices: 51.3 us -> 36.8 us
  starting transfers between devices: 46.7 us -> 52.8 us
  local copies, waits for them, and re-layouts: 12.1 us -> 7.14 us
    ppermute x20 -> x24, waiting for transfers between devices: 41.1 us -> 31.6 us  [onward(): return lax.ppermute(x, ROWS, self.ring)]
    ppermute x14, waiting for transfers between devices: 8.17 us -> 2.7 us  [sibling(): return lax.ppermute(x, 'tensor', self.core)]
    ppermute x20 -> x24, starting transfers between devices: 36.4 us -> 41.8 us  [onward(): return lax.ppermute(x, ROWS, self.ring)]
    unnamed x63 -> x42, local copies, waits for them, and re-layouts: 7.36 us -> 2.95 us
    slice x2 -> x1, local copies, waits for them, and re-layouts: 3.19 us -> 0.97 us  [pieces(): return [x[i * size:(i + 1) * size] for i in range(n)]]
    dot_general x2 -> x3, matrix products: 20.6 us -> 22.8 us  [times_transpose(): lax.dot_general(left, right, (((1,), (1,)), ((), ())), preferred_element_...]
  transfers between devices with their start and end apart: 42 -> 46, of which waited for: 21 -> 18; matrix products, arithmetic and copies ran while one was open for 19% -> 27% of each run, Pallas kernels for 20% -> 26%
where the time goes in v4:
time: 202 us
  Pallas kernels  53.4 us (26%)
  starting transfers between devices  52.8 us (26%)
  matrix products  40.7 us (20%)
  waiting for transfers between devices  36.8 us (18%)
  other arithmetic  9.64 us (5%)
  local copies, waits for them, and re-layouts  7.14 us (4%)
    ppermute x24, starting transfers between devices, onward(): return lax.ppermute(x, ROWS, self.ring)  41.8 us
    pallas_call x6, Pallas kernels, over_rows_tiles(): pl.pallas_call(kernel, grid=(count,), in_specs=in_specs, out_specs=pl.Blo...  32.7 us
    ppermute x24, waiting for transfers between devices, onward(): return lax.ppermute(x, ROWS, self.ring)  31.6 us
    dot_general x3, matrix products, times_transpose(): lax.dot_general(left, right, (((1,), (1,)), ((), ())), preferred_element_...  22.8 us
    pallas_call x2, Pallas kernels, back_rows(): pl.pallas_call(kernel, grid=(width // tile,), in_specs=[pl.BlockSpec((row...  20.7 us
    dot_general x2, matrix products, project(): return jnp.dot(rows, w_in[:, cols], preferred_element_type=f32)  18 us
    ppermute x8, starting transfers between devices, across(): return lax.ppermute(x, 'dp', [(0, 1), (1, 0)])  9.19 us
  transfers between devices with their start and end apart: 46, of which 18 were waited for; matrix products, arithmetic and copies ran while one was open for 27% of the time, Pallas kernels for 26%

profile of v4, /device:TPU:0, one launch (start us, length us, event | category | flops | bytes accessed | tf_op | source)
XLA Modules:
  0.0 201.9 jit_solution(3103893692244429526)
XLA Ops:
  3.5 3.1 %collective-permute-start.1 = (bf16[32,6144]{1,0:T(8,128)(2,1)S(1)}, bf16[32,6144]{1,0:T(8,128)(2,1)S(1)}, u32[]{:S(2)}, u32[]{:S(2)}) collective-permute-start(bf16[32,6144]{1,0:T(8,128)(2,1)S(1)} %pad_maximum_fusion.9), channel_id=1, source_target_pairs={{0,8},{8,16},{16,24},{24,26},{26,18},{18,10},{10,2},{2,0},{9,1},{1... | collective-permute-start | bytes 1179656 | tf_op jit(solution)/shard_map/ppermute | solution.py:70
  6.6 1.6 collective-permute-start.9
  8.2 4.0 %collective-permute-done.1 = bf16[32,6144]{1,0:T(8,128)(2,1)S(1)} collective-permute-done((bf16[32,6144]{1,0:T(8,128)(2,1)S(1)}, bf16[32,6144]{1,0:T(8,128)(2,1)S(1)}, u32[]{:S(2)}, u32[]{:S(2)}) %collective-permute-start.1) | collective-permute-done | bytes 393248 | tf_op jit(solution)/shard_map/ppermute | solution.py:70
  12.2 2.1 %collective-permute-start.2 = (bf16[32,6144]{1,0:T(8,128)(2,1)S(1)}, bf16[32,6144]{1,0:T(8,128)(2,1)S(1)}, u32[]{:S(2)}, u32[]{:S(2)}) collective-permute-start(bf16[32,6144]{1,0:T(8,128)(2,1)S(1)} %collective-permute-done.1), channel_id=1, source_target_pairs={{0,8},{8,16},{16,24},{24,26},{26,18},{18,10},{10,2},{2,0},{9,1},{1... | collective-permute-start | bytes 1179656 | tf_op jit(solution)/shard_map/ppermute | solution.py:70
  14.3 2.1 %collective-permute-done.9 = bf16[32,6144]{1,0:T(8,128)(2,1)S(1)} collective-permute-done((bf16[32,6144]{1,0:T(8,128)(2,1)S(1)}, bf16[32,6144]{1,0:T(8,128)(2,1)S(1)}, u32[]{:S(2)}, u32[]{:S(2)}) %collective-permute-start.9) | collective-permute-done | bytes 393248 | tf_op jit(solution)/shard_map/ppermute | solution.py:70
  16.4 2.1 %collective-permute-start.10 = (bf16[32,6144]{1,0:T(8,128)(2,1)S(1)}, bf16[32,6144]{1,0:T(8,128)(2,1)S(1)}, u32[]{:S(2)}, u32[]{:S(2)}) collective-permute-start(bf16[32,6144]{1,0:T(8,128)(2,1)S(1)} %collective-permute-done.9), channel_id=1, source_target_pairs={{0,8},{8,16},{16,24},{24,26},{26,18},{18,10},{10,2},{2,0},{9,1},{1... | collective-permute-start | bytes 1179656 | tf_op jit(solution)/shard_map/ppermute | solution.py:70
  18.5 2.1 %collective-permute-done.2 = bf16[32,6144]{1,0:T(8,128)(2,1)S(1)} collective-permute-done((bf16[32,6144]{1,0:T(8,128)(2,1)S(1)}, bf16[32,6144]{1,0:T(8,128)(2,1)S(1)}, u32[]{:S(2)}, u32[]{:S(2)}) %collective-permute-start.2) | collective-permute-done | bytes 393248 | tf_op jit(solution)/shard_map/ppermute | solution.py:70
  20.6 2.1 %collective-permute-start.4 = (bf16[32,6144]{1,0:T(8,128)(2,1)S(1)}, bf16[32,6144]{1,0:T(8,128)(2,1)S(1)}, u32[]{:S(2)}, u32[]{:S(2)}) collective-permute-start(bf16[32,6144]{1,0:T(8,128)(2,1)S(1)} %collective-permute-done.2), channel_id=1, source_target_pairs={{0,8},{8,16},{16,24},{24,26},{26,18},{18,10},{10,2},{2,0},{9,1},{1... | collective-permute-start | bytes 1179656 | tf_op jit(solution)/shard_map/ppermute | solution.py:70
  22.8 2.0 collective-permute-done.10
  24.8 2.1 %collective-permute-start.11 = (bf16[32,6144]{1,0:T(8,128)(2,1)S(1)}, bf16[32,6144]{1,0:T(8,128)(2,1)S(1)}, u32[]{:S(2)}, u32[]{:S(2)}) collective-permute-start(bf16[32,6144]{1,0:T(8,128)(2,1)S(1)} %collective-permute-done.10), channel_id=1, source_target_pairs={{0,8},{8,16},{16,24},{24,26},{26,18},{18,10},{10,2},{2,0},{9,1},{1... | collective-permute-start | bytes 1179656 | tf_op jit(solution)/shard_map/ppermute | solution.py:70
  26.9 2.1 %collective-permute-done.4 = bf16[32,6144]{1,0:T(8,128)(2,1)S(1)} collective-permute-done((bf16[32,6144]{1,0:T(8,128)(2,1)S(1)}, bf16[32,6144]{1,0:T(8,128)(2,1)S(1)}, u32[]{:S(2)}, u32[]{:S(2)}) %collective-permute-start.4) | collective-permute-done | bytes 393248 | tf_op jit(solution)/shard_map/ppermute | solution.py:70
  29.1 2.1 %collective-permute-start.5 = (bf16[16,6144]{1,0:T(8,128)(2,1)S(1)}, bf16[16,6144]{1,0:T(8,128)(2,1)S(1)}, u32[]{:S(2)}, u32[]{:S(2)}) collective-permute-start(bf16[16,6144]{1,0:T(8,128)(2,1)S(1)} %slice.153), channel_id=1, source_target_pairs={{0,8},{8,16},{16,24},{24,26},{26,18},{18,10},{10,2},{2,0},{9,1},{1... | collective-permute-start | bytes 589832 | tf_op jit(solution)/shard_map/ppermute | solution.py:70
  31.3 1.9 collective-permute-done.11
  33.3 2.1 %collective-permute-start.15 = (bf16[16,6144]{1,0:T(8,128)(2,1)S(1)}, bf16[16,6144]{1,0:T(8,128)(2,1)S(1)}, u32[]{:S(2)}, u32[]{:S(2)}) collective-permute-start(bf16[16,6144]{1,0:T(8,128)(2,1)S(1)} %slice.157), channel_id=1, source_target_pairs={{0,8},{8,16},{16,24},{24,26},{26,18},{18,10},{10,2},{2,0},{9,1},{1... | collective-permute-start | bytes 589832 | tf_op jit(solution)/shard_map/ppermute | solution.py:70
  35.5 3.5 %collective-permute-done.15 = bf16[16,6144]{1,0:T(8,128)(2,1)S(1)} collective-permute-done((bf16[16,6144]{1,0:T(8,128)(2,1)S(1)}, bf16[16,6144]{1,0:T(8,128)(2,1)S(1)}, u32[]{:S(2)}, u32[]{:S(2)}) %collective-permute-start.15) | collective-permute-done | bytes 196640 | tf_op jit(solution)/shard_map/ppermute | solution.py:70
  39.4 2.1 %collective-permute-start.7 = (bf16[32,6144]{1,0:T(8,128)(2,1)S(1)}, bf16[32,6144]{1,0:T(8,128)(2,1)S(1)}, u32[]{:S(2)}, u32[]{:S(2)}) collective-permute-start(bf16[32,6144]{1,0:T(8,128)(2,1)S(1)} %get-tuple-element.66), channel_id=1, source_target_pairs={{0,8},{8,16},{16,24},{24,26},{26,18},{18,10},{10,2},{2,0},{9,1},{1... | collective-permute-start | bytes 1179656 | tf_op jit(solution)/shard_map/ppermute | solution.py:70
  41.7 1.7 collective-permute-start.12
  43.5 9.0 %fusion.35 = f32[256,1536]{1,0:T(8,128)S(1)} fusion(bf16[256,6144]{1,0:T(8,128)(2,1)S(1)} %constant_dynamic-update-slice_fusion.refs_0_, bf16[6144,1536]{1,0:T(8,128)(2,1)} %w_ref.3), kind=kOutput, calls=%fused_computation.106 | convolution fusion | flops 4831838208 | bytes 23592960 | tf_op jit(solution)/shard_map/dot_general | solution.py:166
  52.6 1.6 collective-permute-start.17
  54.2 1.6 collective-permute-start.18
  55.9 1.6 collective-permute-start.13
  57.5 2.9 %collective-permute-done.17 = bf16[32,6144]{1,0:T(8,128)(2,1)S(1)} collective-permute-done((bf16[32,6144]{1,0:T(8,128)(2,1)S(1)}, bf16[32,6144]{1,0:T(8,128)(2,1)S(1)}, u32[]{:S(2)}, u32[]{:S(2)}) %collective-permute-start.17) | collective-permute-done | bytes 393248 | tf_op jit(solution)/shard_map/ppermute | solution.py:70
  60.5 1.6 collective-permute-start.19
  62.2 6.3 %fusion.2 = f32[256,768]{1,0:T(8,128)S(1)} fusion(bf16[256,6144]{1,0:T(8,128)(2,1)S(1)} %constant_dynamic-update-slice_fusion.8.refs_2_, bf16[1536,6144]{1,0:T(8,128)(2,1)} %param.9), kind=kOutput, calls=%fused_computation.2 | convolution fusion | flops 2415919104 | bytes 13369344 | tf_op jit(solution)/shard_map/dot_general | solution.py:25
  68.9 1.6 collective-permute-start.20
  70.6 1.6 collective-permute-start.21
  72.2 1.5 collective-permute-start.24
  73.7 6.3 %fusion = f32[256,768]{1,0:T(8,128)S(1)} fusion(bf16[256,6144]{1,0:T(8,128)(2,1)S(1)} %constant_dynamic-update-slice_fusion.8.refs_2_, bf16[1536,6144]{1,0:T(8,128)(2,1)} %param.9), kind=kOutput, calls=%fused_computation | convolution fusion | flops 2415919104 | bytes 13369344 | tf_op jit(solution)/shard_map/dot_general | solution.py:25
  80.1 1.8 collective-permute-start.27
  82.7 3.4 %collective-permute-done.27 = bf16[16,6144]{1,0:T(8,128)(2,1)S(1)} collective-permute-done((bf16[16,6144]{1,0:T(8,128)(2,1)S(1)}, bf16[16,6144]{1,0:T(8,128)(2,1)S(1)}, u32[]{:S(2)}, u32[]{:S(2)}) %collective-permute-start.27) | collective-permute-done | bytes 196640 | tf_op jit(solution)/shard_map/ppermute | solution.py:70
  88.3 9.0 %fusion.36 = f32[256,1536]{1,0:T(8,128)S(1)} fusion(bf16[256,6144]{1,0:T(8,128)(2,1)S(1)} %constant_dynamic-update-slice_fusion.16.refs_1_, bf16[6144,1536]{1,0:T(8,128)(2,1)} %w_ref.3), kind=kOutput, calls=%fused_computation.107 | convolution fusion | flops 4831838208 | bytes 23592960 | tf_op jit(solution)/shard_map/dot_general | solution.py:166
  97.3 2.6 %convert_reduce_fusion.1 = (f32[1536]{0:T(1024)S(1)}, bf16[256,1536]{1,0:T(8,128)(2,1)}, bf16[256,1536]{1,0:T(8,128)(2,1)}) fusion(f32[1536]{0:T(1024)S(1)} %copy-done.9, f32[256,1536]{1,0:T(8,128)S(1)} %fusion.35, bf16[256,1536]{1,0:T(8,128)(2,1)S(1)} %collective-permute-done.13, bf16[256,768]{1,0:T(8,128)(2,1)S(1)} %collective-permute-done.25, ...), kind=kLoop, calls=%fused_computation.27 | loop fusion | flops 12581376 | bytes 6303744 | tf_op jit(solution)/shard_map/reduce_sum | solution.py:176
  101.6 10.1 %fusion.37 = f32[256,1536]{1,0:T(8,128)} fusion(bf16[256,6144]{1,0:T(8,128)(2,1)S(1)} %constant_dynamic-update-slice_fusion.24.refs_3_, bf16[1536,6144]{1,0:T(8,128)(2,1)} %param.9), kind=kOutput, calls=%fused_computation.108 | convolution fusion | flops 4831838208 | bytes 23592960 | tf_op jit(solution)/shard_map/dot_general | solution.py:25
  116.5 10.4 %shard_map.84 = (f32[128,6144]{1,0:T(8,128)S(1)}, bf16[128,6144]{1,0:T(8,128)(2,1)S(1)}) custom-call(bf16[256,1536]{1,0:T(8,128)(2,1)S(1)} %copy-done, bf16[6144,1536]{1,0:T(8,128)(2,1)} %w_ref.3), custom_call_target="tpu_custom_call" | custom-call | flops 4831838208 | bytes 24379392 | tf_op jit(solution)/shard_map/pallas_call | solution.py:126
  128.8 1.5 collective-permute-start.34
  132.0 1.6 collective-permute-start.33
  133.6 5.4 %shard_map.85.refs_4_ = bf16[1536,6144]{1,0:T(8,128)(2,1)} custom-call(bf16[256,1536]{1,0:T(8,128)(2,1)S(1)} %copy-done.2, bf16[256,1536]{1,0:T(8,128)(2,1)S(1)} %get-tuple-element.115.refs_1_, bf16[256,6144]{1,0:T(8,128)(2,1)S(1)} %constant_dynamic-update-slice_fusion.8.refs_2_, bf16[256,6144]{1,0:T(8,128)(2,1)S(1)} %constant_dynamic-update-slice_fusion.24.refs_3_), custom_call_target="tpu_custom_call" | custom-call | flops 3221225472 | bytes 13107200 | tf_op jit(solution)/shard_map/pallas_call | solution.py:96
  140.5 1.4 collective-permute-start.36
  141.9 5.4 %shard_map.86.refs_4_ = bf16[1536,6144]{1,0:T(8,128)(2,1)} custom-call(bf16[256,1536]{1,0:T(8,128)(2,1)S(1)} %copy-done.2, bf16[256,1536]{1,0:T(8,128)(2,1)S(1)} %get-tuple-element.115.refs_1_, bf16[256,6144]{1,0:T(8,128)(2,1)S(1)} %constant_dynamic-update-slice_fusion.8.refs_2_, ...), custom_call_target="tpu_custom_call", output_to_operand_aliasing={{}: (4, {})} | custom-call | flops 3221225472 | bytes 13107200 | tf_op jit(solution)/shard_map/pallas_call | solution.py:96
  150.8 10.3 %shard_map.87 = (f32[128,6144]{1,0:T(8,128)S(1)}, bf16[128,6144]{1,0:T(8,128)(2,1)S(1)}) custom-call(bf16[256,1536]{1,0:T(8,128)(2,1)S(1)} %get-tuple-element.129.pg_ref.refs_3_, bf16[6144,1536]{1,0:T(8,128)(2,1)} %w_ref.3), custom_call_target="tpu_custom_call" | custom-call | flops 4831838208 | bytes 24379392 | tf_op jit(solution)/shard_map/pallas_call | solution.py:126
  162.2 5.4 %shard_map.88 = bf16[1536,6144]{1,0:T(8,128)(2,1)} custom-call(bf16[256,1536]{1,0:T(8,128)(2,1)S(1)} %copy-done.2, bf16[256,1536]{1,0:T(8,128)(2,1)S(1)} %get-tuple-element.115.refs_1_, bf16[256,6144]{1,0:T(8,128)(2,1)S(1)} %constant_dynamic-update-slice_fusion.8.refs_2_, ...), custom_call_target="tpu_custom_call", output_to_operand_aliasing={{}: (4, {})} | custom-call | flops 3221225472 | bytes 13107200 | tf_op jit(solution)/shard_map/pallas_call | solution.py:96
  168.1 1.6 collective-permute-start.41
  169.7 5.5 %shard_map.89.refs_4_ = bf16[6144,1536]{1,0:T(8,128)(2,1)} custom-call(bf16[256,6144]{1,0:T(8,128)(2,1)S(1)} %constant_dynamic-update-slice_fusion.refs_0_, bf16[256,6144]{1,0:T(8,128)(2,1)S(1)} %constant_dynamic-update-slice_fusion.16.refs_1_, bf16[256,1536]{1,0:T(8,128)(2,1)S(1)} %copy-done.1, bf16[256,1536]{1,0:T(8,128)(2,1)S(1)} %get-tuple-element.129.pg_ref.refs_3_), custom_call_target="tpu_custom_call" | custom-call | flops 3221225472 | bytes 9961472 | tf_op jit(solution)/shard_map/pallas_call | solution.py:96
  176.7 5.5 %shard_map.90.refs_4_ = bf16[6144,1536]{1,0:T(8,128)(2,1)} custom-call(bf16[256,6144]{1,0:T(8,128)(2,1)S(1)} %constant_dynamic-update-slice_fusion.refs_0_, bf16[256,6144]{1,0:T(8,128)(2,1)S(1)} %constant_dynamic-update-slice_fusion.16.refs_1_, bf16[256,1536]{1,0:T(8,128)(2,1)S(1)} %copy-done.1, ...), custom_call_target="tpu_custom_call", output_to_operand_aliasing={{}: (4, {})} | custom-call | flops 3221225472 | bytes 9961472 | tf_op jit(solution)/shard_map/pallas_call | solution.py:96
  184.6 1.5 collective-permute-start.38
  186.1 5.5 %shard_map.91 = bf16[6144,1536]{1,0:T(8,128)(2,1)} custom-call(bf16[256,6144]{1,0:T(8,128)(2,1)S(1)} %constant_dynamic-update-slice_fusion.refs_0_, bf16[256,6144]{1,0:T(8,128)(2,1)S(1)} %constant_dynamic-update-slice_fusion.16.refs_1_, bf16[256,1536]{1,0:T(8,128)(2,1)S(1)} %copy-done.1, ...), custom_call_target="tpu_custom_call", output_to_operand_aliasing={{}: (4, {})} | custom-call | flops 3221225472 | bytes 9961472 | tf_op jit(solution)/shard_map/pallas_call | solution.py:96
  192.7 2.6 %collective-permute-done.38 = bf16[32,6144]{1,0:T(8,128)(2,1)S(1)} collective-permute-done((bf16[32,6144]{1,0:T(8,128)(2,1)S(1)}, bf16[32,6144]{1,0:T(8,128)(2,1)S(1)}, u32[]{:S(2)}, u32[]{:S(2)}) %collective-permute-start.38) | collective-permute-done | bytes 393248 | tf_op jit(solution)/shard_map/ppermute | solution.py:70
  196.0 3.5 %collective-permute-done.44 = bf16[32,6144]{1,0:T(8,128)(2,1)S(1)} collective-permute-done((bf16[32,6144]{1,0:T(8,128)(2,1)S(1)}, bf16[32,6144]{1,0:T(8,128)(2,1)S(1)}, u32[]{:S(2)}, u32[]{:S(2)}) %collective-permute-start.44) | collective-permute-done | bytes 393248 | tf_op jit(solution)/shard_map/ppermute | solution.py:70
  (150 shorter events, 31.9 us)
Async XLA Ops:
  0.6 2.8 %collective-permute-start = (bf16[32,6144]{1,0:T(8,128)(2,1)}, bf16[32,6144]{1,0:T(8,128)(2,1)S(1)}, u32[]{:S(2)}, u32[]{:S(2)}) collective-permute-start(bf16[32,6144]{1,0:T(8,128)(2,1)} %param.5), channel_id=1, source_target_pairs={{0,1},{1,0},{2,3},{3,2},{4,5},{5,4},{6,7},{7,6},{8,9},{9,8},{10,11... | collective-permute-start | bytes 1179656 | tf_op jit(solution)/shard_map/ppermute | solution.py:73
  1.1 5.4 %collective-permute-start.8 = (bf16[32,6144]{1,0:T(8,128)(2,1)}, bf16[32,6144]{1,0:T(8,128)(2,1)S(1)}, u32[]{:S(2)}, u32[]{:S(2)}) collective-permute-start(bf16[32,6144]{1,0:T(8,128)(2,1)} %param.6), channel_id=1, source_target_pairs={{0,1},{1,0},{2,3},{3,2},{4,5},{5,4},{6,7},{7,6},{8,9},{9,8},{10,11... | collective-permute-start | bytes 1179656 | tf_op jit(solution)/shard_map/ppermute | solution.py:73
  3.5 8.8 %collective-permute-start.1 = (bf16[32,6144]{1,0:T(8,128)(2,1)S(1)}, bf16[32,6144]{1,0:T(8,128)(2,1)S(1)}, u32[]{:S(2)}, u32[]{:S(2)}) collective-permute-start(bf16[32,6144]{1,0:T(8,128)(2,1)S(1)} %pad_maximum_fusion.9), channel_id=1, source_target_pairs={{0,8},{8,16},{16,24},{24,26},{26,18},{18,10},{10,2},{2,0},{9,1},{1... | collective-permute-start | bytes 1179656 | tf_op jit(solution)/shard_map/ppermute | solution.py:70
  6.6 9.9 %collective-permute-start.9 = (bf16[32,6144]{1,0:T(8,128)(2,1)S(1)}, bf16[32,6144]{1,0:T(8,128)(2,1)S(1)}, u32[]{:S(2)}, u32[]{:S(2)}) collective-permute-start(bf16[32,6144]{1,0:T(8,128)(2,1)S(1)} %pad_maximum_fusion.12), channel_id=1, source_target_pairs={{0,8},{8,16},{16,24},{24,26},{26,18},{18,10},{10,2},{2,0},{9,1},{1... | collective-permute-start | bytes 1179656 | tf_op jit(solution)/shard_map/ppermute | solution.py:70
  12.2 8.4 %collective-permute-start.2 = (bf16[32,6144]{1,0:T(8,128)(2,1)S(1)}, bf16[32,6144]{1,0:T(8,128)(2,1)S(1)}, u32[]{:S(2)}, u32[]{:S(2)}) collective-permute-start(bf16[32,6144]{1,0:T(8,128)(2,1)S(1)} %collective-permute-done.1), channel_id=1, source_target_pairs={{0,8},{8,16},{16,24},{24,26},{26,18},{18,10},{10,2},{2,0},{9,1},{1... | collective-permute-start | bytes 1179656 | tf_op jit(solution)/shard_map/ppermute | solution.py:70
  16.4 8.4 %collective-permute-start.10 = (bf16[32,6144]{1,0:T(8,128)(2,1)S(1)}, bf16[32,6144]{1,0:T(8,128)(2,1)S(1)}, u32[]{:S(2)}, u32[]{:S(2)}) collective-permute-start(bf16[32,6144]{1,0:T(8,128)(2,1)S(1)} %collective-permute-done.9), channel_id=1, source_target_pairs={{0,8},{8,16},{16,24},{24,26},{26,18},{18,10},{10,2},{2,0},{9,1},{1... | collective-permute-start | bytes 1179656 | tf_op jit(solution)/shard_map/ppermute | solution.py:70
  20.6 8.4 %collective-permute-start.4 = (bf16[32,6144]{1,0:T(8,128)(2,1)S(1)}, bf16[32,6144]{1,0:T(8,128)(2,1)S(1)}, u32[]{:S(2)}, u32[]{:S(2)}) collective-permute-start(bf16[32,6144]{1,0:T(8,128)(2,1)S(1)} %collective-permute-done.2), channel_id=1, source_target_pairs={{0,8},{8,16},{16,24},{24,26},{26,18},{18,10},{10,2},{2,0},{9,1},{1... | collective-permute-start | bytes 1179656 | tf_op jit(solution)/shard_map/ppermute | solution.py:70
  22.8 16.4 %collective-permute-start.3 = (bf16[64,6144]{1,0:T(8,128)(2,1)S(1)}, bf16[64,6144]{1,0:T(8,128)(2,1)S(1)}, u32[]{:S(2)}, u32[]{:S(2)}) collective-permute-start(bf16[64,6144]{1,0:T(8,128)(2,1)S(1)} %pad_maximum_fusion), channel_id=1, source_target_pairs={{0,1},{1,0},{2,3},{3,2},{4,5},{5,4},{6,7},{7,6},{8,9},{9,8},{10,11... | collective-permute-start | bytes 2359304 | tf_op jit(solution)/shard_map/ppermute | solution.py:73
  24.8 8.4 %collective-permute-start.11 = (bf16[32,6144]{1,0:T(8,128)(2,1)S(1)}, bf16[32,6144]{1,0:T(8,128)(2,1)S(1)}, u32[]{:S(2)}, u32[]{:S(2)}) collective-permute-start(bf16[32,6144]{1,0:T(8,128)(2,1)S(1)} %collective-permute-done.10), channel_id=1, source_target_pairs={{0,8},{8,16},{16,24},{24,26},{26,18},{18,10},{10,2},{2,0},{9,1},{1... | collective-permute-start | bytes 1179656 | tf_op jit(solution)/shard_map/ppermute | solution.py:70
  29.1 6.3 %collective-permute-start.5 = (bf16[16,6144]{1,0:T(8,128)(2,1)S(1)}, bf16[16,6144]{1,0:T(8,128)(2,1)S(1)}, u32[]{:S(2)}, u32[]{:S(2)}) collective-permute-start(bf16[16,6144]{1,0:T(8,128)(2,1)S(1)} %slice.153), channel_id=1, source_target_pairs={{0,8},{8,16},{16,24},{24,26},{26,18},{18,10},{10,2},{2,0},{9,1},{1... | collective-permute-start | bytes 589832 | tf_op jit(solution)/shard_map/ppermute | solution.py:70
  31.3 7.9 %collective-permute-start.14 = (bf16[64,6144]{1,0:T(8,128)(2,1)S(1)}, bf16[64,6144]{1,0:T(8,128)(2,1)S(1)}, u32[]{:S(2)}, u32[]{:S(2)}) collective-permute-start(bf16[64,6144]{1,0:T(8,128)(2,1)S(1)} %pad_maximum_fusion.1), channel_id=1, source_target_pairs={{0,1},{1,0},{2,3},{3,2},{4,5},{5,4},{6,7},{7,6},{8,9},{9,8},{10,11... | collective-permute-start | bytes 2359304 | tf_op jit(solution)/shard_map/ppermute | solution.py:73
  33.3 5.7 %collective-permute-start.15 = (bf16[16,6144]{1,0:T(8,128)(2,1)S(1)}, bf16[16,6144]{1,0:T(8,128)(2,1)S(1)}, u32[]{:S(2)}, u32[]{:S(2)}) collective-permute-start(bf16[16,6144]{1,0:T(8,128)(2,1)S(1)} %slice.157), channel_id=1, source_target_pairs={{0,8},{8,16},{16,24},{24,26},{26,18},{18,10},{10,2},{2,0},{9,1},{1... | collective-permute-start | bytes 589832 | tf_op jit(solution)/shard_map/ppermute | solution.py:70
  35.5 3.8 %collective-permute-start.6 = (bf16[48,6144]{1,0:T(8,128)(2,1)S(1)}, bf16[48,6144]{1,0:T(8,128)(2,1)S(1)}, u32[]{:S(2)}, u32[]{:S(2)}) collective-permute-start(bf16[48,6144]{1,0:T(8,128)(2,1)S(1)} %pad_maximum_fusion.5), channel_id=1, source_target_pairs={{0,1},{1,0},{2,3},{3,2},{4,5},{5,4},{6,7},{7,6},{8,9},{9,8},{10,11... | collective-permute-start | bytes 1769480 | tf_op jit(solution)/shard_map/ppermute | solution.py:73
  39.1 2.5 %collective-permute-start.16 = (bf16[48,6144]{1,0:T(8,128)(2,1)S(1)}, bf16[48,6144]{1,0:T(8,128)(2,1)S(1)}, u32[]{:S(2)}, u32[]{:S(2)}) collective-permute-start(bf16[48,6144]{1,0:T(8,128)(2,1)S(1)} %pad_maximum_fusion.6), channel_id=1, source_target_pairs={{0,1},{1,0},{2,3},{3,2},{4,5},{5,4},{6,7},{7,6},{8,9},{9,8},{10,11... | collective-permute-start | bytes 1769480 | tf_op jit(solution)/shard_map/ppermute | solution.py:73
  39.4 13.1 %collective-permute-start.7 = (bf16[32,6144]{1,0:T(8,128)(2,1)S(1)}, bf16[32,6144]{1,0:T(8,128)(2,1)S(1)}, u32[]{:S(2)}, u32[]{:S(2)}) collective-permute-start(bf16[32,6144]{1,0:T(8,128)(2,1)S(1)} %get-tuple-element.66), channel_id=1, source_target_pairs={{0,8},{8,16},{16,24},{24,26},{26,18},{18,10},{10,2},{2,0},{9,1},{1... | collective-permute-start | bytes 1179656 | tf_op jit(solution)/shard_map/ppermute | solution.py:70
  41.7 10.9 %collective-permute-start.12 = (bf16[32,6144]{1,0:T(8,128)(2,1)S(1)}, bf16[32,6144]{1,0:T(8,128)(2,1)S(1)}, u32[]{:S(2)}, u32[]{:S(2)}) collective-permute-start(bf16[32,6144]{1,0:T(8,128)(2,1)S(1)} %get-tuple-element.67), channel_id=1, source_target_pairs={{0,8},{8,16},{16,24},{24,26},{26,18},{18,10},{10,2},{2,0},{9,1},{1... | collective-permute-start | bytes 1179656 | tf_op jit(solution)/shard_map/ppermute | solution.py:70
  52.6 7.8 %collective-permute-start.17 = (bf16[32,6144]{1,0:T(8,128)(2,1)S(1)}, bf16[32,6144]{1,0:T(8,128)(2,1)S(1)}, u32[]{:S(2)}, u32[]{:S(2)}) collective-permute-start(bf16[32,6144]{1,0:T(8,128)(2,1)S(1)} %collective-permute-done.7), channel_id=1, source_target_pairs={{0,8},{8,16},{16,24},{24,26},{26,18},{18,10},{10,2},{2,0},{9,1},{1... | collective-permute-start | bytes 1179656 | tf_op jit(solution)/shard_map/ppermute | solution.py:70
  54.2 14.3 %collective-permute-start.18 = (bf16[32,6144]{1,0:T(8,128)(2,1)S(1)}, bf16[32,6144]{1,0:T(8,128)(2,1)S(1)}, u32[]{:S(2)}, u32[]{:S(2)}) collective-permute-start(bf16[32,6144]{1,0:T(8,128)(2,1)S(1)} %collective-permute-done.12), channel_id=1, source_target_pairs={{0,8},{8,16},{16,24},{24,26},{26,18},{18,10},{10,2},{2,0},{9,1},{1... | collective-permute-start | bytes 1179656 | tf_op jit(solution)/shard_map/ppermute | solution.py:70
  55.9 41.3 %collective-permute-start.13 = (bf16[256,1536]{1,0:T(8,128)(2,1)S(1)}, bf16[256,1536]{1,0:T(8,128)(2,1)S(1)}, u32[]{:S(2)}, u32[]{:S(2)}) collective-permute-start(bf16[256,1536]{1,0:T(8,128)(2,1)S(1)} %convert_element_type.114), channel_id=1, source_target_pairs={{0,4},{4,0},{1,5},{5,1},{2,6},{6,2},{3,7},{7,3},{8,12},{12,8},{9,1... | collective-permute-start | bytes 2359304 | tf_op jit(solution)/shard_map/ppermute | solution.py:76
  60.5 21.5 %collective-permute-start.22 = (bf16[64,6144]{1,0:T(8,128)(2,1)S(1)}, bf16[64,6144]{1,0:T(8,128)(2,1)S(1)}, u32[]{:S(2)}, u32[]{:S(2)}) collective-permute-start(bf16[64,6144]{1,0:T(8,128)(2,1)S(1)} %pad_maximum_fusion.2), channel_id=1, source_target_pairs={{0,1},{1,0},{2,3},{3,2},{4,5},{5,4},{6,7},{7,6},{8,9},{9,8},{10,11... | collective-permute-start | bytes 2359304 | tf_op jit(solution)/shard_map/ppermute | solution.py:73
  60.5 8.3 %collective-permute-start.19 = (bf16[32,6144]{1,0:T(8,128)(2,1)S(1)}, bf16[32,6144]{1,0:T(8,128)(2,1)S(1)}, u32[]{:S(2)}, u32[]{:S(2)}) collective-permute-start(bf16[32,6144]{1,0:T(8,128)(2,1)S(1)} %collective-permute-done.17), channel_id=1, source_target_pairs={{0,8},{8,16},{16,24},{24,26},{26,18},{18,10},{10,2},{2,0},{9,1},{1... | collective-permute-start | bytes 1179656 | tf_op jit(solution)/shard_map/ppermute | solution.py:70
  68.9 11.2 %collective-permute-start.20 = (bf16[32,6144]{1,0:T(8,128)(2,1)S(1)}, bf16[32,6144]{1,0:T(8,128)(2,1)S(1)}, u32[]{:S(2)}, u32[]{:S(2)}) collective-permute-start(bf16[32,6144]{1,0:T(8,128)(2,1)S(1)} %collective-permute-done.18), channel_id=1, source_target_pairs={{0,8},{8,16},{16,24},{24,26},{26,18},{18,10},{10,2},{2,0},{9,1},{1... | collective-permute-start | bytes 1179656 | tf_op jit(solution)/shard_map/ppermute | solution.py:70
  70.6 9.4 %collective-permute-start.21 = (bf16[16,6144]{1,0:T(8,128)(2,1)S(1)}, bf16[16,6144]{1,0:T(8,128)(2,1)S(1)}, u32[]{:S(2)}, u32[]{:S(2)}) collective-permute-start(bf16[16,6144]{1,0:T(8,128)(2,1)S(1)} %slice.129), channel_id=1, source_target_pairs={{0,8},{8,16},{16,24},{24,26},{26,18},{18,10},{10,2},{2,0},{9,1},{1... | collective-permute-start | bytes 589832 | tf_op jit(solution)/shard_map/ppermute | solution.py:70
  72.2 25.1 %collective-permute-start.24 = (bf16[256,768]{1,0:T(8,128)(2,1)S(1)}, bf16[256,768]{1,0:T(8,128)(2,1)S(1)}, u32[]{:S(2)}, u32[]{:S(2)}) collective-permute-start(bf16[256,768]{1,0:T(8,128)(2,1)S(1)} %convert_element_type.117), channel_id=1, source_target_pairs={{0,4},{4,0},{1,5},{5,1},{2,6},{6,2},{3,7},{7,3},{8,12},{12,8},{9,1... | collective-permute-start | bytes 1179656 | tf_op jit(solution)/shard_map/ppermute | solution.py:76
  80.0 6.1 %collective-permute-start.26 = (bf16[64,6144]{1,0:T(8,128)(2,1)S(1)}, bf16[64,6144]{1,0:T(8,128)(2,1)S(1)}, u32[]{:S(2)}, u32[]{:S(2)}) collective-permute-start(bf16[64,6144]{1,0:T(8,128)(2,1)S(1)} %pad_maximum_fusion.3), channel_id=1, source_target_pairs={{0,1},{1,0},{2,3},{3,2},{4,5},{5,4},{6,7},{7,6},{8,9},{9,8},{10,11... | collective-permute-start | bytes 2359304 | tf_op jit(solution)/shard_map/ppermute | solution.py:73
  80.1 5.9 %collective-permute-start.27 = (bf16[16,6144]{1,0:T(8,128)(2,1)S(1)}, bf16[16,6144]{1,0:T(8,128)(2,1)S(1)}, u32[]{:S(2)}, u32[]{:S(2)}) collective-permute-start(bf16[16,6144]{1,0:T(8,128)(2,1)S(1)} %slice.130), channel_id=1, source_target_pairs={{0,8},{8,16},{16,24},{24,26},{26,18},{18,10},{10,2},{2,0},{9,1},{1... | collective-permute-start | bytes 589832 | tf_op jit(solution)/shard_map/ppermute | solution.py:70
  82.0 15.3 %collective-permute-start.25 = (bf16[256,768]{1,0:T(8,128)(2,1)S(1)}, bf16[256,768]{1,0:T(8,128)(2,1)S(1)}, u32[]{:S(2)}, u32[]{:S(2)}) collective-permute-start(bf16[256,768]{1,0:T(8,128)(2,1)S(1)} %convert_element_type.118), channel_id=1, source_target_pairs={{0,4},{4,0},{1,5},{5,1},{2,6},{6,2},{3,7},{7,3},{8,12},{12,8},{9,1... | collective-permute-start | bytes 1179656 | tf_op jit(solution)/shard_map/ppermute | solution.py:76
  86.0 2.0 collective-permute-start.23
  86.1 15.3 %collective-permute-start.28 = (bf16[48,6144]{1,0:T(8,128)(2,1)S(1)}, bf16[48,6144]{1,0:T(8,128)(2,1)S(1)}, u32[]{:S(2)}, u32[]{:S(2)}) collective-permute-start(bf16[48,6144]{1,0:T(8,128)(2,1)S(1)} %pad_maximum_fusion.8), channel_id=1, source_target_pairs={{0,1},{1,0},{2,3},{3,2},{4,5},{5,4},{6,7},{7,6},{8,9},{9,8},{10,11... | collective-permute-start | bytes 1769480 | tf_op jit(solution)/shard_map/ppermute | solution.py:73
  100.9 11.4 %collective-permute-start.29 = (bf16[128,1536]{1,0:T(8,128)(2,1)}, bf16[128,1536]{1,0:T(8,128)(2,1)S(1)}, u32[]{:S(2)}, u32[]{:S(2)}) collective-permute-start(bf16[128,1536]{1,0:T(8,128)(2,1)} %get-tuple-element.146), channel_id=1, source_target_pairs={{0,4},{4,0},{1,5},{5,1},{2,6},{6,2},{3,7},{7,3},{8,12},{12,8},{9,1... | collective-permute-start | bytes 1179656 | tf_op jit(solution)/shard_map/ppermute | solution.py:76
  113.3 13.7 %collective-permute-start.31 = (bf16[64,1536]{1,0:T(8,128)(2,1)S(1)}, bf16[64,1536]{1,0:T(8,128)(2,1)S(1)}, u32[]{:S(2)}, u32[]{:S(2)}) collective-permute-start(bf16[64,1536]{1,0:T(8,128)(2,1)S(1)} %slice.221), channel_id=1, source_target_pairs={{0,4},{4,0},{1,5},{5,1},{2,6},{6,2},{3,7},{7,3},{8,12},{12,8},{9,1... | collective-permute-start | bytes 589832 | tf_op jit(solution)/shard_map/ppermute | solution.py:76
  114.3 13.6 %collective-permute-start.30 = (bf16[128,1536]{1,0:T(8,128)(2,1)}, bf16[128,1536]{1,0:T(8,128)(2,1)S(1)}, u32[]{:S(2)}, u32[]{:S(2)}) collective-permute-start(bf16[128,1536]{1,0:T(8,128)(2,1)} %get-tuple-element.87), channel_id=1, source_target_pairs={{0,4},{4,0},{1,5},{5,1},{2,6},{6,2},{3,7},{7,3},{8,12},{12,8},{9,1... | collective-permute-start | bytes 1179656 | tf_op jit(solution)/shard_map/ppermute | solution.py:76
  116.5 11.4 %copy-start.3 = (f32[256,1536]{1,0:T(8,128)S(1)}, f32[256,1536]{1,0:T(8,128)}, u32[]{:S(2)}) copy-start(f32[256,1536]{1,0:T(8,128)} %fusion.37) | copy-start | bytes 4718596
  116.5 13.8 %copy-start.5 = (f32[256,1536]{1,0:T(8,128)S(1)}, f32[256,1536]{1,0:T(8,128)}, u32[]{:S(2)}) copy-start(f32[256,1536]{1,0:T(8,128)} %copy-done.4) | copy-start | bytes 4718596
  127.9 3.5 %collective-permute-start.32 = (bf16[128,6144]{1,0:T(8,128)(2,1)S(1)}, bf16[128,6144]{1,0:T(8,128)(2,1)S(1)}, u32[]{:S(2)}, u32[]{:S(2)}) collective-permute-start(bf16[128,6144]{1,0:T(8,128)(2,1)S(1)} %get-tuple-element.89), channel_id=1, source_target_pairs={{0,1},{1,0},{2,3},{3,2},{4,5},{5,4},{6,7},{7,6},{8,9},{9,8},{10,11... | collective-permute-start | bytes 4718600 | tf_op jit(solution)/shard_map/ppermute | solution.py:73
  128.8 10.2 %collective-permute-start.34 = (bf16[96,1536]{1,0:T(8,128)(2,1)}, bf16[96,1536]{1,0:T(8,128)(2,1)}, u32[]{:S(2)}, u32[]{:S(2)}) collective-permute-start(bf16[96,1536]{1,0:T(8,128)(2,1)} %get-tuple-element.96), channel_id=1, source_target_pairs={{0,4},{4,0},{1,5},{5,1},{2,6},{6,2},{3,7},{7,3},{8,12},{12,8},{9,1... | collective-permute-start | bytes 884744 | tf_op jit(solution)/shard_map/ppermute | solution.py:76
  132.0 7.0 %collective-permute-start.33 = (bf16[16,6144]{1,0:T(8,128)(2,1)S(1)}, bf16[16,6144]{1,0:T(8,128)(2,1)S(1)}, u32[]{:S(2)}, u32[]{:S(2)}) collective-permute-start(bf16[16,6144]{1,0:T(8,128)(2,1)S(1)} %get-tuple-element.144), channel_id=1, source_target_pairs={{0,8},{8,16},{16,24},{24,26},{26,18},{18,10},{10,2},{2,0},{9,1},{1... | collective-permute-start | bytes 589832 | tf_op jit(solution)/shard_map/ppermute | solution.py:70
  139.1 9.2 %collective-permute-start.35 = (bf16[32,6144]{1,0:T(8,128)(2,1)S(1)}, bf16[32,6144]{1,0:T(8,128)(2,1)S(1)}, u32[]{:S(2)}, u32[]{:S(2)}) collective-permute-start(bf16[32,6144]{1,0:T(8,128)(2,1)S(1)} %pad_maximum_fusion.13), channel_id=1, source_target_pairs={{0,8},{8,16},{16,24},{24,26},{26,18},{18,10},{10,2},{2,0},{9,1},{1... | collective-permute-start | bytes 1179656 | tf_op jit(solution)/shard_map/ppermute | solution.py:70
  140.5 7.8 %collective-permute-start.36 = (bf16[96,1536]{1,0:T(8,128)(2,1)S(1)}, bf16[96,1536]{1,0:T(8,128)(2,1)S(1)}, u32[]{:S(2)}, u32[]{:S(2)}) collective-permute-start(bf16[96,1536]{1,0:T(8,128)(2,1)S(1)} %copy-done.6), channel_id=1, source_target_pairs={{0,4},{4,0},{1,5},{5,1},{2,6},{6,2},{3,7},{7,3},{8,12},{12,8},{9,1... | collective-permute-start | bytes 884744 | tf_op jit(solution)/shard_map/ppermute | solution.py:76
  148.4 12.8 %collective-permute-start.37 = (bf16[32,6144]{1,0:T(8,128)(2,1)S(1)}, bf16[32,6144]{1,0:T(8,128)(2,1)}, u32[]{:S(2)}, u32[]{:S(2)}) collective-permute-start(bf16[32,6144]{1,0:T(8,128)(2,1)S(1)} %fusion.18), channel_id=1, source_target_pairs={{0,8},{8,16},{16,24},{24,26},{26,18},{18,10},{10,2},{2,0},{9,1},{1... | collective-permute-start | bytes 1179656 | tf_op jit(solution)/shard_map/ppermute | solution.py:70
  161.1 6.6 %collective-permute-start.40 = (bf16[128,6144]{1,0:T(8,128)(2,1)S(1)}, bf16[128,6144]{1,0:T(8,128)(2,1)S(1)}, u32[]{:S(2)}, u32[]{:S(2)}) collective-permute-start(bf16[128,6144]{1,0:T(8,128)(2,1)S(1)} %get-tuple-element.111), channel_id=1, source_target_pairs={{0,1},{1,0},{2,3},{3,2},{4,5},{5,4},{6,7},{7,6},{8,9},{9,8},{10,11... | collective-permute-start | bytes 4718600 | tf_op jit(solution)/shard_map/ppermute | solution.py:73
  168.1 7.1 %collective-permute-start.41 = (bf16[16,6144]{1,0:T(8,128)(2,1)S(1)}, bf16[16,6144]{1,0:T(8,128)(2,1)S(1)}, u32[]{:S(2)}, u32[]{:S(2)}) collective-permute-start(bf16[16,6144]{1,0:T(8,128)(2,1)S(1)} %get-tuple-element.139), channel_id=1, source_target_pairs={{0,8},{8,16},{16,24},{24,26},{26,18},{18,10},{10,2},{2,0},{9,1},{1... | collective-permute-start | bytes 589832 | tf_op jit(solution)/shard_map/ppermute | solution.py:70
  175.3 7.8 %collective-permute-start.42 = (bf16[32,6144]{1,0:T(8,128)(2,1)S(1)}, bf16[32,6144]{1,0:T(8,128)(2,1)S(1)}, u32[]{:S(2)}, u32[]{:S(2)}) collective-permute-start(bf16[32,6144]{1,0:T(8,128)(2,1)S(1)} %pad_maximum_fusion.14), channel_id=1, source_target_pairs={{0,8},{8,16},{16,24},{24,26},{26,18},{18,10},{10,2},{2,0},{9,1},{1... | collective-permute-start | bytes 1179656 | tf_op jit(solution)/shard_map/ppermute | solution.py:70
  183.2 8.4 %collective-permute-start.43 = (bf16[32,6144]{1,0:T(8,128)(2,1)S(1)}, bf16[32,6144]{1,0:T(8,128)(2,1)S(1)}, u32[]{:S(2)}, u32[]{:S(2)}) collective-permute-start(bf16[32,6144]{1,0:T(8,128)(2,1)S(1)} %fusion.16), channel_id=1, source_target_pairs={{0,8},{8,16},{16,24},{24,26},{26,18},{18,10},{10,2},{2,0},{9,1},{1... | collective-permute-start | bytes 1179656 | tf_op jit(solution)/shard_map/ppermute | solution.py:70
  184.6 10.7 %collective-permute-start.38 = (bf16[32,6144]{1,0:T(8,128)(2,1)S(1)}, bf16[32,6144]{1,0:T(8,128)(2,1)S(1)}, u32[]{:S(2)}, u32[]{:S(2)}) collective-permute-start(bf16[32,6144]{1,0:T(8,128)(2,1)S(1)} %fusion.19), channel_id=1, source_target_pairs={{0,8},{8,16},{16,24},{24,26},{26,18},{18,10},{10,2},{2,0},{9,1},{1... | collective-permute-start | bytes 1179656 | tf_op jit(solution)/shard_map/ppermute | solution.py:70
  191.7 7.8 %collective-permute-start.44 = (bf16[32,6144]{1,0:T(8,128)(2,1)S(1)}, bf16[32,6144]{1,0:T(8,128)(2,1)S(1)}, u32[]{:S(2)}, u32[]{:S(2)}) collective-permute-start(bf16[32,6144]{1,0:T(8,128)(2,1)S(1)} %fusion.17), channel_id=1, source_target_pairs={{0,8},{8,16},{16,24},{24,26},{26,18},{18,10},{10,2},{2,0},{9,1},{1... | collective-permute-start | bytes 1179656 | tf_op jit(solution)/shard_map/ppermute | solution.py:70
  195.3 4.3 %collective-permute-start.39 = (bf16[16,6144]{1,0:T(8,128)(2,1)S(1)}, bf16[16,6144]{1,0:T(8,128)(2,1)S(1)}, u32[]{:S(2)}, u32[]{:S(2)}) collective-permute-start(bf16[16,6144]{1,0:T(8,128)(2,1)S(1)} %slice.167), channel_id=1, source_target_pairs={{0,1},{1,0},{2,3},{3,2},{4,5},{5,4},{6,7},{7,6},{8,9},{9,8},{10,11... | collective-permute-start | bytes 589832 | tf_op jit(solution)/shard_map/ppermute | solution.py:73
  199.5 1.5 collective-permute-start.45
  (8 other events, 39.5 us)

commit v5 on v4

--- a/solution.py
+++ b/solution.py
@@ -154,9 +154,10 @@
             block = block[:step]
         return links.onward(after(block, *others) if others else block)
 
-    def rows_of(got):
+    def rows_of(got, last_apart=False):
         early, late = cat(got[1 : far - 1]), cat(got[far - 1 :])
-        others = [links.sibling(early), links.sibling(late)]
+        ends = got[far - 1 :] if last_apart else [late]
+        others = [links.sibling(x) for x in [early, *ends]]
         return cat([got[0][:step], *others, got[0][step:], early, late])
 
     def other_half(own):
@@ -203,7 +204,7 @@
     s_b, g[far - 1], t[far] = pair(signals(after(grad1, s_a), halves[1]), g[far - 1], t[far])
     s_ax, s_bx = other_half(s_a), other_half(s_b)
     g.append(onward(g[-1], far))
-    tok2, grad2 = rows_of(t), rows_of(g)
+    tok2, grad2 = rows_of(t, True), rows_of(g)
     p2, s_ax = pair(project(tok2), s_ax)
     s2 = signals(after(grad2, p2))
     act1, slope1 = activate(p1, p1x)

time: 202 us -> 201 us (level)
  transfers between devices with their start and end apart: 46 -> 47, of which waited for: 18 -> 18; matrix products, arithmetic and copies ran while one was open for 27% -> 27% of each run, Pallas kernels for 26% -> 27%
where the time goes in v5:
time: 201 us; the launch traced here: 200 us
  Pallas kernels  53.4 us (27%)
  starting transfers between devices  51.6 us (26%)
  matrix products  40.7 us (20%)
  waiting for transfers between devices  36.4 us (18%)
  other arithmetic  9.62 us (5%)
  local copies, waits for them, and re-layouts  7.26 us (4%)
    ppermute x24, starting transfers between devices, onward(): return lax.ppermute(x, ROWS, self.ring)  41 us
    pallas_call x6, Pallas kernels, over_rows_tiles(): pl.pallas_call(kernel, grid=(count,), in_specs=in_specs, out_specs=pl.Blo...  32.7 us
    ppermute x24, waiting for transfers between devices, onward(): return lax.ppermute(x, ROWS, self.ring)  30 us
    dot_general x3, matrix products, times_transpose(): lax.dot_general(left, right, (((1,), (1,)), ((), ())), preferred_element_...  22.8 us
    pallas_call x2, Pallas kernels, back_rows(): pl.pallas_call(kernel, grid=(width // tile,), in_specs=[pl.BlockSpec((row...  20.7 us
    dot_general x2, matrix products, project(): return jnp.dot(rows, w_in[:, cols], preferred_element_type=f32)  18 us
    ppermute x8, starting transfers between devices, across(): return lax.ppermute(x, 'dp', [(0, 1), (1, 0)])  9.17 us
  transfers between devices with their start and end apart: 47, of which 18 were waited for; matrix products, arithmetic and copies ran while one was open for 27% of the time, Pallas kernels for 27%

profile of v5, /device:TPU:0, one launch (start us, length us, event | category | flops | bytes accessed | tf_op | source)
XLA Modules:
  0.0 200.4 jit_solution(18316876012201945629)
XLA Ops:
  3.5 3.1 %collective-permute-start.1 = (bf16[32,6144]{1,0:T(8,128)(2,1)S(1)}, bf16[32,6144]{1,0:T(8,128)(2,1)S(1)}, u32[]{:S(2)}, u32[]{:S(2)}) collective-permute-start(bf16[32,6144]{1,0:T(8,128)(2,1)S(1)} %pad_maximum_fusion.8), channel_id=1, source_target_pairs={{0,8},{8,16},{16,24},{24,26},{26,18},{18,10},{10,2},{2,0},{9,1},{1... | collective-permute-start | bytes 1179656 | tf_op jit(solution)/shard_map/ppermute | solution.py:70
  6.6 1.6 collective-permute-start.9
  8.2 4.0 %collective-permute-done.1 = bf16[32,6144]{1,0:T(8,128)(2,1)S(1)} collective-permute-done((bf16[32,6144]{1,0:T(8,128)(2,1)S(1)}, bf16[32,6144]{1,0:T(8,128)(2,1)S(1)}, u32[]{:S(2)}, u32[]{:S(2)}) %collective-permute-start.1) | collective-permute-done | bytes 393248 | tf_op jit(solution)/shard_map/ppermute | solution.py:70
  12.2 2.1 %collective-permute-start.2 = (bf16[32,6144]{1,0:T(8,128)(2,1)S(1)}, bf16[32,6144]{1,0:T(8,128)(2,1)S(1)}, u32[]{:S(2)}, u32[]{:S(2)}) collective-permute-start(bf16[32,6144]{1,0:T(8,128)(2,1)S(1)} %collective-permute-done.1), channel_id=1, source_target_pairs={{0,8},{8,16},{16,24},{24,26},{26,18},{18,10},{10,2},{2,0},{9,1},{1... | collective-permute-start | bytes 1179656 | tf_op jit(solution)/shard_map/ppermute | solution.py:70
  14.3 2.1 %collective-permute-done.9 = bf16[32,6144]{1,0:T(8,128)(2,1)S(1)} collective-permute-done((bf16[32,6144]{1,0:T(8,128)(2,1)S(1)}, bf16[32,6144]{1,0:T(8,128)(2,1)S(1)}, u32[]{:S(2)}, u32[]{:S(2)}) %collective-permute-start.9) | collective-permute-done | bytes 393248 | tf_op jit(solution)/shard_map/ppermute | solution.py:70
  16.4 2.1 %collective-permute-start.10 = (bf16[32,6144]{1,0:T(8,128)(2,1)S(1)}, bf16[32,6144]{1,0:T(8,128)(2,1)S(1)}, u32[]{:S(2)}, u32[]{:S(2)}) collective-permute-start(bf16[32,6144]{1,0:T(8,128)(2,1)S(1)} %collective-permute-done.9), channel_id=1, source_target_pairs={{0,8},{8,16},{16,24},{24,26},{26,18},{18,10},{10,2},{2,0},{9,1},{1... | collective-permute-start | bytes 1179656 | tf_op jit(solution)/shard_map/ppermute | solution.py:70
  18.5 2.1 %collective-permute-done.2 = bf16[32,6144]{1,0:T(8,128)(2,1)S(1)} collective-permute-done((bf16[32,6144]{1,0:T(8,128)(2,1)S(1)}, bf16[32,6144]{1,0:T(8,128)(2,1)S(1)}, u32[]{:S(2)}, u32[]{:S(2)}) %collective-permute-start.2) | collective-permute-done | bytes 393248 | tf_op jit(solution)/shard_map/ppermute | solution.py:70
  20.6 2.1 %collective-permute-start.4 = (bf16[32,6144]{1,0:T(8,128)(2,1)S(1)}, bf16[32,6144]{1,0:T(8,128)(2,1)S(1)}, u32[]{:S(2)}, u32[]{:S(2)}) collective-permute-start(bf16[32,6144]{1,0:T(8,128)(2,1)S(1)} %collective-permute-done.2), channel_id=1, source_target_pairs={{0,8},{8,16},{16,24},{24,26},{26,18},{18,10},{10,2},{2,0},{9,1},{1... | collective-permute-start | bytes 1179656 | tf_op jit(solution)/shard_map/ppermute | solution.py:70
  22.8 2.0 collective-permute-done.10
  24.8 2.1 %collective-permute-start.11 = (bf16[32,6144]{1,0:T(8,128)(2,1)S(1)}, bf16[32,6144]{1,0:T(8,128)(2,1)S(1)}, u32[]{:S(2)}, u32[]{:S(2)}) collective-permute-start(bf16[32,6144]{1,0:T(8,128)(2,1)S(1)} %collective-permute-done.10), channel_id=1, source_target_pairs={{0,8},{8,16},{16,24},{24,26},{26,18},{18,10},{10,2},{2,0},{9,1},{1... | collective-permute-start | bytes 1179656 | tf_op jit(solution)/shard_map/ppermute | solution.py:70
  26.9 2.1 %collective-permute-done.4 = bf16[32,6144]{1,0:T(8,128)(2,1)S(1)} collective-permute-done((bf16[32,6144]{1,0:T(8,128)(2,1)S(1)}, bf16[32,6144]{1,0:T(8,128)(2,1)S(1)}, u32[]{:S(2)}, u32[]{:S(2)}) %collective-permute-start.4) | collective-permute-done | bytes 393248 | tf_op jit(solution)/shard_map/ppermute | solution.py:70
  29.1 2.1 %collective-permute-start.5 = (bf16[16,6144]{1,0:T(8,128)(2,1)S(1)}, bf16[16,6144]{1,0:T(8,128)(2,1)S(1)}, u32[]{:S(2)}, u32[]{:S(2)}) collective-permute-start(bf16[16,6144]{1,0:T(8,128)(2,1)S(1)} %slice.153), channel_id=1, source_target_pairs={{0,8},{8,16},{16,24},{24,26},{26,18},{18,10},{10,2},{2,0},{9,1},{1... | collective-permute-start | bytes 589832 | tf_op jit(solution)/shard_map/ppermute | solution.py:70
  31.3 1.9 collective-permute-done.11
  33.3 2.1 %collective-permute-start.15 = (bf16[16,6144]{1,0:T(8,128)(2,1)S(1)}, bf16[16,6144]{1,0:T(8,128)(2,1)S(1)}, u32[]{:S(2)}, u32[]{:S(2)}) collective-permute-start(bf16[16,6144]{1,0:T(8,128)(2,1)S(1)} %slice.157), channel_id=1, source_target_pairs={{0,8},{8,16},{16,24},{24,26},{26,18},{18,10},{10,2},{2,0},{9,1},{1... | collective-permute-start | bytes 589832 | tf_op jit(solution)/shard_map/ppermute | solution.py:70
  35.5 3.5 %collective-permute-done.15 = bf16[16,6144]{1,0:T(8,128)(2,1)S(1)} collective-permute-done((bf16[16,6144]{1,0:T(8,128)(2,1)S(1)}, bf16[16,6144]{1,0:T(8,128)(2,1)S(1)}, u32[]{:S(2)}, u32[]{:S(2)}) %collective-permute-start.15) | collective-permute-done | bytes 196640 | tf_op jit(solution)/shard_map/ppermute | solution.py:70
  39.4 2.1 %collective-permute-start.7 = (bf16[32,6144]{1,0:T(8,128)(2,1)S(1)}, bf16[32,6144]{1,0:T(8,128)(2,1)S(1)}, u32[]{:S(2)}, u32[]{:S(2)}) collective-permute-start(bf16[32,6144]{1,0:T(8,128)(2,1)S(1)} %get-tuple-element.66), channel_id=1, source_target_pairs={{0,8},{8,16},{16,24},{24,26},{26,18},{18,10},{10,2},{2,0},{9,1},{1... | collective-permute-start | bytes 1179656 | tf_op jit(solution)/shard_map/ppermute | solution.py:70
  41.7 1.7 collective-permute-start.12
  43.5 9.0 %fusion.35 = f32[256,1536]{1,0:T(8,128)S(1)} fusion(bf16[256,6144]{1,0:T(8,128)(2,1)S(1)} %constant_dynamic-update-slice_fusion.refs_0_, bf16[6144,1536]{1,0:T(8,128)(2,1)} %w_ref.3), kind=kOutput, calls=%fused_computation.106 | convolution fusion | flops 4831838208 | bytes 23592960 | tf_op jit(solution)/shard_map/dot_general | solution.py:167
  52.6 1.6 collective-permute-start.17
  54.2 1.6 collective-permute-start.18
  55.9 1.6 collective-permute-start.13
  57.5 2.9 %collective-permute-done.17 = bf16[32,6144]{1,0:T(8,128)(2,1)S(1)} collective-permute-done((bf16[32,6144]{1,0:T(8,128)(2,1)S(1)}, bf16[32,6144]{1,0:T(8,128)(2,1)S(1)}, u32[]{:S(2)}, u32[]{:S(2)}) %collective-permute-start.17) | collective-permute-done | bytes 393248 | tf_op jit(solution)/shard_map/ppermute | solution.py:70
  60.5 1.6 collective-permute-start.19
  62.2 6.3 %fusion.2 = f32[256,768]{1,0:T(8,128)S(1)} fusion(bf16[256,6144]{1,0:T(8,128)(2,1)S(1)} %constant_dynamic-update-slice_fusion.8.refs_2_, bf16[1536,6144]{1,0:T(8,128)(2,1)} %param.9), kind=kOutput, calls=%fused_computation.2 | convolution fusion | flops 2415919104 | bytes 13369344 | tf_op jit(solution)/shard_map/dot_general | solution.py:25
  68.9 1.6 collective-permute-start.21
  70.6 1.6 collective-permute-start.20
  72.1 6.3 %fusion = f32[256,768]{1,0:T(8,128)S(1)} fusion(bf16[256,6144]{1,0:T(8,128)(2,1)S(1)} %constant_dynamic-update-slice_fusion.8.refs_2_, bf16[1536,6144]{1,0:T(8,128)(2,1)} %param.9), kind=kOutput, calls=%fused_computation | convolution fusion | flops 2415919104 | bytes 13369344 | tf_op jit(solution)/shard_map/dot_general | solution.py:25
  78.6 1.6 collective-permute-start.25
  80.2 1.8 collective-permute-start.28
  84.2 1.9 collective-permute-done.28
  86.2 9.0 %fusion.36 = f32[256,1536]{1,0:T(8,128)S(1)} fusion(bf16[256,6144]{1,0:T(8,128)(2,1)S(1)} %constant_dynamic-update-slice_fusion.16.refs_1_, bf16[6144,1536]{1,0:T(8,128)(2,1)} %w_ref.3), kind=kOutput, calls=%fused_computation.107 | convolution fusion | flops 4831838208 | bytes 23592960 | tf_op jit(solution)/shard_map/dot_general | solution.py:167
  97.3 2.6 %convert_reduce_fusion.1 = (f32[1536]{0:T(1024)S(1)}, bf16[256,1536]{1,0:T(8,128)(2,1)}, bf16[256,1536]{1,0:T(8,128)(2,1)}) fusion(f32[1536]{0:T(1024)S(1)} %copy-done.9, f32[256,1536]{1,0:T(8,128)S(1)} %fusion.35, bf16[256,1536]{1,0:T(8,128)(2,1)S(1)} %collective-permute-done.13, bf16[256,768]{1,0:T(8,128)(2,1)S(1)} %collective-permute-done.26, ...), kind=kLoop, calls=%fused_computation.27 | loop fusion | flops 12581376 | bytes 6303744 | tf_op jit(solution)/shard_map/reduce_sum | solution.py:177
  100.1 10.1 %fusion.37 = f32[256,1536]{1,0:T(8,128)} fusion(bf16[256,6144]{1,0:T(8,128)(2,1)S(1)} %constant_dynamic-update-slice_fusion.25.refs_3_, bf16[1536,6144]{1,0:T(8,128)(2,1)} %param.9), kind=kOutput, calls=%fused_computation.108 | convolution fusion | flops 4831838208 | bytes 23592960 | tf_op jit(solution)/shard_map/dot_general | solution.py:25
  111.3 1.6 collective-permute-start.32
  114.5 10.4 %shard_map.84 = (f32[128,6144]{1,0:T(8,128)S(1)}, bf16[128,6144]{1,0:T(8,128)(2,1)S(1)}) custom-call(bf16[256,1536]{1,0:T(8,128)(2,1)S(1)} %copy-done, bf16[6144,1536]{1,0:T(8,128)(2,1)} %w_ref.3), custom_call_target="tpu_custom_call" | custom-call | flops 4831838208 | bytes 24379392 | tf_op jit(solution)/shard_map/pallas_call | solution.py:126
  127.3 1.5 collective-permute-start.35
  130.5 1.6 collective-permute-start.34
  132.1 5.4 %shard_map.85.refs_4_ = bf16[1536,6144]{1,0:T(8,128)(2,1)} custom-call(bf16[256,1536]{1,0:T(8,128)(2,1)S(1)} %copy-done.2, bf16[256,1536]{1,0:T(8,128)(2,1)S(1)} %get-tuple-element.115.refs_1_, bf16[256,6144]{1,0:T(8,128)(2,1)S(1)} %constant_dynamic-update-slice_fusion.8.refs_2_, bf16[256,6144]{1,0:T(8,128)(2,1)S(1)} %constant_dynamic-update-slice_fusion.25.refs_3_), custom_call_target="tpu_custom_call" | custom-call | flops 3221225472 | bytes 13107200 | tf_op jit(solution)/shard_map/pallas_call | solution.py:96
  140.4 5.4 %shard_map.86.refs_4_ = bf16[1536,6144]{1,0:T(8,128)(2,1)} custom-call(bf16[256,1536]{1,0:T(8,128)(2,1)S(1)} %copy-done.2, bf16[256,1536]{1,0:T(8,128)(2,1)S(1)} %get-tuple-element.115.refs_1_, bf16[256,6144]{1,0:T(8,128)(2,1)S(1)} %constant_dynamic-update-slice_fusion.8.refs_2_, ...), custom_call_target="tpu_custom_call", output_to_operand_aliasing={{}: (4, {})} | custom-call | flops 3221225472 | bytes 13107200 | tf_op jit(solution)/shard_map/pallas_call | solution.py:96
  145.8 1.7 collective-permute-done.37
  149.6 10.3 %shard_map.87 = (f32[128,6144]{1,0:T(8,128)S(1)}, bf16[128,6144]{1,0:T(8,128)(2,1)S(1)}) custom-call(bf16[256,1536]{1,0:T(8,128)(2,1)S(1)} %get-tuple-element.129.pg_ref.refs_3_, bf16[6144,1536]{1,0:T(8,128)(2,1)} %w_ref.3), custom_call_target="tpu_custom_call" | custom-call | flops 4831838208 | bytes 24379392 | tf_op jit(solution)/shard_map/pallas_call | solution.py:126
  161.1 5.4 %shard_map.88 = bf16[1536,6144]{1,0:T(8,128)(2,1)} custom-call(bf16[256,1536]{1,0:T(8,128)(2,1)S(1)} %copy-done.2, bf16[256,1536]{1,0:T(8,128)(2,1)S(1)} %get-tuple-element.115.refs_1_, bf16[256,6144]{1,0:T(8,128)(2,1)S(1)} %constant_dynamic-update-slice_fusion.8.refs_2_, ...), custom_call_target="tpu_custom_call", output_to_operand_aliasing={{}: (4, {})} | custom-call | flops 3221225472 | bytes 13107200 | tf_op jit(solution)/shard_map/pallas_call | solution.py:96
  168.2 5.5 %shard_map.89.refs_4_ = bf16[6144,1536]{1,0:T(8,128)(2,1)} custom-call(bf16[256,6144]{1,0:T(8,128)(2,1)S(1)} %constant_dynamic-update-slice_fusion.refs_0_, bf16[256,6144]{1,0:T(8,128)(2,1)S(1)} %constant_dynamic-update-slice_fusion.16.refs_1_, bf16[256,1536]{1,0:T(8,128)(2,1)S(1)} %copy-done.1, bf16[256,1536]{1,0:T(8,128)(2,1)S(1)} %get-tuple-element.129.pg_ref.refs_3_), custom_call_target="tpu_custom_call" | custom-call | flops 3221225472 | bytes 9961472 | tf_op jit(solution)/shard_map/pallas_call | solution.py:96
  175.2 5.5 %shard_map.90.refs_4_ = bf16[6144,1536]{1,0:T(8,128)(2,1)} custom-call(bf16[256,6144]{1,0:T(8,128)(2,1)S(1)} %constant_dynamic-update-slice_fusion.refs_0_, bf16[256,6144]{1,0:T(8,128)(2,1)S(1)} %constant_dynamic-update-slice_fusion.16.refs_1_, bf16[256,1536]{1,0:T(8,128)(2,1)S(1)} %copy-done.1, ...), custom_call_target="tpu_custom_call", output_to_operand_aliasing={{}: (4, {})} | custom-call | flops 3221225472 | bytes 9961472 | tf_op jit(solution)/shard_map/pallas_call | solution.py:96
  183.1 1.5 collective-permute-start.39
  184.6 5.5 %shard_map.91 = bf16[6144,1536]{1,0:T(8,128)(2,1)} custom-call(bf16[256,6144]{1,0:T(8,128)(2,1)S(1)} %constant_dynamic-update-slice_fusion.refs_0_, bf16[256,6144]{1,0:T(8,128)(2,1)S(1)} %constant_dynamic-update-slice_fusion.16.refs_1_, bf16[256,1536]{1,0:T(8,128)(2,1)S(1)} %copy-done.1, ...), custom_call_target="tpu_custom_call", output_to_operand_aliasing={{}: (4, {})} | custom-call | flops 3221225472 | bytes 9961472 | tf_op jit(solution)/shard_map/pallas_call | solution.py:96
  191.2 2.6 %collective-permute-done.39 = bf16[32,6144]{1,0:T(8,128)(2,1)S(1)} collective-permute-done((bf16[32,6144]{1,0:T(8,128)(2,1)S(1)}, bf16[32,6144]{1,0:T(8,128)(2,1)S(1)}, u32[]{:S(2)}, u32[]{:S(2)}) %collective-permute-start.39) | collective-permute-done | bytes 393248 | tf_op jit(solution)/shard_map/ppermute | solution.py:70
  194.4 3.6 %collective-permute-done.45 = bf16[32,6144]{1,0:T(8,128)(2,1)S(1)} collective-permute-done((bf16[32,6144]{1,0:T(8,128)(2,1)S(1)}, bf16[32,6144]{1,0:T(8,128)(2,1)S(1)}, u32[]{:S(2)}, u32[]{:S(2)}) %collective-permute-start.45) | collective-permute-done | bytes 393248 | tf_op jit(solution)/shard_map/ppermute | solution.py:70
  (152 shorter events, 31.6 us)
Async XLA Ops:
  0.6 2.8 %collective-permute-start = (bf16[32,6144]{1,0:T(8,128)(2,1)}, bf16[32,6144]{1,0:T(8,128)(2,1)S(1)}, u32[]{:S(2)}, u32[]{:S(2)}) collective-permute-start(bf16[32,6144]{1,0:T(8,128)(2,1)} %param.5), channel_id=1, source_target_pairs={{0,1},{1,0},{2,3},{3,2},{4,5},{5,4},{6,7},{7,6},{8,9},{9,8},{10,11... | collective-permute-start | bytes 1179656 | tf_op jit(solution)/shard_map/ppermute | solution.py:73
  1.1 5.4 %collective-permute-start.8 = (bf16[32,6144]{1,0:T(8,128)(2,1)}, bf16[32,6144]{1,0:T(8,128)(2,1)S(1)}, u32[]{:S(2)}, u32[]{:S(2)}) collective-permute-start(bf16[32,6144]{1,0:T(8,128)(2,1)} %param.6), channel_id=1, source_target_pairs={{0,1},{1,0},{2,3},{3,2},{4,5},{5,4},{6,7},{7,6},{8,9},{9,8},{10,11... | collective-permute-start | bytes 1179656 | tf_op jit(solution)/shard_map/ppermute | solution.py:73
  3.5 8.8 %collective-permute-start.1 = (bf16[32,6144]{1,0:T(8,128)(2,1)S(1)}, bf16[32,6144]{1,0:T(8,128)(2,1)S(1)}, u32[]{:S(2)}, u32[]{:S(2)}) collective-permute-start(bf16[32,6144]{1,0:T(8,128)(2,1)S(1)} %pad_maximum_fusion.8), channel_id=1, source_target_pairs={{0,8},{8,16},{16,24},{24,26},{26,18},{18,10},{10,2},{2,0},{9,1},{1... | collective-permute-start | bytes 1179656 | tf_op jit(solution)/shard_map/ppermute | solution.py:70
  6.6 9.9 %collective-permute-start.9 = (bf16[32,6144]{1,0:T(8,128)(2,1)S(1)}, bf16[32,6144]{1,0:T(8,128)(2,1)S(1)}, u32[]{:S(2)}, u32[]{:S(2)}) collective-permute-start(bf16[32,6144]{1,0:T(8,128)(2,1)S(1)} %pad_maximum_fusion.11), channel_id=1, source_target_pairs={{0,8},{8,16},{16,24},{24,26},{26,18},{18,10},{10,2},{2,0},{9,1},{1... | collective-permute-start | bytes 1179656 | tf_op jit(solution)/shard_map/ppermute | solution.py:70
  12.2 8.4 %collective-permute-start.2 = (bf16[32,6144]{1,0:T(8,128)(2,1)S(1)}, bf16[32,6144]{1,0:T(8,128)(2,1)S(1)}, u32[]{:S(2)}, u32[]{:S(2)}) collective-permute-start(bf16[32,6144]{1,0:T(8,128)(2,1)S(1)} %collective-permute-done.1), channel_id=1, source_target_pairs={{0,8},{8,16},{16,24},{24,26},{26,18},{18,10},{10,2},{2,0},{9,1},{1... | collective-permute-start | bytes 1179656 | tf_op jit(solution)/shard_map/ppermute | solution.py:70
  16.4 8.4 %collective-permute-start.10 = (bf16[32,6144]{1,0:T(8,128)(2,1)S(1)}, bf16[32,6144]{1,0:T(8,128)(2,1)S(1)}, u32[]{:S(2)}, u32[]{:S(2)}) collective-permute-start(bf16[32,6144]{1,0:T(8,128)(2,1)S(1)} %collective-permute-done.9), channel_id=1, source_target_pairs={{0,8},{8,16},{16,24},{24,26},{26,18},{18,10},{10,2},{2,0},{9,1},{1... | collective-permute-start | bytes 1179656 | tf_op jit(solution)/shard_map/ppermute | solution.py:70
  20.6 8.4 %collective-permute-start.4 = (bf16[32,6144]{1,0:T(8,128)(2,1)S(1)}, bf16[32,6144]{1,0:T(8,128)(2,1)S(1)}, u32[]{:S(2)}, u32[]{:S(2)}) collective-permute-start(bf16[32,6144]{1,0:T(8,128)(2,1)S(1)} %collective-permute-done.2), channel_id=1, source_target_pairs={{0,8},{8,16},{16,24},{24,26},{26,18},{18,10},{10,2},{2,0},{9,1},{1... | collective-permute-start | bytes 1179656 | tf_op jit(solution)/shard_map/ppermute | solution.py:70
  22.8 16.4 %collective-permute-start.3 = (bf16[64,6144]{1,0:T(8,128)(2,1)S(1)}, bf16[64,6144]{1,0:T(8,128)(2,1)S(1)}, u32[]{:S(2)}, u32[]{:S(2)}) collective-permute-start(bf16[64,6144]{1,0:T(8,128)(2,1)S(1)} %pad_maximum_fusion), channel_id=1, source_target_pairs={{0,1},{1,0},{2,3},{3,2},{4,5},{5,4},{6,7},{7,6},{8,9},{9,8},{10,11... | collective-permute-start | bytes 2359304 | tf_op jit(solution)/shard_map/ppermute | solution.py:73
  24.8 8.4 %collective-permute-start.11 = (bf16[32,6144]{1,0:T(8,128)(2,1)S(1)}, bf16[32,6144]{1,0:T(8,128)(2,1)S(1)}, u32[]{:S(2)}, u32[]{:S(2)}) collective-permute-start(bf16[32,6144]{1,0:T(8,128)(2,1)S(1)} %collective-permute-done.10), channel_id=1, source_target_pairs={{0,8},{8,16},{16,24},{24,26},{26,18},{18,10},{10,2},{2,0},{9,1},{1... | collective-permute-start | bytes 1179656 | tf_op jit(solution)/shard_map/ppermute | solution.py:70
  29.1 6.3 %collective-permute-start.5 = (bf16[16,6144]{1,0:T(8,128)(2,1)S(1)}, bf16[16,6144]{1,0:T(8,128)(2,1)S(1)}, u32[]{:S(2)}, u32[]{:S(2)}) collective-permute-start(bf16[16,6144]{1,0:T(8,128)(2,1)S(1)} %slice.153), channel_id=1, source_target_pairs={{0,8},{8,16},{16,24},{24,26},{26,18},{18,10},{10,2},{2,0},{9,1},{1... | collective-permute-start | bytes 589832 | tf_op jit(solution)/shard_map/ppermute | solution.py:70
  31.3 7.9 %collective-permute-start.14 = (bf16[64,6144]{1,0:T(8,128)(2,1)S(1)}, bf16[64,6144]{1,0:T(8,128)(2,1)S(1)}, u32[]{:S(2)}, u32[]{:S(2)}) collective-permute-start(bf16[64,6144]{1,0:T(8,128)(2,1)S(1)} %pad_maximum_fusion.1), channel_id=1, source_target_pairs={{0,1},{1,0},{2,3},{3,2},{4,5},{5,4},{6,7},{7,6},{8,9},{9,8},{10,11... | collective-permute-start | bytes 2359304 | tf_op jit(solution)/shard_map/ppermute | solution.py:73
  33.3 5.7 %collective-permute-start.15 = (bf16[16,6144]{1,0:T(8,128)(2,1)S(1)}, bf16[16,6144]{1,0:T(8,128)(2,1)S(1)}, u32[]{:S(2)}, u32[]{:S(2)}) collective-permute-start(bf16[16,6144]{1,0:T(8,128)(2,1)S(1)} %slice.157), channel_id=1, source_target_pairs={{0,8},{8,16},{16,24},{24,26},{26,18},{18,10},{10,2},{2,0},{9,1},{1... | collective-permute-start | bytes 589832 | tf_op jit(solution)/shard_map/ppermute | solution.py:70
  35.5 3.8 %collective-permute-start.6 = (bf16[48,6144]{1,0:T(8,128)(2,1)S(1)}, bf16[48,6144]{1,0:T(8,128)(2,1)S(1)}, u32[]{:S(2)}, u32[]{:S(2)}) collective-permute-start(bf16[48,6144]{1,0:T(8,128)(2,1)S(1)} %pad_maximum_fusion.5), channel_id=1, source_target_pairs={{0,1},{1,0},{2,3},{3,2},{4,5},{5,4},{6,7},{7,6},{8,9},{9,8},{10,11... | collective-permute-start | bytes 1769480 | tf_op jit(solution)/shard_map/ppermute | solution.py:73
  39.1 2.5 %collective-permute-start.16 = (bf16[48,6144]{1,0:T(8,128)(2,1)S(1)}, bf16[48,6144]{1,0:T(8,128)(2,1)S(1)}, u32[]{:S(2)}, u32[]{:S(2)}) collective-permute-start(bf16[48,6144]{1,0:T(8,128)(2,1)S(1)} %pad_maximum_fusion.6), channel_id=1, source_target_pairs={{0,1},{1,0},{2,3},{3,2},{4,5},{5,4},{6,7},{7,6},{8,9},{9,8},{10,11... | collective-permute-start | bytes 1769480 | tf_op jit(solution)/shard_map/ppermute | solution.py:73
  39.4 13.1 %collective-permute-start.7 = (bf16[32,6144]{1,0:T(8,128)(2,1)S(1)}, bf16[32,6144]{1,0:T(8,128)(2,1)S(1)}, u32[]{:S(2)}, u32[]{:S(2)}) collective-permute-start(bf16[32,6144]{1,0:T(8,128)(2,1)S(1)} %get-tuple-element.66), channel_id=1, source_target_pairs={{0,8},{8,16},{16,24},{24,26},{26,18},{18,10},{10,2},{2,0},{9,1},{1... | collective-permute-start | bytes 1179656 | tf_op jit(solution)/shard_map/ppermute | solution.py:70
  41.7 10.9 %collective-permute-start.12 = (bf16[32,6144]{1,0:T(8,128)(2,1)S(1)}, bf16[32,6144]{1,0:T(8,128)(2,1)S(1)}, u32[]{:S(2)}, u32[]{:S(2)}) collective-permute-start(bf16[32,6144]{1,0:T(8,128)(2,1)S(1)} %get-tuple-element.67), channel_id=1, source_target_pairs={{0,8},{8,16},{16,24},{24,26},{26,18},{18,10},{10,2},{2,0},{9,1},{1... | collective-permute-start | bytes 1179656 | tf_op jit(solution)/shard_map/ppermute | solution.py:70
  52.6 7.8 %collective-permute-start.17 = (bf16[32,6144]{1,0:T(8,128)(2,1)S(1)}, bf16[32,6144]{1,0:T(8,128)(2,1)S(1)}, u32[]{:S(2)}, u32[]{:S(2)}) collective-permute-start(bf16[32,6144]{1,0:T(8,128)(2,1)S(1)} %collective-permute-done.7), channel_id=1, source_target_pairs={{0,8},{8,16},{16,24},{24,26},{26,18},{18,10},{10,2},{2,0},{9,1},{1... | collective-permute-start | bytes 1179656 | tf_op jit(solution)/shard_map/ppermute | solution.py:70
  54.2 14.3 %collective-permute-start.18 = (bf16[32,6144]{1,0:T(8,128)(2,1)S(1)}, bf16[32,6144]{1,0:T(8,128)(2,1)S(1)}, u32[]{:S(2)}, u32[]{:S(2)}) collective-permute-start(bf16[32,6144]{1,0:T(8,128)(2,1)S(1)} %collective-permute-done.12), channel_id=1, source_target_pairs={{0,8},{8,16},{16,24},{24,26},{26,18},{18,10},{10,2},{2,0},{9,1},{1... | collective-permute-start | bytes 1179656 | tf_op jit(solution)/shard_map/ppermute | solution.py:70
  55.9 41.0 %collective-permute-start.13 = (bf16[256,1536]{1,0:T(8,128)(2,1)S(1)}, bf16[256,1536]{1,0:T(8,128)(2,1)S(1)}, u32[]{:S(2)}, u32[]{:S(2)}) collective-permute-start(bf16[256,1536]{1,0:T(8,128)(2,1)S(1)} %convert_element_type.114), channel_id=1, source_target_pairs={{0,4},{4,0},{1,5},{5,1},{2,6},{6,2},{3,7},{7,3},{8,12},{12,8},{9,1... | collective-permute-start | bytes 2359304 | tf_op jit(solution)/shard_map/ppermute | solution.py:76
  60.5 19.7 %collective-permute-start.22 = (bf16[64,6144]{1,0:T(8,128)(2,1)S(1)}, bf16[64,6144]{1,0:T(8,128)(2,1)S(1)}, u32[]{:S(2)}, u32[]{:S(2)}) collective-permute-start(bf16[64,6144]{1,0:T(8,128)(2,1)S(1)} %pad_maximum_fusion.2), channel_id=1, source_target_pairs={{0,1},{1,0},{2,3},{3,2},{4,5},{5,4},{6,7},{7,6},{8,9},{9,8},{10,11... | collective-permute-start | bytes 2359304 | tf_op jit(solution)/shard_map/ppermute | solution.py:73
  60.5 8.3 %collective-permute-start.19 = (bf16[32,6144]{1,0:T(8,128)(2,1)S(1)}, bf16[32,6144]{1,0:T(8,128)(2,1)S(1)}, u32[]{:S(2)}, u32[]{:S(2)}) collective-permute-start(bf16[32,6144]{1,0:T(8,128)(2,1)S(1)} %collective-permute-done.17), channel_id=1, source_target_pairs={{0,8},{8,16},{16,24},{24,26},{26,18},{18,10},{10,2},{2,0},{9,1},{1... | collective-permute-start | bytes 1179656 | tf_op jit(solution)/shard_map/ppermute | solution.py:70
  68.8 13.1 %collective-permute-start.23 = (bf16[32,6144]{1,0:T(8,128)(2,1)S(1)}, bf16[32,6144]{1,0:T(8,128)(2,1)S(1)}, u32[]{:S(2)}, u32[]{:S(2)}) collective-permute-start(bf16[32,6144]{1,0:T(8,128)(2,1)S(1)} %collective-permute-done.19), channel_id=1, source_target_pairs={{0,1},{1,0},{2,3},{3,2},{4,5},{5,4},{6,7},{7,6},{8,9},{9,8},{10,11... | collective-permute-start | bytes 1179656 | tf_op jit(solution)/shard_map/ppermute | solution.py:73
  68.9 9.6 %collective-permute-start.21 = (bf16[16,6144]{1,0:T(8,128)(2,1)S(1)}, bf16[16,6144]{1,0:T(8,128)(2,1)S(1)}, u32[]{:S(2)}, u32[]{:S(2)}) collective-permute-start(bf16[16,6144]{1,0:T(8,128)(2,1)S(1)} %slice.129), channel_id=1, source_target_pairs={{0,8},{8,16},{16,24},{24,26},{26,18},{18,10},{10,2},{2,0},{9,1},{1... | collective-permute-start | bytes 589832 | tf_op jit(solution)/shard_map/ppermute | solution.py:70
  70.6 9.6 %collective-permute-start.20 = (bf16[32,6144]{1,0:T(8,128)(2,1)S(1)}, bf16[32,6144]{1,0:T(8,128)(2,1)S(1)}, u32[]{:S(2)}, u32[]{:S(2)}) collective-permute-start(bf16[32,6144]{1,0:T(8,128)(2,1)S(1)} %collective-permute-done.18), channel_id=1, source_target_pairs={{0,8},{8,16},{16,24},{24,26},{26,18},{18,10},{10,2},{2,0},{9,1},{1... | collective-permute-start | bytes 1179656 | tf_op jit(solution)/shard_map/ppermute | solution.py:70
  78.6 16.6 %collective-permute-start.25 = (bf16[256,768]{1,0:T(8,128)(2,1)S(1)}, bf16[256,768]{1,0:T(8,128)(2,1)S(1)}, u32[]{:S(2)}, u32[]{:S(2)}) collective-permute-start(bf16[256,768]{1,0:T(8,128)(2,1)S(1)} %convert_element_type.117), channel_id=1, source_target_pairs={{0,4},{4,0},{1,5},{5,1},{2,6},{6,2},{3,7},{7,3},{8,12},{12,8},{9,1... | collective-permute-start | bytes 1179656 | tf_op jit(solution)/shard_map/ppermute | solution.py:76
  80.1 16.7 %collective-permute-start.27 = (bf16[64,6144]{1,0:T(8,128)(2,1)S(1)}, bf16[64,6144]{1,0:T(8,128)(2,1)S(1)}, u32[]{:S(2)}, u32[]{:S(2)}) collective-permute-start(bf16[64,6144]{1,0:T(8,128)(2,1)S(1)} %pad_maximum_fusion.3), channel_id=1, source_target_pairs={{0,1},{1,0},{2,3},{3,2},{4,5},{5,4},{6,7},{7,6},{8,9},{9,8},{10,11... | collective-permute-start | bytes 2359304 | tf_op jit(solution)/shard_map/ppermute | solution.py:73
  80.2 5.9 %collective-permute-start.28 = (bf16[16,6144]{1,0:T(8,128)(2,1)S(1)}, bf16[16,6144]{1,0:T(8,128)(2,1)S(1)}, u32[]{:S(2)}, u32[]{:S(2)}) collective-permute-start(bf16[16,6144]{1,0:T(8,128)(2,1)S(1)} %slice.130), channel_id=1, source_target_pairs={{0,8},{8,16},{16,24},{24,26},{26,18},{18,10},{10,2},{2,0},{9,1},{1... | collective-permute-start | bytes 589832 | tf_op jit(solution)/shard_map/ppermute | solution.py:70
  82.0 1.5 collective-permute-start.24
  83.5 13.8 %collective-permute-start.26 = (bf16[256,768]{1,0:T(8,128)(2,1)S(1)}, bf16[256,768]{1,0:T(8,128)(2,1)S(1)}, u32[]{:S(2)}, u32[]{:S(2)}) collective-permute-start(bf16[256,768]{1,0:T(8,128)(2,1)S(1)} %convert_element_type.118), channel_id=1, source_target_pairs={{0,4},{4,0},{1,5},{5,1},{2,6},{6,2},{3,7},{7,3},{8,12},{12,8},{9,1... | collective-permute-start | bytes 1179656 | tf_op jit(solution)/shard_map/ppermute | solution.py:76
  86.1 13.8 %collective-permute-start.29 = (bf16[48,6144]{1,0:T(8,128)(2,1)S(1)}, bf16[48,6144]{1,0:T(8,128)(2,1)S(1)}, u32[]{:S(2)}, u32[]{:S(2)}) collective-permute-start(bf16[48,6144]{1,0:T(8,128)(2,1)S(1)} %pad_maximum_fusion.7), channel_id=1, source_target_pairs={{0,1},{1,0},{2,3},{3,2},{4,5},{5,4},{6,7},{7,6},{8,9},{9,8},{10,11... | collective-permute-start | bytes 1769480 | tf_op jit(solution)/shard_map/ppermute | solution.py:73
  96.3 13.9 %collective-permute-start.30 = (bf16[128,1536]{1,0:T(8,128)(2,1)}, bf16[128,1536]{1,0:T(8,128)(2,1)S(1)}, u32[]{:S(2)}, u32[]{:S(2)}) collective-permute-start(bf16[128,1536]{1,0:T(8,128)(2,1)} %get-tuple-element.146), channel_id=1, source_target_pairs={{0,4},{4,0},{1,5},{5,1},{2,6},{6,2},{3,7},{7,3},{8,12},{12,8},{9,1... | collective-permute-start | bytes 1179656 | tf_op jit(solution)/shard_map/ppermute | solution.py:76
  111.3 13.7 %collective-permute-start.32 = (bf16[64,1536]{1,0:T(8,128)(2,1)S(1)}, bf16[64,1536]{1,0:T(8,128)(2,1)S(1)}, u32[]{:S(2)}, u32[]{:S(2)}) collective-permute-start(bf16[64,1536]{1,0:T(8,128)(2,1)S(1)} %slice.221), channel_id=1, source_target_pairs={{0,4},{4,0},{1,5},{5,1},{2,6},{6,2},{3,7},{7,3},{8,12},{12,8},{9,1... | collective-permute-start | bytes 589832 | tf_op jit(solution)/shard_map/ppermute | solution.py:76
  112.8 13.6 %collective-permute-start.31 = (bf16[128,1536]{1,0:T(8,128)(2,1)}, bf16[128,1536]{1,0:T(8,128)(2,1)S(1)}, u32[]{:S(2)}, u32[]{:S(2)}) collective-permute-start(bf16[128,1536]{1,0:T(8,128)(2,1)} %get-tuple-element.87), channel_id=1, source_target_pairs={{0,4},{4,0},{1,5},{5,1},{2,6},{6,2},{3,7},{7,3},{8,12},{12,8},{9,1... | collective-permute-start | bytes 1179656 | tf_op jit(solution)/shard_map/ppermute | solution.py:76
  114.5 14.3 %copy-start.5 = (f32[256,1536]{1,0:T(8,128)S(1)}, f32[256,1536]{1,0:T(8,128)}, u32[]{:S(2)}) copy-start(f32[256,1536]{1,0:T(8,128)} %copy-done.4) | copy-start | bytes 4718596
  126.4 3.5 %collective-permute-start.33 = (bf16[128,6144]{1,0:T(8,128)(2,1)S(1)}, bf16[128,6144]{1,0:T(8,128)(2,1)S(1)}, u32[]{:S(2)}, u32[]{:S(2)}) collective-permute-start(bf16[128,6144]{1,0:T(8,128)(2,1)S(1)} %get-tuple-element.89), channel_id=1, source_target_pairs={{0,1},{1,0},{2,3},{3,2},{4,5},{5,4},{6,7},{7,6},{8,9},{9,8},{10,11... | collective-permute-start | bytes 4718600 | tf_op jit(solution)/shard_map/ppermute | solution.py:73
  127.3 10.2 %collective-permute-start.35 = (bf16[96,1536]{1,0:T(8,128)(2,1)}, bf16[96,1536]{1,0:T(8,128)(2,1)}, u32[]{:S(2)}, u32[]{:S(2)}) collective-permute-start(bf16[96,1536]{1,0:T(8,128)(2,1)} %get-tuple-element.96), channel_id=1, source_target_pairs={{0,4},{4,0},{1,5},{5,1},{2,6},{6,2},{3,7},{7,3},{8,12},{12,8},{9,1... | collective-permute-start | bytes 884744 | tf_op jit(solution)/shard_map/ppermute | solution.py:76
  130.5 7.0 %collective-permute-start.34 = (bf16[16,6144]{1,0:T(8,128)(2,1)S(1)}, bf16[16,6144]{1,0:T(8,128)(2,1)S(1)}, u32[]{:S(2)}, u32[]{:S(2)}) collective-permute-start(bf16[16,6144]{1,0:T(8,128)(2,1)S(1)} %get-tuple-element.144), channel_id=1, source_target_pairs={{0,8},{8,16},{16,24},{24,26},{26,18},{18,10},{10,2},{2,0},{9,1},{1... | collective-permute-start | bytes 589832 | tf_op jit(solution)/shard_map/ppermute | solution.py:70
  137.5 10.0 %collective-permute-start.36 = (bf16[32,6144]{1,0:T(8,128)(2,1)S(1)}, bf16[32,6144]{1,0:T(8,128)(2,1)S(1)}, u32[]{:S(2)}, u32[]{:S(2)}) collective-permute-start(bf16[32,6144]{1,0:T(8,128)(2,1)S(1)} %pad_maximum_fusion.12), channel_id=1, source_target_pairs={{0,8},{8,16},{16,24},{24,26},{26,18},{18,10},{10,2},{2,0},{9,1},{1... | collective-permute-start | bytes 1179656 | tf_op jit(solution)/shard_map/ppermute | solution.py:70
  139.0 8.5 %collective-permute-start.37 = (bf16[96,1536]{1,0:T(8,128)(2,1)S(1)}, bf16[96,1536]{1,0:T(8,128)(2,1)S(1)}, u32[]{:S(2)}, u32[]{:S(2)}) collective-permute-start(bf16[96,1536]{1,0:T(8,128)(2,1)S(1)} %copy-done.6), channel_id=1, source_target_pairs={{0,4},{4,0},{1,5},{5,1},{2,6},{6,2},{3,7},{7,3},{8,12},{12,8},{9,1... | collective-permute-start | bytes 884744 | tf_op jit(solution)/shard_map/ppermute | solution.py:76
  147.6 12.4 %collective-permute-start.38 = (bf16[32,6144]{1,0:T(8,128)(2,1)S(1)}, bf16[32,6144]{1,0:T(8,128)(2,1)}, u32[]{:S(2)}, u32[]{:S(2)}) collective-permute-start(bf16[32,6144]{1,0:T(8,128)(2,1)S(1)} %fusion.18), channel_id=1, source_target_pairs={{0,8},{8,16},{16,24},{24,26},{26,18},{18,10},{10,2},{2,0},{9,1},{1... | collective-permute-start | bytes 1179656 | tf_op jit(solution)/shard_map/ppermute | solution.py:70
  159.9 6.6 %collective-permute-start.41 = (bf16[128,6144]{1,0:T(8,128)(2,1)S(1)}, bf16[128,6144]{1,0:T(8,128)(2,1)S(1)}, u32[]{:S(2)}, u32[]{:S(2)}) collective-permute-start(bf16[128,6144]{1,0:T(8,128)(2,1)S(1)} %get-tuple-element.111), channel_id=1, source_target_pairs={{0,1},{1,0},{2,3},{3,2},{4,5},{5,4},{6,7},{7,6},{8,9},{9,8},{10,11... | collective-permute-start | bytes 4718600 | tf_op jit(solution)/shard_map/ppermute | solution.py:73
  167.0 6.7 %collective-permute-start.42 = (bf16[16,6144]{1,0:T(8,128)(2,1)S(1)}, bf16[16,6144]{1,0:T(8,128)(2,1)S(1)}, u32[]{:S(2)}, u32[]{:S(2)}) collective-permute-start(bf16[16,6144]{1,0:T(8,128)(2,1)S(1)} %get-tuple-element.139), channel_id=1, source_target_pairs={{0,8},{8,16},{16,24},{24,26},{26,18},{18,10},{10,2},{2,0},{9,1},{1... | collective-permute-start | bytes 589832 | tf_op jit(solution)/shard_map/ppermute | solution.py:70
  173.8 7.8 %collective-permute-start.43 = (bf16[32,6144]{1,0:T(8,128)(2,1)S(1)}, bf16[32,6144]{1,0:T(8,128)(2,1)S(1)}, u32[]{:S(2)}, u32[]{:S(2)}) collective-permute-start(bf16[32,6144]{1,0:T(8,128)(2,1)S(1)} %pad_maximum_fusion.13), channel_id=1, source_target_pairs={{0,8},{8,16},{16,24},{24,26},{26,18},{18,10},{10,2},{2,0},{9,1},{1... | collective-permute-start | bytes 1179656 | tf_op jit(solution)/shard_map/ppermute | solution.py:70
  181.7 8.4 %collective-permute-start.44 = (bf16[32,6144]{1,0:T(8,128)(2,1)S(1)}, bf16[32,6144]{1,0:T(8,128)(2,1)S(1)}, u32[]{:S(2)}, u32[]{:S(2)}) collective-permute-start(bf16[32,6144]{1,0:T(8,128)(2,1)S(1)} %fusion.16), channel_id=1, source_target_pairs={{0,8},{8,16},{16,24},{24,26},{26,18},{18,10},{10,2},{2,0},{9,1},{1... | collective-permute-start | bytes 1179656 | tf_op jit(solution)/shard_map/ppermute | solution.py:70
  183.1 10.7 %collective-permute-start.39 = (bf16[32,6144]{1,0:T(8,128)(2,1)S(1)}, bf16[32,6144]{1,0:T(8,128)(2,1)S(1)}, u32[]{:S(2)}, u32[]{:S(2)}) collective-permute-start(bf16[32,6144]{1,0:T(8,128)(2,1)S(1)} %fusion.19), channel_id=1, source_target_pairs={{0,8},{8,16},{16,24},{24,26},{26,18},{18,10},{10,2},{2,0},{9,1},{1... | collective-permute-start | bytes 1179656 | tf_op jit(solution)/shard_map/ppermute | solution.py:70
  190.2 7.8 %collective-permute-start.45 = (bf16[32,6144]{1,0:T(8,128)(2,1)S(1)}, bf16[32,6144]{1,0:T(8,128)(2,1)S(1)}, u32[]{:S(2)}, u32[]{:S(2)}) collective-permute-start(bf16[32,6144]{1,0:T(8,128)(2,1)S(1)} %fusion.17), channel_id=1, source_target_pairs={{0,8},{8,16},{16,24},{24,26},{26,18},{18,10},{10,2},{2,0},{9,1},{1... | collective-permute-start | bytes 1179656 | tf_op jit(solution)/shard_map/ppermute | solution.py:70
  193.8 4.3 %collective-permute-start.40 = (bf16[16,6144]{1,0:T(8,128)(2,1)S(1)}, bf16[16,6144]{1,0:T(8,128)(2,1)S(1)}, u32[]{:S(2)}, u32[]{:S(2)}) collective-permute-start(bf16[16,6144]{1,0:T(8,128)(2,1)S(1)} %slice.167), channel_id=1, source_target_pairs={{0,1},{1,0},{2,3},{3,2},{4,5},{5,4},{6,7},{7,6},{8,9},{9,8},{10,11... | collective-permute-start | bytes 589832 | tf_op jit(solution)/shard_map/ppermute | solution.py:73
  198.0 1.5 collective-permute-start.46
  (9 other events, 47.0 us)
